TPU v7x, 128 devices: a whole 4x4x4 slice. The times are simulated.
128 devices in a mesh: grp: 2 (over core), blk: 32 (over z_lo, y, x), head: 2 (over z_hi).
Axes of the slice: x: 4, y: 4, z: 4 (z_hi: 2, z_lo: 2; z = z_hi * 2 + z_lo), core: 2. Of those that a mesh axis runs over, the one named last changes fastest.
Arguments:
- tokens: bfloat16 [16384, 768], P(('grp', 'blk', 'head')), parts along dimension 0, may hold values from -16 to 16
- gain_one: bfloat16 [768], P(('blk', 'head')), may hold values from 0.25 to 1.75
- w_query: bfloat16 [768, 768], P(('blk', 'head')), may hold values from -0.3125 to 0.3125
- w_key: bfloat16 [768, 768], P(('blk', 'head')), may hold values from -0.3125 to 0.3125
- w_value: bfloat16 [768, 768], P(('blk', 'head')), may hold values from -0.21875 to 0.21875
- w_out: bfloat16 [768, 768], P(('blk', 'head')), may hold values from -0.875 to 0.875
- gain_two: bfloat16 [768], P(('blk', 'head')), may hold values from 0.25 to 1.75
- w_gate: bfloat16 [768, 3072], P(('blk', 'head')), may hold values from -0.21875 to 0.21875
- w_up: bfloat16 [768, 3072], P(('blk', 'head')), may hold values from -0.21875 to 0.21875
- w_down: bfloat16 [3072, 768], P(('blk', 'head')), may hold values from -0.109375 to 0.109375
- cotangent: bfloat16 [16384, 768], P(('grp', 'blk', 'head')), parts along dimension 0, may hold values from -6 to 6
- segment_ids: int32 [16384], P(('grp', 'blk')), parts along dimension 0, may hold values from 0 to 17, as said below
- positions: int32 [16384], P(('grp', 'blk')), parts along dimension 0, may hold values from 0 to 2303, as said below
Outputs:
- output: bfloat16 [16384, 768], P(('grp', 'blk', 'head')), parts along dimension 0
- input_grad: float32 [16384, 768], P(('grp', 'blk', 'head')), parts along dimension 0
- gain_one_grad: float32 [1536], P(('grp', 'blk', 'head')), parts along dimension 0
- w_query_grad: float32 [1536, 768], P(('grp', 'blk', 'head')), parts along dimension 0
- w_key_grad: float32 [1536, 768], P(('grp', 'blk', 'head')), parts along dimension 0
- w_value_grad: float32 [1536, 768], P(('grp', 'blk', 'head')), parts along dimension 0
- w_out_grad: float32 [1536, 768], P(('grp', 'blk', 'head')), parts along dimension 0
- gain_two_grad: float32 [1536], P(('grp', 'blk', 'head')), parts along dimension 0
- w_gate_grad: float32 [1536, 3072], P(('grp', 'blk', 'head')), parts along dimension 0
- w_up_grad: float32 [1536, 3072], P(('grp', 'blk', 'head')), parts along dimension 0
- w_down_grad: float32 [6144, 768], P(('grp', 'blk', 'head')), parts along dimension 0
There are 2 independent parts, one for each index of `grp`. A program takes and returns all parts, laid end to end along the dimension named above; an argument that names none is the same for every part. Nothing has to cross between parts.
Inputs may be any that keep to these rules, and one draw needn't show every extreme that they name: `segment_ids`: tokens come in aligned slabs of 128 consecutive positions of one sequence, slabs in any order; every group g has a prompt with segment g * (9) and positions 0 to 2047 and continuations c = 1 to 8 with segment g * 9 + c and positions 2048 to 2303, each position of each sequence once. `positions`: positions of the sequences described for segment_ids.
All inputs are finite; a program needn't handle non-finite values.
Results may differ from a plain program's by a relative error of at most 0.035.
Values may be sent and summed in bfloat16 or wider, within the bound.
A program may use at most 192 MiB of HBM per device.

v0:
```python
import math

import jax
import jax.numpy as jnp
from jax import lax
from jax.sharding import PartitionSpec as P

HEADS = 12
KV_HEADS = 12
HD = 64
CONTS = 8


epsilon = 1e-05
rope_base = 10000.0
highest = lax.Precision.HIGHEST
masked_low = -1e30


def rms_parts(values):
    row_scale = lax.rsqrt(jnp.mean(values * values, axis=-1, keepdims=True) + epsilon)
    return (values * row_scale, row_scale)


def norm_back(grad_hidden, normed, row_scale, gain):
    grad_normed = grad_hidden * gain
    grad_values = row_scale * (
        grad_normed - normed * jnp.mean(grad_normed * normed, axis=-1, keepdims=True)
    )
    return (grad_values, jnp.sum(grad_hidden * normed, axis=0))


def rotate(field, positions, direction):
    row_count = field.shape[0]
    pieces = field.reshape(row_count, -1, HD)
    half_dim = HD // 2
    frequency = rope_base ** (-jnp.arange(half_dim, dtype=jnp.float32) * 2.0 / HD)
    angles = positions.astype(jnp.float32)[:, None] * frequency[None, :]
    cosine = jnp.cos(angles)[:, None, :]
    sine_part = direction * jnp.sin(angles)[:, None, :]
    leading = pieces[..., :half_dim]
    trailing = pieces[..., half_dim:]
    turned = jnp.concatenate(
        [leading * cosine - trailing * sine_part, trailing * cosine + leading * sine_part], -1
    )
    return turned.reshape(row_count, -1)


def visible_pairs(seg_query, pos_query, seg_key, pos_key):
    same_group = (seg_query // (CONTS + 1))[:, None] == (seg_key // (CONTS + 1))[None, :]
    readable = (seg_key % (CONTS + 1) == 0)[None, :] | (seg_query[:, None] == seg_key[None, :])
    return same_group & readable & (pos_key[None, :] <= pos_query[:, None])


def dot_right_t(left, right):
    return lax.dot_general(
        left, right, (((1,), (1,)), ((), ())), preferred_element_type=jnp.float32
    )


def dot_left_t(left, right):
    return lax.dot_general(
        left, right, (((0,), (0,)), ((), ())), preferred_element_type=jnp.float32
    )


def split_blocks(shard_piece, kv_local):
    key_piece, value_piece, seg_piece, pos_piece = shard_piece
    piece_rows = key_piece.shape[0]
    key_width = math.gcd(piece_rows, 512)
    blocks = piece_rows // key_width
    operands = (
        key_piece.reshape(blocks, key_width, kv_local, HD),
        value_piece.reshape(blocks, key_width, kv_local, HD),
        seg_piece.reshape(blocks, key_width),
        pos_piece.reshape(blocks, key_width),
        jnp.arange(blocks, dtype=jnp.int32),
    )
    return (operands, key_width)


def per_device(
    tokens,
    gain_one,
    w_query,
    w_key,
    w_value,
    w_out,
    gain_two,
    w_gate,
    w_up,
    w_down,
    cotangent,
    segment_ids,
    positions,
):
    local_rows = tokens.shape[0]
    own_positions = lax.dynamic_slice_in_dim(
        positions, lax.axis_index("head") * local_rows, local_rows
    )
    query_full, key_full, value_full, out_full, gain_first, gain_second = (
        lax.all_gather(w_query, ("blk", "head"), axis=0, tiled=True),
        lax.all_gather(w_key, ("blk", "head"), axis=0, tiled=True),
        lax.all_gather(w_value, ("blk", "head"), axis=0, tiled=True),
        lax.all_gather(w_out, ("blk", "head"), axis=0, tiled=True),
        lax.all_gather(gain_one, ("blk", "head"), axis=0, tiled=True),
        lax.all_gather(gain_two, ("blk", "head"), axis=0, tiled=True),
    )
    inputs = tokens.astype(jnp.float32)
    normed_one, scale_one = rms_parts(inputs)
    hidden_one = (normed_one * gain_first.astype(jnp.float32)).astype(jnp.bfloat16)
    query_tok = rotate(
        jnp.dot(hidden_one, query_full, preferred_element_type=jnp.float32), own_positions, 1.0
    ).astype(jnp.bfloat16)
    key_tok = rotate(
        jnp.dot(hidden_one, key_full, preferred_element_type=jnp.float32), own_positions, 1.0
    ).astype(jnp.bfloat16)
    value_tok = jnp.dot(hidden_one, value_full, preferred_element_type=jnp.float32).astype(
        jnp.bfloat16
    )
    query_head, key_head, value_head = (
        lax.all_to_all(query_tok, "head", split_axis=1, concat_axis=0, tiled=True),
        lax.all_to_all(key_tok, "head", split_axis=1, concat_axis=0, tiled=True),
        lax.all_to_all(value_tok, "head", split_axis=1, concat_axis=0, tiled=True),
    )
    cycle_rows = query_head.shape[0]
    kv_local = key_head.shape[1] // HD
    per_group = HEADS // KV_HEADS
    scale_factor = 1.0 / math.sqrt(HD)
    query_grid = query_head.reshape(cycle_rows, kv_local, per_group, HD).transpose(1, 2, 0, 3)
    start_state = (
        jnp.full((kv_local, per_group, cycle_rows), masked_low, jnp.float32),
        jnp.zeros((kv_local, per_group, cycle_rows), jnp.float32),
        jnp.zeros((kv_local, per_group, cycle_rows, HD), jnp.float32),
    )
    folded = start_state
    operands, key_width = split_blocks(
        (
            lax.all_gather(key_head, "blk", axis=0, tiled=True),
            lax.all_gather(value_head, "blk", axis=0, tiled=True),
            lax.all_gather(segment_ids, "blk", axis=0, tiled=True),
            lax.all_gather(positions, "blk", axis=0, tiled=True),
        ),
        kv_local,
    )

    def forward_advance(status, block_in):
        key_block, value_block, seg_block, pos_block, block_index = block_in
        allowed = visible_pairs(segment_ids, positions, seg_block, pos_block)

        def forward_update(current):
            running_max, running_sum, running_acc = current
            scores = (
                jnp.einsum(
                    "kgqd,nkd->kgqn", query_grid, key_block, preferred_element_type=jnp.float32
                )
                * scale_factor
            )
            new_max = jnp.maximum(
                running_max, jnp.max(jnp.where(allowed, scores, masked_low), axis=-1)
            )
            weights = jnp.where(allowed, jnp.exp(scores - new_max[..., None]), 0.0)
            decay_old = jnp.exp(running_max - new_max)
            running_sum = running_sum * decay_old + jnp.sum(weights, axis=-1)
            running_acc = running_acc * decay_old[..., None] + jnp.einsum(
                "kgqn,nkd->kgqd", weights, value_block.astype(jnp.float32), precision=highest
            )
            return (new_max, running_sum, running_acc)

        return (lax.cond(jnp.any(allowed), forward_update, lambda current: current, status), None)

    folded, unused_out = lax.scan(forward_advance, folded, operands)
    run_max, run_sum, run_acc = folded
    log_total = run_max + jnp.log(run_sum)
    attended_grid = run_acc / run_sum[..., None]
    attended_head = attended_grid.transpose(2, 0, 1, 3).reshape(cycle_rows, -1).astype(jnp.bfloat16)
    attended_tok = lax.all_to_all(attended_head, "head", split_axis=0, concat_axis=1, tiled=True)
    middle = inputs + jnp.dot(attended_tok, out_full, preferred_element_type=jnp.float32)
    normed_two, scale_two = rms_parts(middle)
    hidden_two = (normed_two * gain_second.astype(jnp.float32)).astype(jnp.bfloat16)
    gate_full, up_full, down_full = (
        lax.all_gather(w_gate, ("blk", "head"), axis=0, tiled=True),
        lax.all_gather(w_up, ("blk", "head"), axis=0, tiled=True),
        lax.all_gather(w_down, ("blk", "head"), axis=0, tiled=True),
    )
    gate_pre = jnp.dot(hidden_two, gate_full, preferred_element_type=jnp.float32)
    up_pre = jnp.dot(hidden_two, up_full, preferred_element_type=jnp.float32)
    silu_gate = jax.nn.silu(gate_pre)
    activated = (silu_gate * up_pre).astype(jnp.bfloat16)
    output = (middle + jnp.dot(activated, down_full, preferred_element_type=jnp.float32)).astype(
        jnp.bfloat16
    )
    query_back, key_back, value_back, out_back, gain_first_b, gain_second_b = (
        lax.all_gather(w_query, ("blk", "head"), axis=0, tiled=True),
        lax.all_gather(w_key, ("blk", "head"), axis=0, tiled=True),
        lax.all_gather(w_value, ("blk", "head"), axis=0, tiled=True),
        lax.all_gather(w_out, ("blk", "head"), axis=0, tiled=True),
        lax.all_gather(gain_one, ("blk", "head"), axis=0, tiled=True),
        lax.all_gather(gain_two, ("blk", "head"), axis=0, tiled=True),
    )
    gate_back, up_back, down_back = (
        lax.all_gather(w_gate, ("blk", "head"), axis=0, tiled=True),
        lax.all_gather(w_up, ("blk", "head"), axis=0, tiled=True),
        lax.all_gather(w_down, ("blk", "head"), axis=0, tiled=True),
    )
    grad_act = dot_right_t(cotangent, down_back)
    sigmoid_gate = jax.nn.sigmoid(gate_pre)
    grad_gate = (
        grad_act * up_pre * (sigmoid_gate * (1.0 + gate_pre * (1.0 - sigmoid_gate)))
    ).astype(jnp.bfloat16)
    grad_up = (grad_act * silu_gate).astype(jnp.bfloat16)
    grad_hidden_two = dot_right_t(grad_gate, gate_back) + dot_right_t(grad_up, up_back)
    down_grad = dot_left_t(activated, cotangent)
    gate_grad = dot_left_t(hidden_two, grad_gate)
    up_grad = dot_left_t(hidden_two, grad_up)
    gate_share, up_share, down_share = (
        lax.psum_scatter(gate_grad, ("blk", "head"), scatter_dimension=0, tiled=True),
        lax.psum_scatter(up_grad, ("blk", "head"), scatter_dimension=0, tiled=True),
        lax.psum_scatter(down_grad, ("blk", "head"), scatter_dimension=0, tiled=True),
    )
    grad_mid_norm, gain_two_term = norm_back(
        grad_hidden_two, normed_two, scale_two, gain_second_b.astype(jnp.float32)
    )
    grad_middle = cotangent.astype(jnp.float32) + grad_mid_norm
    grad_middle_low = grad_middle.astype(jnp.bfloat16)
    out_grad = dot_left_t(attended_tok, grad_middle_low)
    grad_attended = dot_right_t(grad_middle_low, out_back).astype(jnp.bfloat16)
    grad_head = lax.all_to_all(grad_attended, "head", split_axis=1, concat_axis=0, tiled=True)
    grad_grid = grad_head.reshape(cycle_rows, kv_local, per_group, HD).transpose(1, 2, 0, 3)
    grad_single = grad_grid.astype(jnp.float32)
    delta_rows = jnp.sum(grad_single * attended_grid, axis=-1)
    key_total = cycle_rows * lax.axis_size("blk")
    back_state = (
        jnp.zeros((kv_local, per_group, cycle_rows, HD), jnp.float32),
        jnp.zeros((key_total, kv_local, HD), jnp.float32),
        jnp.zeros((key_total, kv_local, HD), jnp.float32),
    )
    folded = back_state
    operands, key_width = split_blocks(
        (
            lax.all_gather(key_head, "blk", axis=0, tiled=True),
            lax.all_gather(value_head, "blk", axis=0, tiled=True),
            lax.all_gather(segment_ids, "blk", axis=0, tiled=True),
            lax.all_gather(positions, "blk", axis=0, tiled=True),
        ),
        kv_local,
    )

    def backward_advance(status, block_in):
        key_block, value_block, seg_block, pos_block, block_index = block_in
        allowed = visible_pairs(segment_ids, positions, seg_block, pos_block)

        def backward_update(current):
            grad_query, grad_keys, grad_values = current
            scores = (
                jnp.einsum(
                    "kgqd,nkd->kgqn", query_grid, key_block, preferred_element_type=jnp.float32
                )
                * scale_factor
            )
            weights = jnp.where(allowed, jnp.exp(scores - log_total[..., None]), 0.0)
            grad_weights = jnp.einsum(
                "kgqd,nkd->kgqn", grad_grid, value_block, preferred_element_type=jnp.float32
            )
            grad_scores = (weights * (grad_weights - delta_rows[..., None])).astype(jnp.bfloat16)
            grad_query = grad_query + jnp.einsum(
                "kgqn,nkd->kgqd", grad_scores, key_block, preferred_element_type=jnp.float32
            )
            key_term = jnp.einsum(
                "kgqn,kgqd->nkd", grad_scores, query_grid, preferred_element_type=jnp.float32
            )
            value_term = jnp.einsum("kgqn,kgqd->nkd", weights, grad_single, precision=highest)
            first_row = block_index * key_width
            grad_keys = lax.dynamic_update_slice_in_dim(
                grad_keys,
                lax.dynamic_slice_in_dim(grad_keys, first_row, key_width, 0) + key_term,
                first_row,
                0,
            )
            grad_values = lax.dynamic_update_slice_in_dim(
                grad_values,
                lax.dynamic_slice_in_dim(grad_values, first_row, key_width, 0) + value_term,
                first_row,
                0,
            )
            return (grad_query, grad_keys, grad_values)

        return (lax.cond(jnp.any(allowed), backward_update, lambda current: current, status), None)

    folded, unused_out = lax.scan(backward_advance, folded, operands)
    grad_query, grad_keys, grad_values = folded
    key_own, value_own = (
        lax.psum_scatter(
            grad_keys.astype(jnp.bfloat16), "blk", scatter_dimension=0, tiled=True
        ).astype(jnp.float32),
        lax.psum_scatter(
            grad_values.astype(jnp.bfloat16), "blk", scatter_dimension=0, tiled=True
        ).astype(jnp.float32),
    )
    query_ret = (
        (grad_query * scale_factor)
        .transpose(2, 0, 1, 3)
        .reshape(cycle_rows, -1)
        .astype(jnp.bfloat16)
    )
    key_ret = (key_own * scale_factor).reshape(cycle_rows, -1).astype(jnp.bfloat16)
    value_ret = value_own.reshape(cycle_rows, -1).astype(jnp.bfloat16)
    query_tokgrad, key_tokgrad, value_tokgrad = (
        lax.all_to_all(query_ret, "head", split_axis=0, concat_axis=1, tiled=True),
        lax.all_to_all(key_ret, "head", split_axis=0, concat_axis=1, tiled=True),
        lax.all_to_all(value_ret, "head", split_axis=0, concat_axis=1, tiled=True),
    )
    grad_q_lin = rotate(query_tokgrad.astype(jnp.float32), own_positions, -1.0).astype(jnp.bfloat16)
    grad_k_lin = rotate(key_tokgrad.astype(jnp.float32), own_positions, -1.0).astype(jnp.bfloat16)
    grad_hidden_one = (
        dot_right_t(grad_q_lin, query_back)
        + dot_right_t(grad_k_lin, key_back)
        + dot_right_t(value_tokgrad, value_back)
    )
    query_grad = dot_left_t(hidden_one, grad_q_lin)
    key_grad = dot_left_t(hidden_one, grad_k_lin)
    value_grad = dot_left_t(hidden_one, value_tokgrad)
    grad_in_norm, gain_one_term = norm_back(
        grad_hidden_one, normed_one, scale_one, gain_first_b.astype(jnp.float32)
    )
    input_grad = grad_middle + grad_in_norm
    query_share, key_share, value_share, out_share, gain_one_share, gain_two_share = (
        lax.psum_scatter(query_grad, ("blk", "head"), scatter_dimension=0, tiled=True),
        lax.psum_scatter(key_grad, ("blk", "head"), scatter_dimension=0, tiled=True),
        lax.psum_scatter(value_grad, ("blk", "head"), scatter_dimension=0, tiled=True),
        lax.psum_scatter(out_grad, ("blk", "head"), scatter_dimension=0, tiled=True),
        lax.psum_scatter(gain_one_term, ("blk", "head"), scatter_dimension=0, tiled=True),
        lax.psum_scatter(gain_two_term, ("blk", "head"), scatter_dimension=0, tiled=True),
    )
    return (
        output,
        input_grad,
        gain_one_share,
        query_share,
        key_share,
        value_share,
        out_share,
        gain_two_share,
        gate_share,
        up_share,
        down_share,
    )


def solution(mesh):
    in_specs = (
        P(("grp", "blk", "head"), None),
        P(("blk", "head")),
        P(("blk", "head"), None),
        P(("blk", "head"), None),
        P(("blk", "head"), None),
        P(("blk", "head"), None),
        P(("blk", "head")),
        P(("blk", "head"), None),
        P(("blk", "head"), None),
        P(("blk", "head"), None),
        P(("grp", "blk", "head"), None),
        P(("grp", "blk")),
        P(("grp", "blk")),
    )
    out_specs = (
        P(("grp", "blk", "head"), None),
        P(("grp", "blk", "head"), None),
        P(("grp", "blk", "head")),
        P(("grp", "blk", "head"), None),
        P(("grp", "blk", "head"), None),
        P(("grp", "blk", "head"), None),
        P(("grp", "blk", "head"), None),
        P(("grp", "blk", "head")),
        P(("grp", "blk", "head"), None),
        P(("grp", "blk", "head"), None),
        P(("grp", "blk", "head"), None),
    )
    return jax.shard_map(
        per_device, mesh=mesh, in_specs=in_specs, out_specs=out_specs, check_vma=False
    )
```

profile of v0, /device:TPU:0, one launch (start us, length us, event | category | flops | bytes accessed | tf_op | source)
XLA Modules:
  0.0 5029.0 jit_solution(10484500154729583871)
XLA Ops:
  13.2 181.3 %all-reduce.17 = (bf16[768]{0:T(1024)(128)(2,1)S(1)}, bf16[768]{0:T(1024)(128)(2,1)}) all-reduce(bf16[768]{0:T(1024)(128)(2,1)S(1)} %dynamic-update-slice, bf16[768]{0:T(1024)(128)(2,1)S(1)} %dynamic-update-slice.1), channel_id=1, replica_groups=mesh['grp'=2,'blk'=32,'head'=2] {'blk','head'}, use_global_device_ids=true, to_apply=%add | all-reduce | flops 1536 | bytes 6144
  197.1 146.6 %all-gather.26.cloned.1.call-done = bf16[64,12,768]{2,1,0:T(8,128)(2,1)} async-done(((bf16[1,12,768]{2,1,0:T(8,128)(2,1)}), bf16[64,12,768]{2,1,0:T(8,128)(2,1)}) %all-gather.26.cloned.1.call-update) | async-done | bytes 1179664 | tf_op jit(solution)/shard_map/all_gather | solution.py:102
  346.0 329.0 %all-gather.24.cloned.1.call-done = bf16[64,12,768]{2,1,0:T(8,128)(2,1)} async-done(((bf16[1,12,768]{2,1,0:T(8,128)(2,1)}), bf16[64,12,768]{2,1,0:T(8,128)(2,1)}) %all-gather.24.cloned.1.call-update) | async-done | bytes 1179664 | tf_op jit(solution)/shard_map/all_gather | solution.py:103
  678.6 9.0 all_to_all.116
  688.5 317.7 %all-gather.28.cloned.1.call-done = bf16[64,12,768]{2,1,0:T(8,128)(2,1)} async-done(((bf16[1,12,768]{2,1,0:T(8,128)(2,1)}), bf16[64,12,768]{2,1,0:T(8,128)(2,1)}) %all-gather.28.cloned.1.call-update) | async-done | bytes 1179664 | tf_op jit(solution)/shard_map/all_gather | solution.py:104
  1008.9 9.4 all_to_all.117
  1025.3 79.9 %all-gather = s32[32,1,256]{2,1,0:T(1,128)S(1)} all-gather(s32[1,1,256]{2,1,0:T(1,128)S(1)} %bitcast.271), channel_id=1, replica_groups=mesh['grp'=2,'blk'=32,'head'=2] {'blk'}, dimensions={0}, use_global_device_ids=true | all-gather | bytes 33792 | tf_op jit(solution)/shard_map/all_gather | solution.py:141
  1105.9 75.5 %all-gather.1 = s32[32,1,256]{2,1,0:T(1,128)S(1)} all-gather(s32[1,1,256]{2,1,0:T(1,128)S(1)} %bitcast.278), channel_id=1, replica_groups=mesh['grp'=2,'blk'=32,'head'=2] {'blk'}, dimensions={0}, use_global_device_ids=true | all-gather | bytes 33792 | tf_op jit(solution)/shard_map/all_gather | solution.py:142
  1182.4 8.6 copy.94
  1196.8 6.3 copy.99
  1203.1 131.7 %all-gather.20.cloned.1.call-done = bf16[8192,384]{1,0:T(8,128)(2,1)} async-done(((bf16[256,384]{1,0:T(8,128)(2,1)}), bf16[8192,384]{1,0:T(8,128)(2,1)}) %all-gather.20.cloned.1.call-update) | async-done | bytes 6291472 | tf_op jit(solution)/shard_map/all_gather | solution.py:140
  1334.8 8.9 copy.98
  1349.4 6.3 copy.100
  1355.7 110.6 %while.35 = (s32[]{:T(128)}, f32[6,1,256]{2,0,1:T(8,128)S(1)}, f32[6,1,256]{2,0,1:T(8,128)S(1)}, f32[6,1,256,64]{2,3,0,1:T(8,128)S(1)}, s32[256,1]{0,1:T(1,128)S...) while((s32[]{:T(128)}, f32[6,1,256]{2,0,1:T(8,128)S(1)}, ...), condition=%wide.region_7.8_spmd, body=%wide.region_1.7_spmd.sunk | while | flops 713635584 | bytes 11856651 | solution.py:172
  1472.0 196.2 %all-gather.30.cloned.1.call-done = bf16[64,12,768]{2,1,0:T(8,128)(2,1)} async-done(((bf16[1,12,768]{2,1,0:T(8,128)(2,1)}), bf16[64,12,768]{2,1,0:T(8,128)(2,1)}) %all-gather.30.cloned.1.call-update) | async-done | bytes 1179664 | tf_op jit(solution)/shard_map/all_gather | solution.py:105
  1670.8 340.1 %all-gather.32.cloned.1.call-done = bf16[64,12,3072]{2,1,0:T(8,128)(2,1)} async-done(((bf16[1,12,3072]{2,1,0:T(8,128)(2,1)}), bf16[64,12,3072]{2,1,0:T(8,128)(2,1)}) %all-gather.32.cloned.1.call-update) | async-done | bytes 4718608 | tf_op jit(solution)/shard_map/all_gather | solution.py:182
  2010.9 7.5 reshape.357
  2018.4 333.5 %all-gather.34.cloned.1.call-done = bf16[64,12,3072]{2,1,0:T(8,128)(2,1)} async-done(((bf16[1,12,3072]{2,1,0:T(8,128)(2,1)}), bf16[64,12,3072]{2,1,0:T(8,128)(2,1)}) %all-gather.34.cloned.1.call-update) | async-done | bytes 4718608 | tf_op jit(solution)/shard_map/all_gather | solution.py:183
  2351.9 7.5 reshape.359
  2368.5 320.8 %all-gather.22.cloned.1.call-done = bf16[3072,768]{1,0:T(8,128)(2,1)} async-done(((bf16[48,768]{1,0:T(8,128)(2,1)}), bf16[3072,768]{1,0:T(8,128)(2,1)}) %all-gather.22.cloned.1.call-update) | async-done | bytes 4718608 | tf_op jit(solution)/shard_map/all_gather | solution.py:184
  2689.3 5.9 multiply_convert_fusion
  2720.4 6.1 broadcast.339
  2726.5 6.1 broadcast.339.clone
  2732.6 236.5 %while.36 = (s32[]{:T(128)}, f32[6,1,256,64]{2,3,0,1:T(8,128)S(1)}, f32[8192,6,64]{0,2,1:T(8,128)}, f32[8192,6,64]{0,2,1:T(8,128)}, s32[256,1]{0,1:T(1,128)S(1)}...) while((s32[]{:T(128)}, f32[6,1,256,64]{2,3,0,1:T(8,128)S(1)}, ...), condition=%wide.region_15.16_spmd.clone, body=%wide.region_11.15_spmd.clone.sunk | while | flops 1015129344 | bytes 46911040 | solution.py:290
  2736.6 15.9 conditional.6
  2746.6 5.9 fusion.45
  2760.2 15.9 conditional.6
  2770.2 5.9 fusion.45
  2783.8 15.9 conditional.6
  2793.8 5.9 fusion.45
  2803.5 15.9 conditional.6
  2813.5 6.0 fusion.45
  2827.1 15.9 conditional.6
  2850.7 15.9 conditional.6
  2870.4 15.9 conditional.6
  2880.4 5.9 fusion.45
  2890.2 15.9 conditional.6
  2900.1 6.0 fusion.45
  2909.9 15.9 conditional.6
  2919.8 5.9 fusion.45
  2929.6 15.9 conditional.6
  2939.6 6.0 fusion.45
  2953.2 15.9 conditional.6
  2963.2 5.9 fusion.45
  2969.1 8.1 convert_element_type.178
  2977.3 8.2 convert_element_type.186
  2992.6 6.2 fusion.99
  3008.1 212.2 %reduce-scatter.16.cloned.1.call-done = bf16[256,6,64]{0,2,1:T(8,128)(2,1)} async-done(((bf16[8192,6,64]{0,2,1:T(8,128)(2,1)}), bf16[256,6,64]{0,2,1:T(8,128)(2,1)}) %reduce-scatter.16.cloned.1.call-update) | async-done | bytes 196624 | tf_op jit(solution)/shard_map/reduce_scatter | solution.py:293
  3229.1 165.3 %reduce-scatter.18.cloned.1.call-done = bf16[256,6,64]{0,2,1:T(8,128)(2,1)} async-done(((bf16[8192,6,64]{0,2,1:T(8,128)(2,1)}), bf16[256,6,64]{0,2,1:T(8,128)(2,1)}) %reduce-scatter.18.cloned.1.call-update) | async-done | bytes 196624 | tf_op jit(solution)/shard_map/reduce_scatter | solution.py:296
  3404.4 7.2 all-to-all-done.7
  3413.6 978.3 %fusion.91 = (f32[16,768]{1,0:T(8,128)}, f32[16,768]{1,0:T(8,128)}, f32[16,768]{1,0:T(8,128)}, f32[16,768]{1,0:T(8,128)}, f32[16,3072]{1,0:T(8,128)S(1)}, /*index=5*/f32[16,3072]{1,0:T(8,128)}) fusion(f32[768,768]{1,0:T(8,128)} %fusion.84, f32[768,768]{1,0:T(8,128)} %fusion.82, f32[768,768]{1,0:T(8,128)} %fusion.80, f32[768,768]{1,0:T(8,128)} %fusion.77, ...), kind=kCustom, calls=%all-reduce-scatter.6 | all-reduce-scatter fusion | flops 9437185 | bytes 28901888
  4394.6 10.6 collective-permute-start.14
  4423.3 7.0 collective-permute-start.9
  4598.2 14.6 collective-permute-done.95
  4625.1 9.0 collective-permute-start.70
  4637.5 176.2 %all-reduce.16 = (f32[768]{0:T(1024)S(1)}, f32[768]{0:T(1024)S(1)}) all-reduce(f32[768]{0:T(1024)S(1)} %get-tuple-element.815, f32[768]{0:T(1024)S(1)} %copy-done.69), channel_id=4, replica_groups=mesh['grp'=2,'blk'=32,'head'=2] {'blk','head'}, use_global_device_ids=true, to_apply=%region_20.21.clone | all-reduce | flops 1536 | bytes 12288
  4827.2 10.7 collective-permute-start.92
  4837.9 14.1 collective-permute-start.91
  4855.2 14.8 concatenate.20
  4870.0 14.0 concatenate.21
  4884.1 14.0 concatenate.22
  4898.1 14.8 concatenate.23
  4945.7 30.0 concatenate.24
  4975.7 43.9 concatenate.25
  (899 shorter events, 694.8 us)
Async XLA Ops:
  7.2 336.5 %all-gather.26.cloned.1.call-start = ((), (), s32[]{:S(2)}) async-start(), calls=%async_computation.18 | async-start | bytes 1597440 | tf_op jit(solution)/shard_map/all_gather | solution.py:102
  7.9 667.0 %all-gather.24.cloned.1.call-start = ((), (), s32[]{:S(2)}) async-start(), calls=%async_computation.17 | async-start | bytes 1597440 | tf_op jit(solution)/shard_map/all_gather | solution.py:103
  8.7 997.5 %all-gather.28.cloned.1.call-start = ((), (), s32[]{:S(2)}) async-start(), calls=%async_computation.19 | async-start | bytes 1597440 | tf_op jit(solution)/shard_map/all_gather | solution.py:104
  9.4 1173.0 %all-gather.18.cloned.1.call-start = ((), (), s32[]{:S(2)}) async-start(), calls=%async_computation.11 | async-start | bytes 6488064 | tf_op jit(solution)/shard_map/all_gather | solution.py:139
  688.5 646.4 %all-gather.20.cloned.1.call-start = ((), (), s32[]{:S(2)}) async-start(), calls=%async_computation.12 | async-start | bytes 6488064 | tf_op jit(solution)/shard_map/all_gather | solution.py:140
  1018.3 649.8 %all-gather.30.cloned.1.call-start = ((), (), s32[]{:S(2)}) async-start(), calls=%async_computation.20 | async-start | bytes 1597440 | tf_op jit(solution)/shard_map/all_gather | solution.py:105
  1018.9 992.0 %all-gather.32.cloned.1.call-start = ((), (), s32[]{:S(2)}) async-start(), calls=%async_computation.21 | async-start | bytes 6389760 | tf_op jit(solution)/shard_map/all_gather | solution.py:182
  1019.6 1332.3 %all-gather.34.cloned.1.call-start = ((), (), s32[]{:S(2)}) async-start(), calls=%async_computation.22 | async-start | bytes 6389760 | tf_op jit(solution)/shard_map/all_gather | solution.py:183
  1021.1 161.0 %all-to-all-start.1 = ((bf16[128,2,384]{0,2,1:T(8,128)(2,1)}), bf16[128,2,384]{0,2,1:T(8,128)(2,1)S(1)}, u32[]{:S(2)}, u32[]{:S(2)}) async-start(bf16[128,2,384]{0,2,1:T(8,128)(2,1)} %bitcast.36), calls=%async_computation.1 | async-start | bytes 393216 | tf_op jit(solution)/shard_map/all_to_all | solution.py:122
  1024.5 1664.8 %all-gather.22.cloned.1.call-start = ((), (), s32[]{:S(2)}) async-start(), calls=%async_computation.13 | async-start | bytes 4792320 | tf_op jit(solution)/shard_map/all_gather | solution.py:184
  1467.2 892.2 %all-to-all-start.3 = ((bf16[2,128,384]{1,2,0:T(8,128)(2,1)}), bf16[2,128,384]{1,2,0:T(8,128)(2,1)S(1)}, u32[]{:S(2)}, u32[]{:S(2)}) async-start(bf16[2,128,384]{1,2,0:T(8,128)(2,1)} %copy.101), calls=%async_computation.3 | async-start | bytes 393216 | tf_op jit(solution)/shard_map/all_to_all | solution.py:177
  2709.6 510.7 %reduce-scatter.16.cloned.1.call-start = ((), (), s32[]{:S(2)}) async-start(), calls=%async_computation.14 | async-start | bytes 6488064 | tf_op jit(solution)/shard_map/reduce_scatter | solution.py:293
  2977.3 417.1 %reduce-scatter.18.cloned.1.call-start = ((), (), s32[]{:S(2)}) async-start(), calls=%async_computation.15 | async-start | bytes 6488064 | tf_op jit(solution)/shard_map/reduce_scatter | solution.py:296
  2985.5 2036.4 %reduce-scatter.20.cloned.1.call-start = ((), (), s32[]{:S(2)}) async-start(), calls=%async_computation.16 | async-start | bytes 9584640 | tf_op jit(solution)/shard_map/reduce_scatter | solution.py:219
  3004.6 217.4 %all-to-all-start.5 = ((bf16[2,128,384]{1,2,0:T(8,128)(2,1)}), bf16[2,128,384]{1,2,0:T(8,128)(2,1)S(1)}, u32[]{:S(2)}, u32[]{:S(2)}) async-start(bf16[2,128,384]{1,2,0:T(8,128)(2,1)} %copy.106), calls=%async_computation.5 | async-start | bytes 393216 | tf_op jit(solution)/shard_map/all_to_all | solution.py:309
  3222.0 174.0 %all-to-all-start.6 = ((bf16[2,128,384]{1,2,0:T(8,128)(2,1)}), bf16[2,128,384]{1,2,0:T(8,128)(2,1)S(1)}, u32[]{:S(2)}, u32[]{:S(2)}) async-start(bf16[2,128,384]{1,2,0:T(8,128)(2,1)} %copy.107), calls=%async_computation.7 | async-start | bytes 393216 | tf_op jit(solution)/shard_map/all_to_all | solution.py:310
  3396.1 15.6 all-to-all-start.7
  4392.7 22.0 collective-permute-start.15
  4394.6 28.7 collective-permute-start.14
  4405.2 25.0 collective-permute-start.13
  4416.7 16.9 collective-permute-start.12
  4419.5 16.0 collective-permute-start.11
  4421.4 19.4 collective-permute-start.10
  4423.3 19.4 collective-permute-start.9
  4430.2 16.8 collective-permute-start.8
  4433.5 16.7 collective-permute-start.7
  4435.4 17.0 collective-permute-start.6
  4442.7 18.1 collective-permute-start.4
  4477.1 16.4 collective-permute-start.22
  4517.9 16.1 collective-permute-start.38
  4524.4 16.6 collective-permute-start.36
  4552.8 15.6 collective-permute-start.56
  4557.0 18.1 collective-permute-start.55
  4558.4 19.8 collective-permute-start.54
  4563.4 18.5 collective-permute-start.53
  4564.7 21.8 collective-permute-start.52
  4568.4 19.5 collective-permute-start.51
  4587.8 24.9 collective-permute-start.95
  4589.7 25.6 collective-permute-start.78
  4591.8 25.7 collective-permute-start.77
  4593.1 29.0 collective-permute-start.76
  4596.2 28.9 collective-permute-start.75
  4613.4 20.7 collective-permute-start.74
  4615.3 199.6 %collective-permute-start.73 = (f32[16,3072]{1,0:T(8,128)S(1)}, f32[16,3072]{1,0:T(8,128)}, u32[]{:S(2)}, u32[]{:S(2)}) collective-permute-start(f32[16,3072]{1,0:T(8,128)S(1)} %get-tuple-element.887), channel_id=1, source_target_pairs={{0,10},{1,11},{2,12},{3,13},{4,14},{5,15},{6,16},{7,17},{8,18},{9,... | collective-permute-start | bytes 589832
  4617.5 198.7 %collective-permute-start.72 = (f32[16,3072]{1,0:T(8,128)S(1)}, f32[16,3072]{1,0:T(8,128)}, u32[]{:S(2)}, u32[]{:S(2)}) collective-permute-start(f32[16,3072]{1,0:T(8,128)S(1)} %get-tuple-element.887), channel_id=1, source_target_pairs={{0,9},{1,10},{2,11},{3,12},{4,13},{5,14},{6,15},{7,16},{8,17},{9,1... | collective-permute-start | bytes 589832
  4622.1 195.4 %collective-permute-start.71 = (f32[16,3072]{1,0:T(8,128)S(1)}, f32[16,3072]{1,0:T(8,128)}, u32[]{:S(2)}, u32[]{:S(2)}) collective-permute-start(f32[16,3072]{1,0:T(8,128)S(1)} %get-tuple-element.887), channel_id=1, source_target_pairs={{0,8},{1,9},{2,10},{3,11},{4,12},{5,13},{6,14},{7,15},{8,16},{9,17... | collective-permute-start | bytes 589832
  4625.1 193.7 %collective-permute-start.70 = (f32[16,3072]{1,0:T(8,128)S(1)}, f32[16,3072]{1,0:T(8,128)}, u32[]{:S(2)}, u32[]{:S(2)}) collective-permute-start(f32[16,3072]{1,0:T(8,128)S(1)} %get-tuple-element.887), channel_id=1, source_target_pairs={{0,7},{1,8},{2,9},{3,10},{4,11},{5,12},{6,13},{7,14},{8,15},{9,16}... | collective-permute-start | bytes 589832
  4634.8 185.4 %collective-permute-start.69 = (f32[16,3072]{1,0:T(8,128)S(1)}, f32[16,3072]{1,0:T(8,128)}, u32[]{:S(2)}, u32[]{:S(2)}) collective-permute-start(f32[16,3072]{1,0:T(8,128)S(1)} %get-tuple-element.887), channel_id=1, source_target_pairs={{0,6},{1,7},{2,8},{3,9},{4,10},{5,11},{6,12},{7,13},{8,14},{9,15},... | collective-permute-start | bytes 589832
  4818.8 19.0 collective-permute-start.65
  4820.2 31.8 collective-permute-start.64
  4823.3 89.6 %collective-permute-start.94 = (f32[16,3072]{1,0:T(8,128)}, f32[16,3072]{1,0:T(8,128)}, u32[]{:S(2)}, u32[]{:S(2)}) collective-permute-start(f32[16,3072]{1,0:T(8,128)} %get-tuple-element.888), channel_id=1, source_target_pairs={{0,15},{1,16},{2,17},{3,18},{4,19},{5,20},{6,21},{7,22},{8,23},{9,... | collective-permute-start | bytes 589832
  4825.2 89.1 %collective-permute-start.93 = (f32[16,3072]{1,0:T(8,128)}, f32[16,3072]{1,0:T(8,128)}, u32[]{:S(2)}, u32[]{:S(2)}) collective-permute-start(f32[16,3072]{1,0:T(8,128)} %get-tuple-element.888), channel_id=1, source_target_pairs={{0,14},{1,15},{2,16},{3,17},{4,18},{5,19},{6,20},{7,21},{8,22},{9,... | collective-permute-start | bytes 589832
  4827.2 90.6 %collective-permute-start.92 = (f32[16,3072]{1,0:T(8,128)}, f32[16,3072]{1,0:T(8,128)}, u32[]{:S(2)}, u32[]{:S(2)}) collective-permute-start(f32[16,3072]{1,0:T(8,128)} %get-tuple-element.888), channel_id=1, source_target_pairs={{0,13},{1,14},{2,15},{3,16},{4,17},{5,18},{6,19},{7,20},{8,21},{9,... | collective-permute-start | bytes 589832
  4837.9 81.2 %collective-permute-start.91 = (f32[16,3072]{1,0:T(8,128)}, f32[16,3072]{1,0:T(8,128)}, u32[]{:S(2)}, u32[]{:S(2)}) collective-permute-start(f32[16,3072]{1,0:T(8,128)} %get-tuple-element.888), channel_id=1, source_target_pairs={{0,12},{1,13},{2,14},{3,15},{4,16},{5,17},{6,18},{7,19},{8,20},{9,... | collective-permute-start | bytes 589832
  4852.0 71.4 %collective-permute-start.90 = (f32[16,3072]{1,0:T(8,128)}, f32[16,3072]{1,0:T(8,128)}, u32[]{:S(2)}, u32[]{:S(2)}) collective-permute-start(f32[16,3072]{1,0:T(8,128)} %get-tuple-element.888), channel_id=1, source_target_pairs={{0,11},{1,12},{2,13},{3,14},{4,15},{5,16},{6,17},{7,18},{8,19},{9,... | collective-permute-start | bytes 589832
  4914.3 16.6 collective-permute-start.88
  4917.8 16.9 collective-permute-start.87
  4919.1 18.5 collective-permute-start.86
  4923.4 16.9 collective-permute-start.85
  4926.0 49.6 collective-permute-start.84
  4930.9 44.7 collective-permute-start.83
  4934.7 40.9 collective-permute-start.82
  4937.6 38.1 collective-permute-start.81
  4940.3 35.4 collective-permute-start.80
  (165 other events, 10381.2 us)
Sparse Core Ops, SparseCore 0:
  9.7 333.9 all-gather.25
  345.3 329.5 all-gather.23
  676.6 329.5 all-gather.27
  1008.3 161.1 all-gather.17
  1171.0 163.8 all-gather.19
  1336.3 331.7 all-gather.29
  1669.8 341.0 all-gather.31
  2012.5 339.3 all-gather.33
  2353.5 335.7 all-gather.21
  2977.4 242.8 reduce-scatter.15
  3222.7 171.5 reduce-scatter.17
  3397.2 511.0 reduce-scatter.19
where the time goes:
time: 5050 us; the launch traced here: 5030 us
  waiting for transfers between devices  2530 us (50%)
  blocking collectives  1510 us (30%)
  starting transfers between devices  310 us (6%)
  local copies, waits for them, and re-layouts  266 us (5%)
  matrix products  266 us (5%)
  other arithmetic  104 us (2%)
    unnamed x3, blocking collectives  1340 us
    all_gather x1, waiting for transfers between devices, per_device(): lax.all_gather(w_gate, ('blk', 'head'), axis=0, tiled=True)  340 us
    all_gather x1, waiting for transfers between devices, per_device(): lax.all_gather(w_up, ('blk', 'head'), axis=0, tiled=True)  334 us
    all_gather x1, waiting for transfers between devices, per_device(): lax.all_gather(w_key, ('blk', 'head'), axis=0, tiled=True)  329 us
    all_gather x1, waiting for transfers between devices, per_device(): lax.all_gather(w_down, ('blk', 'head'), axis=0, tiled=True)  321 us
    all_gather x1, waiting for transfers between devices, per_device(): lax.all_gather(w_value, ('blk', 'head'), axis=0, tiled=True)  318 us
    unnamed x96, starting transfers between devices  287 us
    reduce_scatter x1, waiting for transfers between devices, per_device(): lax.psum_scatter(grad_keys.astype(jnp.bfloat16), 'blk', scatter_dimension...  212 us
  transfers between devices with their start and end apart: 114, of which 13 were waited for; matrix products, arithmetic and copies ran while one was open for 27% of the time, Pallas kernels for 0%

commit v1 on v0

v1 whole, which is shorter than its diff:
```python
import functools

import jax
import jax.numpy as jnp
import numpy as np
from jax import lax
from jax.experimental import pallas as pl
from jax.experimental.pallas import tpu as pltpu
from jax.sharding import PartitionSpec as P

MESH = pl.DeviceIdType.MESH
F32 = jnp.float32
BF16 = jnp.bfloat16
HD = 64
CONTS = 8
SLAB = 128
LOW = -1e30
EPS = 1e-05
MIB = 1 << 20
VMEM = pl.BlockSpec(memory_space=pltpu.VMEM)
SMEM = pl.BlockSpec(memory_space=pltpu.SMEM)


def feature_order():
    place = np.arange(768)
    p, z, r = place // 48, place // 12 % 4, place % 12
    t = (z % 2) * 32 + p * 2 + z // 2
    return t * 12 + r


ORDER = feature_order()
TO_PERM = np.zeros((768, 768), np.float32)
TO_PERM[ORDER, np.arange(768)] = 1.0


class Place:
    def __init__(self):
        self.core = lax.axis_index("grp")
        blk = lax.axis_index("blk")
        self.x = lax.rem(blk, 4)
        self.y = lax.rem(lax.div(blk, 4), 4)
        self.z = lax.axis_index("head") * 2 + lax.div(blk, 16)

    def device(self, x=None, y=None, z=None):
        x = self.x if x is None else x
        y = self.y if y is None else y
        z = self.z if z is None else z
        return (self.core, lax.rem(z, 2) * 16 + y * 4 + x, lax.div(z, 2))

    def ring(self, axis):
        return Ring(self, axis)


class Ring:
    def __init__(self, place, axis):
        self.place, self.axis = place, axis
        self.own = getattr(place, axis)
        self.next = lax.rem(self.own + 1, 4)
        self.prev = lax.rem(self.own + 3, 4)
        self.far = lax.rem(self.own + 2, 4)

    def device(self, index):
        return self.place.device(**{self.axis: index})


def enter(place, axes):
    barrier = pltpu.get_barrier_semaphore()
    partners = []
    for axis in axes:
        ring = place.ring(axis)
        partners += [ring.device(ring.next), ring.device(ring.prev)]
        if axis == "z":
            partners.append(ring.device(ring.far))
    for partner in partners:
        pl.semaphore_signal(barrier, inc=1, device_id=partner, device_id_type=MESH)
    pl.semaphore_wait(barrier, len(partners))


class Links:
    def __init__(self, send, recv):
        self.send, self.recv, self.used, self.sent = send, recv, 0, []

    def copy(self, source, target, device):
        k = self.used
        self.used += 1
        copy = pltpu.make_async_remote_copy(
            src_ref=source,
            dst_ref=target,
            send_sem=self.send.at[k],
            recv_sem=self.recv.at[k],
            device_id=device,
            device_id_type=MESH,
        )
        copy.start()
        self.sent.append(copy)
        return copy

    def finish(self):
        for copy in self.sent:
            copy.wait_send()


def together(steps):
    steps = list(steps)
    while steps:
        left = []
        for step in steps:
            try:
                next(step)
                left.append(step)
            except StopIteration:
                pass
        steps = left


def ring_gather(links, ring, slot):
    right = links.copy(slot(ring.own, None), slot(ring.own, None), ring.device(ring.next))
    left = links.copy(slot(ring.own, None), slot(ring.own, None), ring.device(ring.prev))
    yield
    right.wait_recv()
    on_right = links.copy(slot(ring.prev, 0), slot(ring.prev, 0), ring.device(ring.next))
    left.wait_recv()
    on_left = links.copy(slot(ring.next, 1), slot(ring.next, 1), ring.device(ring.prev))
    yield
    on_right.wait_recv()
    on_left.wait_recv()


def add_into(target, terms, kind):
    lead, rows, columns = target.shape
    step = 16
    for size in (128, 64, 48, 32):
        if rows % size == 0 and size * columns <= 48 * 1024:
            step = size
            break
    count = rows // step

    def body(k, carry):
        i, r = lax.div(k, count), pl.multiple_of(lax.rem(k, count) * step, step)
        total = terms[0][i, pl.ds(r, step), :].astype(F32)
        for term in terms[1:]:
            total = total + term[i, pl.ds(r, step), :].astype(F32)
        target[i, pl.ds(r, step), :] = total.astype(kind)
        return carry

    lax.fori_loop(0, lead * count, body, 0)


def ring_scatter(links, ring, part, room, target, kind):
    low, high, sum_low, sum_high, from_prev, from_next = room
    nxt, prv = ring.device(ring.next), ring.device(ring.prev)
    far_low = links.copy(part(ring.far, 0), low, nxt)
    far_high = links.copy(part(ring.far, 1), high, prv)
    next_high = links.copy(part(ring.next, 1), from_prev(1), nxt)
    prev_low = links.copy(part(ring.prev, 0), from_next(0), prv)
    yield
    far_low.wait_recv()
    add_into(sum_low, [part(ring.next, 0), low], BF16)
    next_low = links.copy(sum_low, from_prev(0), nxt)
    far_high.wait_recv()
    add_into(sum_high, [part(ring.prev, 1), high], BF16)
    prev_high = links.copy(sum_high, from_next(1), prv)
    yield
    for copy in (next_high, prev_low, next_low, prev_high):
        copy.wait_recv()
    add_into(target, [part(ring.own, None), from_prev(None), from_next(None)], kind)


def lead_part(part):
    return pl.ds(0, 4) if part is None else pl.ds(2 * part, 2)


def row_part(rows, part):
    first = (rows // 2 + 15) // 16 * 16
    if part is None:
        return 0, rows
    return (0, first) if part == 0 else (first, rows - first)


def regions(rows, columns, by_rows):
    if by_rows:
        return [(0, rows // 2, 0, columns), (rows // 2, rows // 2, 0, columns)]
    return [(0, rows, 0, columns // 2), (0, rows, columns // 2, columns // 2)]


def plane_gather(links, place, buf, by_rows):
    rows, columns = buf.shape[2:]

    def half(region, x_first):
        r0, rn, c0, cn = region

        def one(k, part):
            off, size = row_part(rn, part)
            y, x = (place.y, k) if x_first else (k, place.x)
            return buf.at[y, x, pl.ds(r0 + off, size), pl.ds(c0, cn)]

        def line(k, part):
            y, x = (k, lead_part(part)) if x_first else (lead_part(part), k)
            return buf.at[y, x, pl.ds(r0, rn), pl.ds(c0, cn)]

        yield from ring_gather(links, place.ring("x" if x_first else "y"), one)
        yield from ring_gather(links, place.ring("y" if x_first else "x"), line)

    a, b = regions(rows, columns, by_rows)
    return half(a, True), half(b, False)


def plane_scatter_room(rows, columns, by_rows):
    rooms = []
    for _, rn, _, cn in regions(rows, columns, by_rows):
        rooms += [pltpu.VMEM((2, rn, cn), BF16)] * 4 + [pltpu.VMEM((4, rn, cn), BF16)] * 3
        low, high = row_part(rn, 0)[1], row_part(rn, 1)[1]
        rooms += [pltpu.VMEM((1, low, cn), BF16), pltpu.VMEM((1, high, cn), BF16)] * 2
        rooms += [pltpu.VMEM((1, rn, cn), BF16)] * 2
    return rooms


def plane_scatter(links, place, buf, rooms, target, by_rows):
    rows, columns = buf.shape[2:]

    def half(region, room, x_first):
        r0, rn, c0, cn = region
        low, high, sum_low, sum_high, prev, nxt, lined = room[:7]
        low1, high1, sum_low1, sum_high1, prev1, nxt1 = room[7:]

        def line(k, part):
            y, x = (lead_part(part), k) if x_first else (k, lead_part(part))
            return buf.at[y, x, pl.ds(r0, rn), pl.ds(c0, cn)]

        def one(k, part):
            off, size = row_part(rn, part)
            return lined.at[pl.ds(k, 1), pl.ds(off, size), :]

        def lined_part(ref):
            return lambda part: ref.at[lead_part(part)]

        def one_part(ref):
            def view(part):
                off, size = row_part(rn, part)
                return ref.at[:, pl.ds(off, size), :]

            return view

        room_a = (low, high, sum_low, sum_high, lined_part(prev), lined_part(nxt))
        room_b = (low1, high1, sum_low1, sum_high1, one_part(prev1), one_part(nxt1))
        yield from ring_scatter(links, place.ring("x" if x_first else "y"), line, room_a, lined, BF16)
        out = target.at[:, pl.ds(r0, rn), pl.ds(c0, cn)]
        yield from ring_scatter(links, place.ring("y" if x_first else "x"), one, room_b, out, F32)

    a, b = regions(rows, columns, by_rows)
    return half(a, rooms[:13], False), half(b, rooms[13:], True)


def line_scatter_room(rows, columns):
    low, high = row_part(rows, 0)[1], row_part(rows, 1)[1]
    return [pltpu.VMEM((1, low, columns), BF16), pltpu.VMEM((1, high, columns), BF16)] * 2 + [
        pltpu.VMEM((1, rows, columns), BF16)
    ] * 2


def line_scatter(links, place, buf, room, target):
    rows = buf.shape[1]

    def part(k, half):
        off, size = row_part(rows, half)
        return buf.at[pl.ds(k, 1), pl.ds(off, size), :]

    def view(ref):
        def cut(half):
            off, size = row_part(rows, half)
            return ref.at[:, pl.ds(off, size), :]

        return cut

    low, high, sum_low, sum_high, prev, nxt = room
    yield from ring_scatter(
        links, place.ring("z"), part, (low, high, sum_low, sum_high, view(prev), view(nxt)), target, F32
    )


def line_gather(links, place, buf):
    rows = buf.shape[1]

    def slot(k, half):
        off, size = row_part(rows, half)
        return buf.at[k, pl.ds(off, size)]

    yield from ring_gather(links, place.ring("z"), slot)


def line_swap(links, place, source, target):
    ring = place.ring("z")
    copies = []
    for other in (ring.next, ring.prev, ring.far):
        copies.append(links.copy(source.at[other], target.at[ring.own], ring.device(other)))
    target[ring.own] = source[ring.own]
    yield
    for copy in copies:
        copy.wait_recv()


COPIES = {"line_gather": 4, "line_swap": 3, "plane_gather": 16, "line_scatter": 6, "plane_scatter": 24}


def exchange(collective_id, ops):
    axes = []
    for name, _, _ in ops:
        for axis in ("x", "y") if name.startswith("plane") else ("z",):
            if axis not in axes:
                axes.append(axis)
    shapes, rooms = [], []
    for name, array, by_rows in ops:
        shape = array.shape
        if name == "line_gather":
            shapes.append(jax.ShapeDtypeStruct((4,) + shape, array.dtype))
            rooms.append([])
        elif name == "line_swap":
            shapes.append(jax.ShapeDtypeStruct(shape, array.dtype))
            rooms.append([])
        elif name == "plane_gather":
            shapes.append(jax.ShapeDtypeStruct((4, 4) + shape, array.dtype))
            rooms.append([])
        elif name == "line_scatter":
            shapes.append(jax.ShapeDtypeStruct((1,) + shape[1:], F32))
            rooms.append(line_scatter_room(*shape[1:]))
        else:
            shapes.append(jax.ShapeDtypeStruct((1,) + shape[2:], F32))
            rooms.append(plane_scatter_room(shape[2], shape[3], by_rows))
    count = sum(COPIES[name] for name, _, _ in ops)
    flat = [room for group in rooms for room in group]

    def kernel(*refs):
        n = len(ops)
        ins, outs, scratch = refs[:n], refs[n : 2 * n], list(refs[2 * n :])
        send, recv = scratch[-2:]
        place = Place()
        enter(place, axes)
        links = Links(send, recv)
        steps, at = [], 0
        for (name, _, by_rows), source, target, room in zip(ops, ins, outs, rooms):
            own = scratch[at : at + len(room)]
            at += len(room)
            if name == "line_gather":
                target[place.z] = source[...]
                steps.append(line_gather(links, place, target))
            elif name == "line_swap":
                steps.append(line_swap(links, place, source, target))
            elif name == "plane_gather":
                target[place.y, place.x] = source[...]
                steps += plane_gather(links, place, target, by_rows)
            elif name == "line_scatter":
                steps.append(line_scatter(links, place, source, own, target))
            else:
                steps += plane_scatter(links, place, source, own, target, by_rows)
        together(steps)
        links.finish()

    return pl.pallas_call(
        kernel,
        out_shape=tuple(shapes),
        in_specs=[VMEM] * len(ops),
        out_specs=tuple([VMEM] * len(ops)),
        scratch_shapes=flat + [pltpu.SemaphoreType.DMA((count,))] * 2,
        compiler_params=pltpu.CompilerParams(
            collective_id=collective_id, has_side_effects=True, vmem_limit_bytes=60 * MIB
        ),
        name="exchange_" + str(collective_id),
    )(*[array for _, array, _ in ops])


def gather_weights(collective_id, to_line, down, hidden, cotangent, desc):
    columns = to_line.shape[2]
    width = columns + down.shape[1]
    count = 3 + 16 + 4 + 4 + 4 + 16

    def kernel(line_ref, down_ref, hid_ref, cot_ref, desc_ref, w_ref, hids_ref, cots_ref, descs_ref, rows, lined, send, recv):
        place = Place()
        enter(place, ("x", "y", "z"))
        links = Links(send, recv)

        def weights():
            yield from line_swap(links, place, line_ref, rows)
            i = lax.broadcasted_iota(jnp.int32, (48, 64), 0)
            k = lax.broadcasted_iota(jnp.int32, (48, 64), 1)
            pick = (k == lax.div(i, 12) * 16 + lax.rem(i, 12)).astype(BF16)
            for c in range(0, columns, 768):
                block = rows[:, :, pl.ds(c, 768)].reshape(64, 768)
                packed = jnp.dot(pick, block, preferred_element_type=F32).astype(BF16)
                w_ref[place.y, place.x, :, pl.ds(c, 768)] = packed
            w_ref[place.y, place.x, :, pl.ds(columns, 768)] = down_ref[...]
            yield
            halves = plane_gather(links, place, w_ref, False)
            while True:
                live = 0
                for half in halves:
                    live += next(half, 1) is None
                if not live:
                    return
                yield

        def describe():
            lined[place.z] = desc_ref[...]
            yield from line_gather_small(links, place, lined)
            descs_ref[place.y, place.x] = lined[0] + lined[1] + lined[2] + lined[3]
            yield from plane_gather_small(links, place, descs_ref)

        hids_ref[place.z] = hid_ref[...]
        cots_ref[place.z] = cot_ref[...]
        together(
            [
                line_gather(links, place, hids_ref),
                weights(),
                describe(),
                line_gather(links, place, cots_ref),
            ]
        )
        links.finish()

    return pl.pallas_call(
        kernel,
        out_shape=(
            jax.ShapeDtypeStruct((4, 4, 48, width), BF16),
            jax.ShapeDtypeStruct((4,) + hidden.shape, BF16),
            jax.ShapeDtypeStruct((4,) + cotangent.shape, BF16),
            jax.ShapeDtypeStruct((4, 4) + desc.shape, jnp.int32),
        ),
        in_specs=[VMEM] * 5,
        out_specs=(VMEM,) * 4,
        scratch_shapes=[
            pltpu.VMEM((4, 16, columns), BF16),
            pltpu.VMEM((4,) + desc.shape, jnp.int32),
            pltpu.SemaphoreType.DMA((count,)),
            pltpu.SemaphoreType.DMA((count,)),
        ],
        compiler_params=pltpu.CompilerParams(
            collective_id=collective_id, has_side_effects=True, vmem_limit_bytes=60 * MIB
        ),
        name="gather_weights",
    )(to_line, down, hidden, cotangent, desc)


def small_gather(links, ring, slot):
    right = links.copy(slot(ring.own), slot(ring.own), ring.device(ring.next))
    left = links.copy(slot(ring.own), slot(ring.own), ring.device(ring.prev))
    yield
    right.wait_recv()
    left.wait_recv()
    on = links.copy(slot(ring.prev), slot(ring.prev), ring.device(ring.next))
    yield
    on.wait_recv()


def line_gather_small(links, place, buf):
    yield from small_gather(links, place.ring("z"), lambda k: buf.at[k])


def plane_gather_small(links, place, buf):
    yield from small_gather(links, place.ring("x"), lambda k: buf.at[place.y, k])
    yield from small_gather(links, place.ring("y"), lambda k: buf.at[k])


def attend_kernel(meta, q_ref, kv_ref, out_ref, lse_ref):
    row = lax.broadcasted_iota(jnp.int32, (SLAB, 1), 0)
    lane = lax.broadcasted_iota(jnp.int32, (SLAB, SLAB), 1)

    def slab(s, carry):
        pos_q = meta[s, 20] + row
        queries = [q_ref[s, :, pl.ds(j * 128, 128)] for j in range(3)]

        def fold(state, places, first):
            width = len(places) * SLAB
            pos_k = first + lax.broadcasted_iota(jnp.int32, (1, width), 1)
            allowed = pos_k <= pos_q
            out = []
            for j in range(3):
                top, total, acc = state[j]
                keys = jnp.concatenate([kv_ref[at, :, pl.ds(j * 128, 128)] for at in places], 0)
                scores = lax.dot_general(queries[j], keys, (((1,), (1,)), ((), ())), preferred_element_type=F32)
                scores = jnp.where(allowed, scores, LOW)
                new_top = jnp.maximum(top, jnp.max(scores, axis=1, keepdims=True))
                weights = jnp.exp(scores - new_top)
                decay = jnp.exp(top - new_top)
                total = total * decay + jnp.sum(weights, axis=1, keepdims=True)
                acc = acc * decay + jnp.dot(weights.astype(BF16), keys, preferred_element_type=F32)
                out.append((new_top, total, acc))
            return tuple(out)

        start = tuple(
            (jnp.full((SLAB, 1), LOW, F32), jnp.zeros((SLAB, 1), F32), jnp.zeros((SLAB, SLAB), F32)) for _ in range(3)
        )

        def prompt(c, state):
            return fold(state, [meta[s, c * 4 + a] for a in range(4)], c * 512)

        def own(c, state):
            return fold(state, [meta[s, 16], meta[s, 17]], 2048)

        state = lax.fori_loop(0, meta[s, 18], prompt, start)
        state = lax.fori_loop(0, meta[s, 19], own, state)
        heads = [acc / total for _, total, acc in state]
        out_ref[s, :, 0:128] = jnp.where(lane < 64, pltpu.roll(heads[0], 64, 1), heads[1]).astype(BF16)
        out_ref[s, :, 128:256] = jnp.where(lane < 64, pltpu.roll(heads[2], 64, 1), 0.0).astype(BF16)
        logs = [top + jnp.log(total) for top, total, _ in state]
        lse_ref[s] = jnp.where(lane == 0, logs[0], jnp.where(lane == 1, logs[1], logs[2]))
        return carry

    lax.fori_loop(0, 4, slab, 0)


def attend(meta, q, kv):
    return pl.pallas_call(
        attend_kernel,
        out_shape=(jax.ShapeDtypeStruct((4, SLAB, 256), BF16), jax.ShapeDtypeStruct((4, SLAB, SLAB), F32)),
        in_specs=[SMEM, VMEM, VMEM],
        out_specs=(VMEM, VMEM),
        compiler_params=pltpu.CompilerParams(vmem_limit_bytes=60 * MIB),
        name="attend",
    )(meta, q, kv)


def attend_back_kernel(meta, q_ref, kv_ref, grad_ref, stat_ref, dq_ref, dkv_ref, acc_ref):
    lane = lax.broadcasted_iota(jnp.int32, (SLAB, SLAB), 1)
    which = lax.broadcasted_iota(jnp.int32, (8, SLAB), 0)

    def clear(k, carry):
        acc_ref[k] = jnp.zeros((SLAB, 384), F32)
        return carry

    lax.fori_loop(0, 64, clear, 0)

    def slab(s, carry):
        pos_q = meta[s, 20] + lax.broadcasted_iota(jnp.int32, (1, SLAB), 1)
        table = stat_ref[s]
        stats = [jnp.sum(jnp.where(which == k, table, 0.0), axis=0, keepdims=True) for k in range(6)]
        first = grad_ref[s, :, 0:128].astype(F32)
        last = grad_ref[s, :, 128:256].astype(F32)
        right = [pltpu.roll(first, 64, 1), first, pltpu.roll(last, 64, 1)]
        pairs = []
        for j in range(3):
            grads = jnp.where(lane < 64, 0.0, right[j]).astype(BF16)
            pairs.append(jnp.concatenate([q_ref[s, :, pl.ds(j * 128, 128)], grads], 0))
        for j in range(3):
            dq_ref[s, :, pl.ds(j * 128, 128)] = jnp.zeros((SLAB, SLAB), F32)

        def fold(places, first_key):
            width = len(places) * SLAB
            pos_k = first_key + lax.broadcasted_iota(jnp.int32, (width, 1), 0)
            allowed = pos_k <= pos_q
            for j in range(3):
                keys = jnp.concatenate([kv_ref[at, :, pl.ds(j * 128, 128)] for at in places], 0)
                both = lax.dot_general(keys, pairs[j], (((1,), (1,)), ((), ())), preferred_element_type=F32)
                weights = jnp.where(allowed, jnp.exp(both[:, :128] - stats[j]), 0.0)
                slopes = (weights * (both[:, 128:] - stats[3 + j])).astype(BF16)
                terms = jnp.dot(
                    jnp.concatenate([slopes, weights.astype(BF16)], 1), pairs[j], preferred_element_type=F32
                )
                for n, at in enumerate(places):
                    acc_ref[at, :, pl.ds(j * 128, 128)] += terms[n * 128 : (n + 1) * 128]
                dq_ref[s, :, pl.ds(j * 128, 128)] += lax.dot_general(
                    slopes, keys, (((0,), (0,)), ((), ())), preferred_element_type=F32
                )

        def prompt(c, state):
            fold([meta[s, c * 4 + a] for a in range(4)], c * 512)
            return state

        def own(c, state):
            fold([meta[s, 16], meta[s, 17]], 2048)
            return state

        lax.fori_loop(0, meta[s, 18], prompt, 0)
        lax.fori_loop(0, meta[s, 19], own, 0)
        return carry

    lax.fori_loop(0, 4, slab, 0)

    def store(k, carry):
        dkv_ref[k] = acc_ref[k].astype(BF16)
        return carry

    lax.fori_loop(0, 64, store, 0)


def attend_back(meta, q, kv, grads, stats):
    return pl.pallas_call(
        attend_back_kernel,
        out_shape=(jax.ShapeDtypeStruct((4, SLAB, 384), F32), jax.ShapeDtypeStruct((64, SLAB, 384), BF16)),
        in_specs=[SMEM, VMEM, VMEM, VMEM, VMEM],
        out_specs=(VMEM, VMEM),
        scratch_shapes=[pltpu.VMEM((64, SLAB, 384), F32)],
        compiler_params=pltpu.CompilerParams(vmem_limit_bytes=60 * MIB),
        name="attend_back",
    )(meta, q, kv, grads, stats)


def dot(left, right):
    return jnp.dot(left, right, preferred_element_type=F32)


def dot_right_t(left, right):
    return lax.dot_general(left, right, (((1,), (1,)), ((), ())), preferred_element_type=F32)


def dot_left_t(left, right):
    return lax.dot_general(left, right, (((0,), (0,)), ((), ())), preferred_element_type=F32)


def split_columns(w):
    rows = w.shape[0]
    return w.reshape(rows, 2, 16, 2, 48).transpose(3, 1, 0, 2, 4).reshape(4, rows, 768)


def join_columns(w):
    rows = w.shape[1]
    return w.reshape(2, 2, rows, 16, 48).transpose(2, 1, 3, 0, 4).reshape(rows, 3072)


def describe_queries(descs, own):
    seg, base = descs[:, :4, 0].reshape(64), descs[:, :4, 1].reshape(64)
    seg_q = lax.dynamic_slice(seg, (own * 4,), (4,))
    base_q = lax.dynamic_slice(base, (own * 4,), (4,))
    slabs = jnp.arange(64, dtype=jnp.int32)
    n = jnp.arange(18, dtype=jnp.int32)
    want = jnp.where(n[None] < 16, (seg_q // (CONTS + 1) * (CONTS + 1))[:, None], seg_q[:, None])
    hit = (seg[None, None] == want[:, :, None]) & (base[None, None] == (n * SLAB)[None, :, None])
    places = jnp.sum(jnp.where(hit, slabs[None, None], 0), axis=-1).astype(jnp.int32)
    follows = seg_q % (CONTS + 1) != 0
    blocks = jnp.where(follows, 4, base_q // 512 + 1)
    return jnp.concatenate(
        [places, blocks[:, None], follows[:, None].astype(jnp.int32), base_q[:, None], jnp.zeros((4, 3), jnp.int32)], 1
    )


def turns(base):
    positions = (base[:, None] + jnp.arange(SLAB, dtype=jnp.int32)[None]).reshape(-1)
    frequency = 10000.0 ** (-jnp.arange(32, dtype=F32) * 2.0 / HD)
    angles = positions.astype(F32)[:, None] * frequency[None]
    cosine, sine = jnp.cos(angles), jnp.sin(angles)
    rest = jnp.ones((positions.shape[0], 64), F32)
    return (
        jnp.concatenate([cosine, cosine, rest], 1)[:, None],
        jnp.concatenate([-sine, sine, 0.0 * rest], 1)[:, None],
    )


def rotate(field, cosine, sine):
    rows = field.shape[0]
    pieces = field.reshape(rows, 6, 128)
    swapped = jnp.concatenate([pieces[..., 32:64], pieces[..., :32], pieces[..., 64:]], -1)
    return pieces * cosine + swapped * sine


def per_device(
    tokens, gain_one, w_query, w_key, w_value, w_out, gain_two, w_gate, w_up, w_down, cotangent, segment_ids, positions
):
    blk, head = lax.axis_index("blk"), lax.axis_index("head")
    z, own = head * 2 + blk // 16, blk % 16
    to_perm = jnp.asarray(TO_PERM, BF16)
    first_gain, second_gain = gain_one.astype(F32)[:, None], gain_two.astype(F32)[:, None]

    def by_head(w):
        return w.reshape(12, 4, 3, HD)

    raw_qkv = jnp.stack([by_head(w_query), jnp.zeros((12, 4, 3, HD), BF16), by_head(w_key), by_head(w_value)], 3)
    raw_qkv = raw_qkv.transpose(1, 0, 2, 3, 4).reshape(4, 12, 768)
    raw_ff = jnp.concatenate([split_columns(w_gate), split_columns(w_up)], 2)
    to_line = jnp.concatenate(
        [
            (raw_qkv * first_gain).astype(BF16),
            (raw_ff * second_gain).astype(BF16),
            jnp.broadcast_to(w_out[None], (4, 12, 768)),
        ],
        2,
    )
    to_line = jnp.pad(to_line, ((0, 0), (0, 4), (0, 0)))
    seg_own = lax.dynamic_slice(segment_ids, (head * SLAB,), (1,))[0]
    base_own = lax.dynamic_slice(positions, (head * SLAB,), (1,))[0]
    row = lax.broadcasted_iota(jnp.int32, (8, SLAB), 0)
    lane = lax.broadcasted_iota(jnp.int32, (8, SLAB), 1)
    desc = jnp.where(row == z, jnp.where(lane == 0, seg_own, jnp.where(lane == 1, base_own, 0)), 0)

    inputs = tokens.astype(F32)
    scale_one = lax.rsqrt(jnp.mean(inputs * inputs, axis=-1, keepdims=True) + EPS)
    normed_one = inputs * scale_one
    normed_one_perm = dot(normed_one.astype(BF16), to_perm).astype(BF16)

    weights, line_one, line_cot, descs = gather_weights(0, to_line, w_down, normed_one_perm, cotangent, desc)
    weights = weights.reshape(768, 3840)
    line_one = line_one.reshape(512, 768)
    line_cot = line_cot.reshape(512, 768)
    w_qkv, w_ff, w_o, w_d = weights[:, :768], weights[:, 768:2304], weights[:, 2304:3072], weights[:, 3072:]
    descs = descs.reshape(16, 8, SLAB)
    meta = describe_queries(descs, own)
    cosine, sine = turns(meta[:, 20])

    qkv = rotate(dot(line_one, w_qkv), cosine, sine).reshape(512, 3, 2, 128)
    q = (qkv[:, :, 0] * 0.125).astype(BF16).reshape(4, SLAB, 384)
    kv_own = qkv[:, :, 1].astype(BF16).reshape(512, 384)
    (kv,) = exchange(1, [("plane_gather", kv_own, True)])
    kv = kv.reshape(64, SLAB, 384)
    heads_out, lse = attend(meta, q, kv)

    (attended,) = exchange(2, [("line_swap", heads_out, None)])
    attended = attended[:, :, :192].transpose(1, 0, 2).reshape(SLAB, 768)
    attended_perm = dot(attended, to_perm).astype(BF16)
    middle = inputs + dot(attended_perm, w_o)
    scale_two = lax.rsqrt(jnp.mean(middle * middle, axis=-1, keepdims=True) + EPS)
    normed_two = middle * scale_two
    normed_two_perm = dot(normed_two.astype(BF16), to_perm).astype(BF16)
    (line_two,) = exchange(3, [("line_gather", normed_two_perm, None)])
    line_two = line_two.reshape(512, 768)

    pre = dot(line_two, w_ff)
    gate_pre, up_pre = pre[:, :768], pre[:, 768:]
    sigmoid_gate = jax.nn.sigmoid(gate_pre)
    silu_gate = gate_pre * sigmoid_gate
    activated = (silu_gate * up_pre).astype(BF16)
    out_part = dot(activated, w_d).astype(BF16).reshape(4, SLAB, 768)
    grad_act = dot_right_t(line_cot, w_d)
    grad_gate = grad_act * up_pre * (sigmoid_gate * (1.0 + gate_pre * (1.0 - sigmoid_gate)))
    grad_pre = jnp.concatenate([grad_gate, grad_act * silu_gate], 1).astype(BF16)
    back_part = dot_right_t(grad_pre, w_ff).astype(BF16).reshape(4, SLAB, 768)
    ff_grads = jnp.concatenate([dot_left_t(line_two, grad_pre), dot_left_t(activated, line_cot)], 1).astype(BF16)
    back_sum, out_sum, ff_sum = exchange(
        4,
        [
            ("line_scatter", back_part, None),
            ("line_scatter", out_part, None),
            ("plane_scatter", ff_grads.reshape(4, 4, 48, 2304), False),
        ],
    )
    output = (middle + out_sum[0]).astype(BF16)

    grad_normed = dot_right_t(back_sum[0].astype(BF16), to_perm)
    grad_middle = cotangent.astype(F32) + scale_two * (
        grad_normed - normed_two * jnp.mean(grad_normed * normed_two, axis=-1, keepdims=True)
    )
    grad_low = grad_middle.astype(BF16)
    grad_attended = dot_right_t(dot_right_t(grad_low, w_o).astype(BF16), to_perm).astype(BF16)
    out_grad = dot_left_t(attended_perm, grad_low).astype(BF16).reshape(4, 4, 48, 768)
    to_heads = jnp.pad(grad_attended.reshape(SLAB, 4, 192).transpose(1, 0, 2), ((0, 0), (0, 0), (0, 64)))
    grad_heads, out_plane = exchange(5, [("line_swap", to_heads, None), ("plane_scatter", out_grad, False)])

    delta = (grad_heads.astype(F32) * heads_out.astype(F32))[:, :, :192].reshape(4, SLAB, 3, HD).sum(-1)
    stats = jnp.concatenate([lse[:, :, :3], delta, jnp.zeros((4, SLAB, 2), F32)], 2).transpose(0, 2, 1)
    dq, dkv = attend_back(meta, q, kv, grad_heads, stats)
    (dkv_own,) = exchange(6, [("plane_scatter", dkv.reshape(4, 4, 512, 384), True)])

    pieces = jnp.concatenate([dq.reshape(512, 3, 1, 128) * 0.125, dkv_own.reshape(512, 3, 1, 128)], 2)
    pieces = rotate(pieces.reshape(512, 768), cosine, -sine).reshape(512, 3, 2, 2, HD)
    blank = jnp.asarray(np.array([[1.0, 0.0], [1.0, 1.0]], np.float32))[None, None, :, :, None]
    grad_qkv = jnp.where(blank > 0, pieces, 0.0).astype(BF16).reshape(512, 768)
    one_part = dot_right_t(grad_qkv, w_qkv).astype(BF16).reshape(4, SLAB, 768)
    qkv_grads = dot_left_t(line_one, grad_qkv).astype(BF16).reshape(4, 4, 48, 768)
    one_sum, qkv_plane = exchange(7, [("line_scatter", one_part, None), ("plane_scatter", qkv_grads, False)])

    grad_normed = dot_right_t(one_sum[0].astype(BF16), to_perm)
    input_grad = grad_middle + scale_one * (
        grad_normed - normed_one * jnp.mean(grad_normed * normed_one, axis=-1, keepdims=True)
    )

    to_rows = jnp.concatenate([qkv_plane[0], ff_sum[0, :, :1536], out_plane[0]], 1).reshape(4, 12, 3072)
    to_rows = jnp.pad(to_rows, ((0, 0), (0, 4), (0, 0)))
    (from_line,) = exchange(8, [("line_swap", to_rows, None)])
    from_line = from_line[:, :12]
    got_qkv, got_ff, got_out = from_line[:, :, :768], from_line[:, :, 768:2304], from_line[:, :, 2304:]
    by_kind = got_qkv.reshape(4, 12, 3, 4, HD).transpose(3, 1, 0, 2, 4).reshape(4, 12, 768)
    gain_one_grad = jnp.sum(got_qkv * raw_qkv.astype(F32), axis=(0, 2))
    gain_two_grad = jnp.sum(got_ff * raw_ff.astype(F32), axis=(0, 2))
    return (
        output,
        input_grad,
        gain_one_grad,
        by_kind[0] * first_gain,
        by_kind[2] * first_gain,
        by_kind[3] * first_gain,
        jnp.sum(got_out, axis=0),
        gain_two_grad,
        join_columns(got_ff[:, :, :768]) * second_gain,
        join_columns(got_ff[:, :, 768:]) * second_gain,
        ff_sum[0, :, 1536:],
    )


def solution(mesh):
    rows = P(("grp", "blk", "head"), None)
    flat = P(("grp", "blk", "head"))
    weight = P(("blk", "head"), None)
    gain = P(("blk", "head"))
    ids = P(("grp", "blk"))
    in_specs = (rows, gain, weight, weight, weight, weight, gain, weight, weight, weight, rows, ids, ids)
    out_specs = (rows, rows, flat, rows, rows, rows, rows, flat, rows, rows, rows)
    return jax.shard_map(per_device, mesh=mesh, in_specs=in_specs, out_specs=out_specs, check_vma=False)
```

time: 5050 us -> 395 us (0.08)
  waiting for transfers between devices: 2530 us -> 0 us
  blocking collectives: 1510 us -> 0 us
  starting transfers between devices: 310 us -> 0 us
  Pallas kernels: 0 us -> 291 us
  matrix products: 266 us -> 34.9 us
  local copies, waits for them, and re-layouts: 266 us -> 39.1 us
  other arithmetic: 104 us -> 27.1 us
    all_gather x9 -> x0, waiting for transfers between devices: 2120 us -> none  [the longest x1 340 us: per_device(): lax.all_gather(w_gate, ('blk', 'head'), axis=0, tiled=True)]
    unnamed x3 -> x0, blocking collectives: 1340 us -> none
    reduce_scatter x3 -> x0, waiting for transfers between devices: 378 us -> none  [the longest x1 212 us: per_device(): lax.psum_scatter(grad_keys.astype(jnp.bfloat16), 'blk', scatter_dimension...]
    pallas_call x0 -> x11, Pallas kernels: none -> 291 us  [the longest x8 189 us: exchange(): pl.pallas_call(kernel, out_shape=tuple(shapes), in_specs=[VMEM] * len(ops...]
    unnamed x96 -> x0, starting transfers between devices: 287 us -> none
    dot_general x84 -> x7, matrix products: 225 us -> 11.6 us  [dot(): return jnp.dot(left, right, preferred_element_type=F32)]
    unnamed x175 -> x87, local copies, waits for them, and re-layouts: 185 us -> 3.82 us
    all_gather x2 -> x0, blocking collectives: 155 us -> none  [the longest x1 79.9 us: per_device(): lax.all_gather(segment_ids, 'blk', axis=0, tiled=True)]
  transfers between devices with their start and end apart: 114 -> 0, of which waited for: 13 -> 0; matrix products, arithmetic and copies ran while one was open for 27% -> 0% of each run, Pallas kernels for 0% -> 0%
where the time goes in v1:
time: 395 us; the launch traced here: 394 us
  Pallas kernels  291 us (74%)
  local copies, waits for them, and re-layouts  39.1 us (10%)
  matrix products  34.9 us (9%)
  other arithmetic  27.1 us (7%)
    pallas_call x8, Pallas kernels, exchange(): pl.pallas_call(kernel, out_shape=tuple(shapes), in_specs=[VMEM] * len(ops...  189 us
    pallas_call x1, Pallas kernels, gather_weights(): pl.pallas_call(kernel, out_shape=(jax.ShapeDtypeStruct((4, 4, 48, width),...  65.6 us
    pallas_call x1, Pallas kernels, attend_back(): pl.pallas_call(attend_back_kernel, out_shape=(jax.ShapeDtypeStruct((4, SL...  20.3 us
    pallas_call x1, Pallas kernels, attend(): pl.pallas_call(attend_kernel, out_shape=(jax.ShapeDtypeStruct((4, SLAB, 2...  16.5 us
    dot_general x6, matrix products, dot_right_t(): lax.dot_general(left, right, (((1,), (1,)), ((), ())), preferred_element_...  13.7 us
    dot_general x7, matrix products, dot(): return jnp.dot(left, right, preferred_element_type=F32)  11.6 us
    dot_general x4, matrix products, dot_left_t(): lax.dot_general(left, right, (((0,), (0,)), ((), ())), preferred_element_...  9.67 us

profile of v1, /device:TPU:0, one launch (start us, length us, event | category | flops | bytes accessed | tf_op | source)
XLA Modules:
  0.0 393.9 jit_solution(15046170945482976125)
XLA Ops:
  0.7 0.8 broadcast_in_dim.113
  2.1 1.1 reshape.432
  3.5 1.1 reshape.430
  6.7 0.8 fusion.35.line_ref
  7.7 1.1 convolution_convert_fusion.10.hid_ref
  10.6 1.3 select_select_fusion.desc_ref
  11.9 65.6 %gather_weights.1 = (bf16[4,4,48,3840]{3,2,1,0:T(8,128)(2,1)}, bf16[4,128,768]{2,1,0:T(8,128)(2,1)}, bf16[4,128,768]{2,1,0:T(8,128)(2,1)}, s32[4,4,8,128]{3,2,1,0:T(8,128)}) custom-call(bf16[4,16,3072]{2,1,0:T(8,128)(2,1)} %fusion.35.line_ref, bf16[48,768]{1,0:T(8,128)(2,1)} %down_ref.1, bf16[128,768]{1,0:T(8,128)(2,1)} %convolution_convert_fusion.10.hid_ref, ...), custom_call_target="tpu_custom_call" | custom-call | tf_op jit(solution)/shard_map/gather_weights/pallas_call | solution.py:419
  77.5 1.6 slice_reduce_fusion.4
  81.1 1.3 slice_bitcast_fusion
  82.5 1.7 copy.134
  84.1 2.3 fusion.56
  86.5 1.1 copy-done.2
  88.2 0.8 fusion.52
  89.0 1.9 fusion.4
  91.0 0.8 fusion.20
  91.8 1.1 convert_element_type.163
  92.9 1.0 copy.138.q_ref
  94.0 0.9 copy.137.refs_0_
  94.9 40.3 %exchange_1.1 = bf16[4,4,512,384]{3,2,1,0:T(8,128)(2,1)} custom-call(bf16[512,384]{1,0:T(8,128)(2,1)} %copy.137.refs_0_), custom_call_target="tpu_custom_call" | custom-call | tf_op jit(solution)/shard_map/exchange_1/pallas_call | solution.py:358
  135.2 16.5 %attend.1 = (bf16[4,128,256]{2,1,0:T(8,128)(2,1)}, f32[4,128,128]{2,1,0:T(8,128)}) custom-call(s32[4,24]{1,0:T(4,128)} %concatenate.58.meta, bf16[4,128,384]{2,1,0:T(8,128)(2,1)} %copy.138.q_ref, bf16[64,128,384]{2,1,0:T(8,128)(2,1)} %bitcast.140), custom_call_target="tpu_custom_call" | custom-call | tf_op jit(solution)/shard_map/attend/pallas_call | solution.py:511
  151.7 8.5 %exchange_2.1 = bf16[4,128,256]{2,1,0:T(8,128)(2,1)} custom-call(bf16[4,128,256]{2,1,0:T(8,128)(2,1)} %get-tuple-element.29.refs_0_), custom_call_target="tpu_custom_call" | custom-call | tf_op jit(solution)/shard_map/exchange_2/pallas_call | solution.py:358
  160.2 1.0 slice_bitcast_fusion.1
  161.7 1.7 multiply_reduce_fusion.1
  163.4 1.1 convolution_convert_fusion.8.refs_0_
  164.5 12.2 %exchange_3.1 = bf16[4,128,768]{2,1,0:T(8,128)(2,1)} custom-call(bf16[128,768]{1,0:T(8,128)(2,1)} %convolution_convert_fusion.8.refs_0_), custom_call_target="tpu_custom_call" | custom-call | tf_op jit(solution)/shard_map/exchange_3/pallas_call | solution.py:358
  176.7 3.4 fusion.2
  180.2 2.7 multiply_convert_fusion.2
  182.9 2.3 fusion.10
  185.2 1.7 convolution_convert_fusion.5
  186.9 1.2 copy.141
  188.0 3.2 convolution_convert_fusion.3
  191.3 1.2 copy.140
  192.5 3.1 convolution_convert_fusion
  195.6 2.1 pad_maximum_fusion.refs_2_
  197.7 36.4 %exchange_4.1 = (f32[1,128,768]{2,1,0:T(8,128)}, f32[1,128,768]{2,1,0:T(8,128)}, f32[1,48,2304]{2,1,0:T(8,128)}) custom-call(bf16[4,128,768]{2,1,0:T(8,128)(2,1)} %bitcast.173, bf16[4,128,768]{2,1,0:T(8,128)(2,1)} %bitcast.174, bf16[4,4,48,2304]{3,2,1,0:T(8,128)(2,1)} %pad_maximum_fusion.refs_2_), custom_call_target="tpu_custom_call" | custom-call | tf_op jit(solution)/shard_map/exchange_4/pallas_call | solution.py:358
  234.1 1.7 multiply_reduce_fusion
  236.6 2.3 convolution_convert_fusion.6
  239.3 0.8 pad.13.refs_0_
  240.0 1.5 convolution_convert_fusion.2
  241.5 20.7 %exchange_5.1 = (bf16[4,128,256]{2,1,0:T(8,128)(2,1)}, f32[1,48,768]{2,1,0:T(8,128)}) custom-call(bf16[4,128,256]{2,1,0:T(8,128)(2,1)} %pad.13.refs_0_, bf16[4,4,48,768]{3,2,1,0:T(8,128)(2,1)} %bitcast.150), custom_call_target="tpu_custom_call" | custom-call | tf_op jit(solution)/shard_map/exchange_5/pallas_call | solution.py:358
  262.3 1.0 convert_multiply_fusion.2
  264.4 20.3 %attend_back.1 = (f32[4,128,384]{2,1,0:T(8,128)}, bf16[64,128,384]{2,1,0:T(8,128)(2,1)}) custom-call(s32[4,24]{1,0:T(4,128)} %concatenate.58.meta, bf16[4,128,384]{2,1,0:T(8,128)(2,1)} %copy.138.q_ref, bf16[64,128,384]{2,1,0:T(8,128)(2,1)} %bitcast.141, bf16[4,128,256]{2,1,0:T(8,128)(2,1)} %get-tuple-element.33.grad_ref, ...), custom_call_target="tpu_custom_call" | custom-call | tf_op jit(solution)/shard_map/attend_back/pallas_call | solution.py:585
  284.7 36.9 %exchange_6.1 = f32[1,512,384]{2,1,0:T(8,128)} custom-call(bf16[4,4,512,384]{3,2,1,0:T(8,128)(2,1)} %bitcast.147), custom_call_target="tpu_custom_call" | custom-call | tf_op jit(solution)/shard_map/exchange_6/pallas_call | solution.py:358
  321.6 1.5 copy.148
  323.8 0.9 copy-done.1
  324.7 1.3 pad_maximum_fusion.2
  326.0 1.9 copy.150
  328.9 0.9 pad_maximum_fusion.3
  329.8 1.6 copy.151
  331.4 2.8 copy.149
  334.5 0.8 maximum_negate_fusion
  335.5 2.3 fusion.8
  337.8 3.0 convolution_convert_fusion.4
  340.8 1.6 copy.152
  342.6 2.0 select_convert_fusion
  344.7 1.1 copy-done.34
  345.8 1.9 convolution_convert_fusion.1
  347.6 22.3 %exchange_7.1 = (f32[1,128,768]{2,1,0:T(8,128)}, f32[1,48,768]{2,1,0:T(8,128)}) custom-call(bf16[4,128,768]{2,1,0:T(8,128)(2,1)} %bitcast.183, bf16[4,4,48,768]{3,2,1,0:T(8,128)(2,1)} %bitcast.159), custom_call_target="tpu_custom_call" | custom-call | tf_op jit(solution)/shard_map/exchange_7/pallas_call | solution.py:358
  370.0 1.7 fusion.29
  371.7 0.9 fusion.32
  372.8 1.0 select_maximum_fusion.refs_0_
  373.7 11.4 %exchange_8.1 = f32[4,16,3072]{2,1,0:T(8,128)} custom-call(f32[4,16,3072]{2,1,0:T(8,128)} %select_maximum_fusion.refs_0_), custom_call_target="tpu_custom_call" | custom-call | tf_op jit(solution)/shard_map/exchange_8/pallas_call | solution.py:358
  385.2 2.1 fusion.55
  392.4 0.8 broadcast_multiply_fusion.1
  (182 shorter events, 18.4 us)
Async XLA Ops:
  0.6 5.0 %copy-start.25 = (bf16[12,768]{1,0:T(8,128)(2,1)S(1)}, bf16[12,768]{1,0:T(8,128)(2,1)}, u32[]{:S(2)}) copy-start(bf16[12,768]{1,0:T(8,128)(2,1)} %param.19) | copy-start | bytes 55300
  0.7 5.1 %copy-start.26 = (bf16[12,768]{1,0:T(8,128)(2,1)S(1)}, bf16[12,768]{1,0:T(8,128)(2,1)}, u32[]{:S(2)}) copy-start(bf16[12,768]{1,0:T(8,128)(2,1)} %param.18) | copy-start | bytes 55300
  0.7 5.2 %copy-start.27 = (bf16[12,768]{1,0:T(8,128)(2,1)S(1)}, bf16[12,768]{1,0:T(8,128)(2,1)}, u32[]{:S(2)}) copy-start(bf16[12,768]{1,0:T(8,128)(2,1)} %param.17) | copy-start | bytes 55300
  2.1 3.6 copy-start.30
  3.5 1.6 copy-start.14
  4.7 1.9 copy-start.38
  5.0 0.6 copy-start.16
  5.6 1.9 copy-start.8
  5.7 1.9 copy-start
  6.4 2.3 copy-start.36
  6.4 3.6 copy-start.37
  6.6 70.9 %copy-start.10 = (f32[4,12,768]{2,1,0:T(8,128)}, f32[4,12,768]{2,1,0:T(8,128)S(1)}, u32[]{:S(2)}) copy-start(f32[4,12,768]{2,1,0:T(8,128)S(1)} %reshape.461) | copy-start | bytes 442372
  86.4 1.2 copy-start.2
  87.6 1.4 slice-start
  87.7 3.2 copy-start.28
  89.0 2.0 copy-start.6
  176.7 3.5 copy-start.35
  176.7 6.2 %slice-start.1 = ((s8[5898240]{0:T(1024)(128)(4,1)}), s8[4194304]{0:T(1024)(128)(4,1)S(1)}, s32[]{:S(2)}) async-start(s8[5898240]{0:T(1024)(128)(4,1)} %bitcast.168), calls=%async_computation.1 | async-start | bytes 8388608
  180.1 2.7 slice-start.2
  182.8 2.4 copy-start.39
  182.8 2.4 copy-start.40
  188.0 3.2 copy-start.7
  192.5 3.1 copy-start.12
  234.1 1.7 copy-start.19
  234.1 1.7 copy-start.21
  236.6 3.4 copy-start.3
  240.0 22.2 %copy-start.13 = (bf16[4,128,256]{2,1,0:T(8,128)(2,1)S(1)}, bf16[4,128,256]{2,1,0:T(8,128)(2,1)}, u32[]{:S(2)}) copy-start(bf16[4,128,256]{2,1,0:T(8,128)(2,1)} %get-tuple-element.29.refs_0_) | copy-start | bytes 786436
  241.5 22.0 %copy-start.22 = (f32[4,128,128]{2,1,0:T(8,128)S(1)}, f32[4,128,128]{2,1,0:T(8,128)}, u32[]{:S(2)}) copy-start(f32[4,128,128]{2,1,0:T(8,128)} %get-tuple-element.34) | copy-start | bytes 786436
  321.6 1.5 copy-start.18
  323.8 0.9 copy-start.1
  331.4 2.8 copy-start.29
  331.4 3.9 copy-start.32
  340.8 1.7 copy-start.33
  344.6 1.1 copy-start.34
  347.6 22.3 %copy-start.9 = (bf16[128,768]{1,0:T(8,128)(2,1)S(1)}, bf16[128,768]{1,0:T(8,128)(2,1)}, u32[]{:S(2)}) copy-start(bf16[128,768]{1,0:T(8,128)(2,1)} %param.15) | copy-start | bytes 589828
  369.9 1.8 copy-start.4
  369.9 2.7 copy-start.23
  369.9 2.7 copy-start.20
  371.7 1.1 copy-start.24
  372.8 12.4 %copy-start.11 = (f32[4,12,768]{2,1,0:T(8,128)S(1)}, f32[4,12,768]{2,1,0:T(8,128)}, u32[]{:S(2)}) copy-start(f32[4,12,768]{2,1,0:T(8,128)} %copy-done.10) | copy-start | bytes 442372
  385.2 4.2 %copy-start.5 = (f32[4,16,3072]{2,1,0:T(8,128)S(1)}, f32[4,16,3072]{2,1,0:T(8,128)}, u32[]{:S(2)}) copy-start(f32[4,16,3072]{2,1,0:T(8,128)} %exchange_8.1) | copy-start | bytes 2359300
  385.2 4.1 %copy-start.15 = (bf16[4,12,768]{2,1,0:T(8,128)(2,1)S(1)}, bf16[4,12,768]{2,1,0:T(8,128)(2,1)}, u32[]{:S(2)}) copy-start(bf16[4,12,768]{2,1,0:T(8,128)(2,1)} %copy-done.14) | copy-start | bytes 221188
  385.2 4.1 %copy-start.17 = (bf16[4,12,768]{2,1,0:T(8,128)(2,1)S(1)}, bf16[4,12,768]{2,1,0:T(8,128)(2,1)}, u32[]{:S(2)}) copy-start(bf16[4,12,768]{2,1,0:T(8,128)(2,1)} %copy-done.16) | copy-start | bytes 221188
  390.7 1.7 copy-start.31

commit v2 on v1

v2 whole, which is shorter than its diff:
```python
import functools

import jax
import jax.numpy as jnp
import numpy as np
from jax import lax
from jax.experimental import pallas as pl
from jax.experimental.pallas import tpu as pltpu
from jax.sharding import PartitionSpec as P

MESH = pl.DeviceIdType.MESH
F32 = jnp.float32
BF16 = jnp.bfloat16
HD = 64
CONTS = 8
SLAB = 128
LOW = -1e30
EPS = 1e-05
LANES = (((1,), (1,)), ((), ()))
HIGHEST = lax.Precision.HIGHEST
MIB = 1 << 20
VMEM = pl.BlockSpec(memory_space=pltpu.VMEM)
SMEM = pl.BlockSpec(memory_space=pltpu.SMEM)


def feature_order():
    place = np.arange(768)
    p, z, r = place // 48, place // 12 % 4, place % 12
    t = (z % 2) * 32 + p * 2 + z // 2
    return t * 12 + r


ORDER = feature_order()
TO_PERM = np.zeros((768, 768), np.float32)
TO_PERM[ORDER, np.arange(768)] = 1.0


LANE_FREQUENCY = 10000.0 ** (-(np.arange(128) % 32) * 2.0 / HD) * (np.arange(128) < HD)
FREQUENCY = LANE_FREQUENCY.astype(np.float32)
OFFSET_ANGLES = np.arange(SLAB)[:, None] * LANE_FREQUENCY[None]
OFFSET_TURNS = np.stack([np.cos(OFFSET_ANGLES), np.sin(OFFSET_ANGLES)]).astype(np.float32)


class Place:
    def __init__(self):
        self.core = lax.axis_index("grp")
        blk = lax.axis_index("blk")
        self.x = lax.rem(blk, 4)
        self.y = lax.rem(lax.div(blk, 4), 4)
        self.z = lax.axis_index("head") * 2 + lax.div(blk, 16)

    def device(self, x=None, y=None, z=None):
        x = self.x if x is None else x
        y = self.y if y is None else y
        z = self.z if z is None else z
        return (self.core, lax.rem(z, 2) * 16 + y * 4 + x, lax.div(z, 2))

    def ring(self, axis):
        return Ring(self, axis)


class Ring:
    def __init__(self, place, axis):
        self.place, self.axis = place, axis
        self.own = getattr(place, axis)
        self.next = lax.rem(self.own + 1, 4)
        self.prev = lax.rem(self.own + 3, 4)
        self.far = lax.rem(self.own + 2, 4)

    def device(self, index):
        return self.place.device(**{self.axis: index})


def enter(place, axes):
    barrier = pltpu.get_barrier_semaphore()
    partners = []
    for axis in axes:
        ring = place.ring(axis)
        partners += [ring.device(ring.next), ring.device(ring.prev)]
        if axis == "z":
            partners.append(ring.device(ring.far))
    for partner in partners:
        pl.semaphore_signal(barrier, inc=1, device_id=partner, device_id_type=MESH)
    pl.semaphore_wait(barrier, len(partners))


class Links:
    def __init__(self, send, recv):
        self.send, self.recv, self.used, self.sent = send, recv, 0, []

    def copy(self, source, target, device):
        k = self.used
        self.used += 1
        copy = pltpu.make_async_remote_copy(
            src_ref=source,
            dst_ref=target,
            send_sem=self.send.at[k],
            recv_sem=self.recv.at[k],
            device_id=device,
            device_id_type=MESH,
        )
        copy.start()
        self.sent.append(copy)
        return copy

    def finish(self):
        for copy in self.sent:
            copy.wait_send()


def together(steps):
    steps = list(steps)
    while steps:
        left = []
        for step in steps:
            try:
                next(step)
                left.append(step)
            except StopIteration:
                pass
        steps = left


def ring_gather(links, ring, slot):
    right = links.copy(slot(ring.own, None), slot(ring.own, None), ring.device(ring.next))
    left = links.copy(slot(ring.own, None), slot(ring.own, None), ring.device(ring.prev))
    yield
    right.wait_recv()
    on_right = links.copy(slot(ring.prev, 0), slot(ring.prev, 0), ring.device(ring.next))
    left.wait_recv()
    on_left = links.copy(slot(ring.next, 1), slot(ring.next, 1), ring.device(ring.prev))
    yield
    on_right.wait_recv()
    on_left.wait_recv()


def add_into(target, terms, kind):
    lead, rows, columns = target.shape
    step = 16
    for size in (128, 64, 48, 32):
        if rows % size == 0 and size * columns <= 48 * 1024:
            step = size
            break
    count = rows // step

    def body(k, carry):
        i, r = lax.div(k, count), pl.multiple_of(lax.rem(k, count) * step, step)
        total = terms[0][i, pl.ds(r, step), :].astype(F32)
        for term in terms[1:]:
            total = total + term[i, pl.ds(r, step), :].astype(F32)
        target[i, pl.ds(r, step), :] = total.astype(kind)
        return carry

    lax.fori_loop(0, lead * count, body, 0)


def ring_scatter(links, ring, part, room, target, kind):
    low, high, sum_low, sum_high, from_prev, from_next = room
    nxt, prv = ring.device(ring.next), ring.device(ring.prev)
    far_low = links.copy(part(ring.far, 0), low, nxt)
    far_high = links.copy(part(ring.far, 1), high, prv)
    next_high = links.copy(part(ring.next, 1), from_prev(1), nxt)
    prev_low = links.copy(part(ring.prev, 0), from_next(0), prv)
    yield
    far_low.wait_recv()
    add_into(sum_low, [part(ring.next, 0), low], BF16)
    next_low = links.copy(sum_low, from_prev(0), nxt)
    far_high.wait_recv()
    add_into(sum_high, [part(ring.prev, 1), high], BF16)
    prev_high = links.copy(sum_high, from_next(1), prv)
    yield
    for copy in (next_high, prev_low, next_low, prev_high):
        copy.wait_recv()
    add_into(target, [part(ring.own, None), from_prev(None), from_next(None)], kind)


def lead_part(part):
    return pl.ds(0, 4) if part is None else pl.ds(2 * part, 2)


def row_part(rows, part):
    first = (rows // 2 + 15) // 16 * 16
    if part is None:
        return 0, rows
    return (0, first) if part == 0 else (first, rows - first)


def regions(rows, columns, by_rows):
    if by_rows:
        return [(0, rows // 2, 0, columns), (rows // 2, rows // 2, 0, columns)]
    return [(0, rows, 0, columns // 2), (0, rows, columns // 2, columns // 2)]


def plane_gather(links, place, buf, by_rows):
    rows, columns = buf.shape[2:]

    def half(region, x_first):
        r0, rn, c0, cn = region

        def one(k, part):
            off, size = row_part(rn, part)
            y, x = (place.y, k) if x_first else (k, place.x)
            return buf.at[y, x, pl.ds(r0 + off, size), pl.ds(c0, cn)]

        def line(k, part):
            y, x = (k, lead_part(part)) if x_first else (lead_part(part), k)
            return buf.at[y, x, pl.ds(r0, rn), pl.ds(c0, cn)]

        yield from ring_gather(links, place.ring("x" if x_first else "y"), one)
        yield from ring_gather(links, place.ring("y" if x_first else "x"), line)

    a, b = regions(rows, columns, by_rows)
    return half(a, True), half(b, False)


def plane_scatter_room(rows, columns, by_rows):
    rooms = []
    for _, rn, _, cn in regions(rows, columns, by_rows):
        rooms += [pltpu.VMEM((2, rn, cn), BF16)] * 4 + [pltpu.VMEM((4, rn, cn), BF16)] * 3
        low, high = row_part(rn, 0)[1], row_part(rn, 1)[1]
        rooms += [pltpu.VMEM((1, low, cn), BF16), pltpu.VMEM((1, high, cn), BF16)] * 2
        rooms += [pltpu.VMEM((1, rn, cn), BF16)] * 2
    return rooms


def plane_scatter(links, place, buf, rooms, target, by_rows):
    rows, columns = buf.shape[2:]

    def half(region, room, x_first):
        r0, rn, c0, cn = region
        low, high, sum_low, sum_high, prev, nxt, lined = room[:7]
        low1, high1, sum_low1, sum_high1, prev1, nxt1 = room[7:]

        def line(k, part):
            y, x = (lead_part(part), k) if x_first else (k, lead_part(part))
            return buf.at[y, x, pl.ds(r0, rn), pl.ds(c0, cn)]

        def one(k, part):
            off, size = row_part(rn, part)
            return lined.at[pl.ds(k, 1), pl.ds(off, size), :]

        def lined_part(ref):
            return lambda part: ref.at[lead_part(part)]

        def one_part(ref):
            def view(part):
                off, size = row_part(rn, part)
                return ref.at[:, pl.ds(off, size), :]

            return view

        room_a = (low, high, sum_low, sum_high, lined_part(prev), lined_part(nxt))
        room_b = (low1, high1, sum_low1, sum_high1, one_part(prev1), one_part(nxt1))
        yield from ring_scatter(links, place.ring("x" if x_first else "y"), line, room_a, lined, BF16)
        out = target.at[:, pl.ds(r0, rn), pl.ds(c0, cn)]
        yield from ring_scatter(links, place.ring("y" if x_first else "x"), one, room_b, out, F32)

    a, b = regions(rows, columns, by_rows)
    return half(a, rooms[:13], False), half(b, rooms[13:], True)


def line_scatter_room(rows, columns):
    low, high = row_part(rows, 0)[1], row_part(rows, 1)[1]
    return [pltpu.VMEM((1, low, columns), BF16), pltpu.VMEM((1, high, columns), BF16)] * 2 + [
        pltpu.VMEM((1, rows, columns), BF16)
    ] * 2


def line_scatter(links, place, buf, room, target):
    rows = buf.shape[1]

    def part(k, half):
        off, size = row_part(rows, half)
        return buf.at[pl.ds(k, 1), pl.ds(off, size), :]

    def view(ref):
        def cut(half):
            off, size = row_part(rows, half)
            return ref.at[:, pl.ds(off, size), :]

        return cut

    low, high, sum_low, sum_high, prev, nxt = room
    yield from ring_scatter(
        links, place.ring("z"), part, (low, high, sum_low, sum_high, view(prev), view(nxt)), target, F32
    )


def line_gather(links, place, buf):
    rows = buf.shape[1]

    def slot(k, half):
        off, size = row_part(rows, half)
        return buf.at[k, pl.ds(off, size)]

    yield from ring_gather(links, place.ring("z"), slot)


def line_swap(links, place, source, target):
    ring = place.ring("z")
    copies = []
    for other in (ring.next, ring.prev, ring.far):
        copies.append(links.copy(source.at[other], target.at[ring.own], ring.device(other)))
    target[ring.own] = source[ring.own]
    yield
    for copy in copies:
        copy.wait_recv()


def small_gather(links, ring, slot):
    right = links.copy(slot(ring.own), slot(ring.own), ring.device(ring.next))
    left = links.copy(slot(ring.own), slot(ring.own), ring.device(ring.prev))
    yield
    right.wait_recv()
    left.wait_recv()
    on = links.copy(slot(ring.prev), slot(ring.prev), ring.device(ring.next))
    yield
    on.wait_recv()


def advance(*steps):
    for step in steps:
        next(step, None)


def finish(*steps):
    together(steps)


def dot(left, right):
    return jnp.dot(left, right, preferred_element_type=F32)


def dot_right_t(left, right):
    return lax.dot_general(left, right, (((1,), (1,)), ((), ())), preferred_element_type=F32)


def pack_rows():
    i = lax.broadcasted_iota(jnp.int32, (48, 64), 0)
    k = lax.broadcasted_iota(jnp.int32, (48, 64), 1)
    return (k == lax.div(i, 12) * 16 + lax.rem(i, 12)).astype(BF16)


def spread_rows():
    k = lax.broadcasted_iota(jnp.int32, (64, 48), 0)
    i = lax.broadcasted_iota(jnp.int32, (64, 48), 1)
    return (k == lax.div(i, 12) * 16 + lax.rem(i, 12)).astype(BF16)


def merged(ref):
    rows, columns = ref.shape[0] * ref.shape[1] * ref.shape[2], ref.shape[3]
    return ref[...].reshape(rows, columns)


def mean_square(values):
    return jnp.mean(values * values, axis=-1, keepdims=True)


def norm_back(grad, normed, scale):
    return scale * (grad - normed * jnp.mean(grad * normed, axis=-1, keepdims=True))


def slab_turns(line_ref, turn_ref, s):
    rows = line_ref[s]
    cos_base, sin_base = rows[0:1], rows[1:2]
    cos_off, sin_off = turn_ref[0], turn_ref[1]
    lane = lax.broadcasted_iota(jnp.int32, (SLAB, SLAB), 1)
    sign = jnp.where(lane < 32, -1.0, jnp.where(lane < 64, 1.0, 0.0))
    return cos_base * cos_off - sin_base * sin_off, (sin_base * cos_off + cos_base * sin_off) * sign


def turned(field, cosine, sine):
    lane = lax.broadcasted_iota(jnp.int32, (SLAB, SLAB), 1)
    return field * cosine + jnp.where(lane < 32, pltpu.roll(field, 96, 1), pltpu.roll(field, 32, 1)) * sine


def front_kernel(
    tok_ref, w_ref, gain_ref, perm_ref, turn_ref, desc_ref,
    kv_ref, q_ref, wqkv_ref, wo_ref, one_ref, meta_ref, line_ref,
    for_line, for_line_o, rows, rows_o, descs, send, recv,
):
    place = Place()
    enter(place, ("x", "y", "z"))
    links = Links(send, recv)
    own = place.y * 4 + place.x

    line_ref[place.z] = desc_ref[...]
    lined = small_gather(links, place.ring("z"), lambda k: line_ref.at[k])

    w = w_ref[...].astype(F32)
    gain = gain_ref[:, 0:1]
    none = jnp.zeros((16, HD), F32)
    for z in range(4):
        pieces = []
        for j in range(3):
            c = 192 * z + 64 * j
            pieces += [w[:, c : c + 64] * gain, none, w[:, 768 + c : 832 + c] * gain, w[:, 1536 + c : 1600 + c] * gain]
        for_line[z] = jnp.concatenate(pieces, 1).astype(BF16)
        rows_o[z] = jnp.zeros((16, 768), BF16)
    for_line_o[...] = w_ref[:, pl.ds(2304, 768)]
    swap = line_swap(links, place, for_line, rows)
    advance(swap, lined)

    x = dot(tok_ref[...], perm_ref[...])
    one_ref[place.z] = (x * lax.rsqrt(mean_square(x) + EPS)).astype(BF16)
    ones = line_gather(links, place, one_ref)
    advance(ones)
    rows_o[place.z] = for_line_o[...]
    o_line = small_gather(links, place.ring("z"), lambda k: rows_o.at[k])
    finish(swap)
    wqkv_ref[place.y, place.x] = dot(pack_rows(), rows[...].reshape(64, 768)).astype(BF16)
    qkv_a, qkv_b = plane_gather(links, place, wqkv_ref, False)
    advance(qkv_a, qkv_b, lined, ones, o_line)
    advance(qkv_a, qkv_b, lined)
    finish(lined)
    total = line_ref[0] + line_ref[1] + line_ref[2] + line_ref[3]
    descs[place.y, place.x] = total
    desc_x = small_gather(links, place.ring("x"), lambda k: descs.at[place.y, k])
    desc_y = small_gather(links, place.ring("y"), lambda k: descs.at[k])
    advance(desc_x)
    advance(qkv_a, qkv_b, o_line, ones)
    finish(o_line)
    wo_ref[place.y, place.x] = dot(pack_rows(), rows_o[...].reshape(64, 768)).astype(BF16)
    finish(qkv_a, qkv_b, ones)
    o_a, o_b = plane_gather(links, place, wo_ref, False)

    halves = plane_gather(links, place, kv_ref, True)
    for half in range(2):
        lines = one_ref[2 * half : 2 * half + 2].reshape(256, 768)
        field = dot(lines, merged(wqkv_ref))
        for k in range(2):
            s = 2 * half + k
            cosine, sine = slab_turns(line_ref, turn_ref, s)
            for j in range(3):
                query = turned(field[k * SLAB : (k + 1) * SLAB, 256 * j : 256 * j + 128], cosine, sine)
                q_ref[s, :, pl.ds(128 * j, 128)] = (query * 0.125).astype(BF16)
                pair = turned(field[k * SLAB : (k + 1) * SLAB, 256 * j + 128 : 256 * j + 256], cosine, sine)
                kv_ref[place.y, place.x, pl.ds(s * SLAB, SLAB), pl.ds(128 * j, 128)] = pair.astype(BF16)
        advance(halves[half])
    advance(o_a, o_b)
    finish(desc_x)
    advance(desc_y)
    advance(*halves)
    advance(o_a, o_b)
    advance(desc_y)
    advance(*halves)
    finish(desc_y)

    table = jnp.zeros((8, SLAB), F32)
    for y in range(4):
        for x in range(4):
            table = table + descs[y, x]
    seg, base = table[2:3], table[3:4]
    lane = lax.broadcasted_iota(jnp.int32, (1, SLAB), 1)
    lane_at = lane.astype(F32)
    n = lax.broadcasted_iota(jnp.int32, (24, 1), 0)
    for s in range(4):
        mine = lane == own * 4 + s
        seg_q = jnp.sum(jnp.where(mine, seg, 0.0), axis=1, keepdims=True)
        base_q = jnp.sum(jnp.where(mine, base, 0.0), axis=1, keepdims=True)
        prompt = jnp.where(seg_q >= CONTS + 1.0, CONTS + 1.0, 0.0)
        want = jnp.where(n < 16, prompt, seg_q)
        hit = (seg == want) & (base == n.astype(F32) * SLAB) & (lane < 64)
        places = jnp.sum(jnp.where(hit, lane_at, 0.0), axis=1, keepdims=True)
        follows = jnp.where(seg_q == prompt, 0.0, 1.0)
        blocks = jnp.where(seg_q == prompt, jnp.floor(base_q * (1.0 / 512.0)) + 1.0, 4.0)
        listed = jnp.where(n == 18, blocks, jnp.where(n == 19, follows, jnp.where(n == 20, base_q, places)))
        meta_ref[pl.ds(s * 24, 24), :] = jnp.broadcast_to(listed, (24, SLAB)).astype(jnp.int32)

    together([*halves, o_a, o_b])
    links.finish()


def front(collective_id, tokens, w, gain, perm, turn, desc):
    return pl.pallas_call(
        front_kernel,
        out_shape=(
            jax.ShapeDtypeStruct((4, 4, 512, 384), BF16),
            jax.ShapeDtypeStruct((4, SLAB, 384), BF16),
            jax.ShapeDtypeStruct((4, 4, 48, 768), BF16),
            jax.ShapeDtypeStruct((4, 4, 48, 768), BF16),
            jax.ShapeDtypeStruct((4, SLAB, 768), BF16),
            jax.ShapeDtypeStruct((96, SLAB), jnp.int32),
            jax.ShapeDtypeStruct((4, 8, SLAB), F32),
        ),
        in_specs=[VMEM] * 6,
        out_specs=(VMEM,) * 7,
        scratch_shapes=[
            pltpu.VMEM((4, 16, 768), BF16),
            pltpu.VMEM((16, 768), BF16),
            pltpu.VMEM((4, 16, 768), BF16),
            pltpu.VMEM((4, 16, 768), BF16),
            pltpu.VMEM((4, 4, 8, SLAB), F32),
            pltpu.SemaphoreType.DMA((72,)),
            pltpu.SemaphoreType.DMA((72,)),
        ],
        compiler_params=pltpu.CompilerParams(
            collective_id=collective_id, has_side_effects=True, vmem_limit_bytes=60 * MIB
        ),
        name="front",
    )(tokens, w, gain, perm, turn, desc)


def middle_kernel(
    att_ref, tok_ref, cot_ref, wo_ref, w_ref, gain_ref, down_ref, perm_ref, perm_att_ref,
    out_ref, gm_ref, grads_ref, ff_ref, og_ref,
    atts, cots, for_line, rows, wff, two, mid_s, att_s, act, pre, two_t, act_t, part_out, part_back, sum_out, sum_back,
    ff_part, og_part, to_heads, *rest,
):
    send, recv = rest[-2:]
    rooms = list(rest[:-2])
    back_room, rooms = rooms[:6], rooms[6:]
    out_room, rooms = rooms[:6], rooms[6:]
    ff_room, og_room = rooms[:26], rooms[26:]
    place = Place()
    enter(place, ("x", "y", "z"))
    links = Links(send, recv)

    att_swap = line_swap(links, place, att_ref, atts)
    advance(att_swap)
    cots[place.z] = cot_ref[...]
    cot_gather = line_gather(links, place, cots)
    advance(cot_gather)

    gain = gain_ref[:, 0:1]
    for z in range(4):
        for k in range(2):
            pieces = []
            for p in range(16):
                c = 3072 * k + ((z % 2) * 32 + p * 2 + z // 2) * 48
                pieces.append(w_ref[:, c : c + 48].astype(F32) * gain)
            for_line[z, :, pl.ds(768 * k, 768)] = jnp.concatenate(pieces, 1).astype(BF16)
    w_swap = line_swap(links, place, for_line, rows)
    advance(w_swap)
    finish(att_swap)

    att = dot(atts[0], perm_att_ref[pl.ds(0, 256), :])
    for z in range(1, 4):
        att = att + dot(atts[z], perm_att_ref[pl.ds(256 * z, 256), :])
    att_s[...] = att.astype(BF16)
    mid_s[...] = tok_ref[...].astype(F32) + dot(att_s[...], merged(wo_ref))
    middle = mid_s[...]
    scale_two = lax.rsqrt(mean_square(middle) + EPS)
    two[place.z] = dot((middle * scale_two).astype(BF16), perm_ref[...]).astype(BF16)
    two_gather = line_gather(links, place, two)
    advance(cot_gather, two_gather)
    finish(w_swap)
    for c in range(0, 1536, 768):
        wff[place.y, place.x, :, pl.ds(c, 768)] = dot(
            pack_rows(), rows[:, :, pl.ds(c, 768)].reshape(64, 768)
        ).astype(BF16)
    wff[place.y, place.x, :, pl.ds(1536, 768)] = down_ref[...]
    w_a, w_b = plane_gather(links, place, wff, False)
    advance(w_a, w_b, cot_gather, two_gather)
    together([w_a, w_b, cot_gather, two_gather])

    def block(r, carry):
        at = pl.ds(pl.multiple_of(r * 256, 256), 256)
        two_b = two[pl.ds(r * 2, 2)].reshape(256, 768)
        cot_b = cots[pl.ds(r * 2, 2)].reshape(256, 768)
        gate_w = wff[:, :, :, pl.ds(0, 768)].reshape(768, 768)
        up_w = wff[:, :, :, pl.ds(768, 768)].reshape(768, 768)
        down_w = wff[:, :, :, pl.ds(1536, 768)].reshape(768, 768)
        gate = dot(two_b, gate_w)
        up = dot(two_b, up_w)
        sig = 1.0 / (1.0 + jnp.exp(-gate))
        silu = gate * sig
        act_b = (silu * up).astype(BF16)
        act[at, :] = act_b
        grad_act = dot_right_t(cot_b, down_w)
        grad_gate = (grad_act * up * (sig * (1.0 + gate * (1.0 - sig)))).astype(BF16)
        grad_up = (grad_act * silu).astype(BF16)
        pre[at, pl.ds(0, 768)] = grad_gate
        pre[at, pl.ds(768, 768)] = grad_up
        back = dot_right_t(grad_gate, gate_w) + dot_right_t(grad_up, up_w)
        part_back[pl.ds(r * 2, 2)] = back.astype(BF16).reshape(2, SLAB, 768)
        part_out[pl.ds(r * 2, 2)] = dot(act_b, down_w).astype(BF16).reshape(2, SLAB, 768)
        return carry

    lax.fori_loop(0, 2, block, 0)
    back_sum = line_scatter(links, place, part_back, back_room, sum_back)
    out_sum = line_scatter(links, place, part_out, out_room, sum_out)
    advance(back_sum)
    two_t[...] = two[...].reshape(512, 768).T

    def first_grads(c, carry):
        at = pl.ds(pl.multiple_of(c * 256, 256), 256)
        ff_part[:, :, :, at] = dot(two_t[...], pre[:, at]).astype(BF16).reshape(4, 4, 48, 256)
        return carry

    def last_grads(c, carry):
        at = pl.ds(pl.multiple_of(c * 256, 256), 256)
        to = pl.ds(pl.multiple_of(1536 + c * 256, 256), 256)
        cot_all = cots[:, :, at].reshape(512, 256)
        ff_part[:, :, :, to] = dot(act_t[...], cot_all).astype(BF16).reshape(4, 4, 48, 256)
        return carry

    lax.fori_loop(0, 3, first_grads, 0)
    advance(back_sum)
    lax.fori_loop(3, 6, first_grads, 0)
    act_t[...] = act[...].T
    lax.fori_loop(0, 3, last_grads, 0)
    ff_a, ff_b = plane_scatter(links, place, ff_part, ff_room, ff_ref, False)
    advance(ff_a, ff_b)
    finish(back_sum)
    advance(out_sum)

    grad = dot_right_t(sum_back[0].astype(BF16), perm_ref[...])
    middle = mid_s[...]
    scale_two = lax.rsqrt(mean_square(middle) + EPS)
    gm_ref[...] = cot_ref[...].astype(F32) + norm_back(grad, middle * scale_two, scale_two)
    low = gm_ref[...].astype(BF16)
    grad_att = dot_right_t(low, merged(wo_ref)).astype(BF16)
    for z in range(4):
        to_heads[z] = dot_right_t(grad_att, perm_att_ref[pl.ds(256 * z, 256), :]).astype(BF16)
    heads_swap = line_swap(links, place, to_heads, grads_ref)
    advance(heads_swap)
    advance(ff_a, ff_b, out_sum)
    og_part[...] = dot(att_s[...].T, low).astype(BF16).reshape(4, 4, 48, 768)
    og_a, og_b = plane_scatter(links, place, og_part, og_room, og_ref, False)
    advance(og_a, og_b)
    together([ff_a, ff_b, out_sum, heads_swap, og_a, og_b])
    out_ref[...] = (mid_s[...] + sum_out[0]).astype(BF16)
    links.finish()


def middle(collective_id, att, tokens, cotangent, w_o, w, gain, down, perm, perm_att):
    line = pltpu.VMEM((4, SLAB, 768), BF16)
    return pl.pallas_call(
        middle_kernel,
        out_shape=(
            jax.ShapeDtypeStruct((SLAB, 768), BF16),
            jax.ShapeDtypeStruct((SLAB, 768), F32),
            jax.ShapeDtypeStruct((4, SLAB, 256), BF16),
            jax.ShapeDtypeStruct((1, 48, 2304), F32),
            jax.ShapeDtypeStruct((1, 48, 768), F32),
        ),
        in_specs=[VMEM] * 9,
        out_specs=(VMEM,) * 5,
        scratch_shapes=[
            pltpu.VMEM((4, SLAB, 256), BF16),
            line,
            pltpu.VMEM((4, 16, 1536), BF16),
            pltpu.VMEM((4, 16, 1536), BF16),
            pltpu.VMEM((4, 4, 48, 2304), BF16),
            line,
            pltpu.VMEM((SLAB, 768), F32),
            pltpu.VMEM((SLAB, 768), BF16),
            pltpu.VMEM((512, 768), BF16),
            pltpu.VMEM((512, 1536), BF16),
            pltpu.VMEM((768, 512), BF16),
            pltpu.VMEM((768, 512), BF16),
            line,
            line,
            pltpu.VMEM((1, SLAB, 768), F32),
            pltpu.VMEM((1, SLAB, 768), F32),
            pltpu.VMEM((4, 4, 48, 2304), BF16),
            pltpu.VMEM((4, 4, 48, 768), BF16),
            pltpu.VMEM((4, SLAB, 256), BF16),
        ]
        + line_scatter_room(SLAB, 768)
        + line_scatter_room(SLAB, 768)
        + plane_scatter_room(48, 2304, False)
        + plane_scatter_room(48, 768, False)
        + [pltpu.SemaphoreType.DMA((96,))] * 2,
        compiler_params=pltpu.CompilerParams(
            collective_id=collective_id, has_side_effects=True, vmem_limit_bytes=60 * MIB
        ),
        name="middle",
    )(att, tokens, cotangent, w_o, w, gain, down, perm, perm_att)


def back_kernel(
    dq_ref, dkv_ref, wqkv_ref, one_ref, line_ref, turn_ref, gm_ref, tok_ref, perm_ref, ff_ref, og_ref,
    in_ref, got_ff_ref, got_ref,
    own_kv, d_s, one_t, part, sum_s, qkv_part, qkv_sum, ff_rows, qkv_rows, *rest,
):
    send, recv = rest[-2:]
    rooms = list(rest[:-2])
    kv_room, rooms = rooms[:26], rooms[26:]
    qkv_room, line_room = rooms[:26], rooms[26:]
    place = Place()
    enter(place, ("x", "y", "z"))
    links = Links(send, recv)

    kv_a, kv_b = plane_scatter(links, place, dkv_ref, kv_room, own_kv, True)
    advance(kv_a, kv_b)
    spread = spread_rows()
    for c in range(0, 1536, 768):
        ff_rows[:, :, pl.ds(c, 768)] = (
            dot(spread, ff_ref[0, :, pl.ds(c, 768)].astype(BF16)).astype(BF16).reshape(4, 16, 768)
        )
    ff_rows[:, :, pl.ds(1536, 768)] = dot(spread, og_ref[0].astype(BF16)).astype(BF16).reshape(4, 16, 768)
    ff_swap = line_swap(links, place, ff_rows, got_ff_ref)
    advance(ff_swap)
    lane = lax.broadcasted_iota(jnp.int32, (SLAB, SLAB), 1)
    advance(kv_a, kv_b)
    for s in range(4):
        cosine, sine = slab_turns(line_ref, turn_ref, s)
        for j in range(3):
            grad = jnp.where(lane < 64, dq_ref[s, :, pl.ds(128 * j, 128)] * 0.125, 0.0)
            d_s[pl.ds(s * SLAB, SLAB), pl.ds(256 * j, 128)] = turned(grad, cosine, -sine).astype(BF16)
    one_t[...] = one_ref[...].reshape(512, 768).T
    finish(kv_a, kv_b)
    for s in range(4):
        cosine, sine = slab_turns(line_ref, turn_ref, s)
        for j in range(3):
            grad = own_kv[0, pl.ds(s * SLAB, SLAB), pl.ds(128 * j, 128)]
            d_s[pl.ds(s * SLAB, SLAB), pl.ds(256 * j + 128, 128)] = turned(grad, cosine, -sine).astype(BF16)

    def block(r, carry):
        at = pl.ds(pl.multiple_of(r * 256, 256), 256)
        part[pl.ds(r * 2, 2)] = dot_right_t(d_s[at, :], merged(wqkv_ref)).astype(BF16).reshape(2, SLAB, 768)
        return carry

    lax.fori_loop(0, 2, block, 0)
    in_sum = line_scatter(links, place, part, line_room, sum_s)
    advance(in_sum)

    def grads(c, carry):
        at = pl.ds(pl.multiple_of(c * 256, 256), 256)
        qkv_part[:, :, :, at] = dot(one_t[...], d_s[:, at]).astype(BF16).reshape(4, 4, 48, 256)
        return carry

    lax.fori_loop(0, 3, grads, 0)
    qkv_a, qkv_b = plane_scatter(links, place, qkv_part, qkv_room, qkv_sum, False)
    advance(qkv_a, qkv_b, in_sum)
    advance(qkv_a, qkv_b)
    finish(in_sum)
    advance(qkv_a, qkv_b)
    grad = dot_right_t(sum_s[0].astype(BF16), perm_ref[...])
    x = tok_ref[...].astype(F32)
    scale = lax.rsqrt(mean_square(x) + EPS)
    in_ref[...] = gm_ref[...] + norm_back(grad, x * scale, scale)
    together([qkv_a, qkv_b])
    qkv_rows[...] = dot(spread, qkv_sum[0].astype(BF16)).astype(BF16).reshape(4, 16, 768)
    finish(ff_swap, line_swap(links, place, qkv_rows, got_ref))
    links.finish()


def back(collective_id, dq, dkv, w_qkv, one, line, turn, grad_middle, tokens, perm, ff_sum, og_sum):
    return pl.pallas_call(
        back_kernel,
        out_shape=(
            jax.ShapeDtypeStruct((SLAB, 768), F32),
            jax.ShapeDtypeStruct((4, 16, 2304), BF16),
            jax.ShapeDtypeStruct((4, 16, 768), BF16),
        ),
        in_specs=[VMEM] * 11,
        out_specs=(VMEM,) * 3,
        scratch_shapes=[
            pltpu.VMEM((1, 512, 384), F32),
            pltpu.VMEM((512, 768), BF16),
            pltpu.VMEM((768, 512), BF16),
            pltpu.VMEM((4, SLAB, 768), BF16),
            pltpu.VMEM((1, SLAB, 768), F32),
            pltpu.VMEM((4, 4, 48, 768), BF16),
            pltpu.VMEM((1, 48, 768), F32),
            pltpu.VMEM((4, 16, 2304), BF16),
            pltpu.VMEM((4, 16, 768), BF16),
        ]
        + plane_scatter_room(512, 384, True)
        + plane_scatter_room(48, 768, False)
        + line_scatter_room(SLAB, 768)
        + [pltpu.SemaphoreType.DMA((64,))] * 2,
        compiler_params=pltpu.CompilerParams(
            collective_id=collective_id, has_side_effects=True, vmem_limit_bytes=60 * MIB
        ),
        name="back",
    )(dq, dkv, w_qkv, one, line, turn, grad_middle, tokens, perm, ff_sum, og_sum)


def attend_kernel(meta, q_ref, kv_ref, out_ref, lse_ref):
    row = lax.broadcasted_iota(jnp.int32, (SLAB, 1), 0)
    lane = lax.broadcasted_iota(jnp.int32, (SLAB, SLAB), 1)

    def slab(s, carry):
        pos_q = meta[s * 24 + 20, 0] + row
        queries = [q_ref[s, :, pl.ds(j * 128, 128)] for j in range(3)]

        def fold(state, places, first):
            width = len(places) * SLAB
            pos_k = first + lax.broadcasted_iota(jnp.int32, (1, width), 1)
            allowed = pos_k <= pos_q
            out = []
            for j in range(3):
                top, total, acc = state[j]
                keys = jnp.concatenate([kv_ref[at, :, pl.ds(j * 128, 128)] for at in places], 0)
                scores = lax.dot_general(queries[j], keys, (((1,), (1,)), ((), ())), preferred_element_type=F32)
                scores = jnp.where(allowed, scores, LOW)
                new_top = jnp.maximum(top, jnp.max(scores, axis=1, keepdims=True))
                weights = jnp.exp(scores - new_top)
                decay = jnp.exp(top - new_top)
                total = total * decay + jnp.sum(weights, axis=1, keepdims=True)
                acc = acc * decay + jnp.dot(weights.astype(BF16), keys, preferred_element_type=F32)
                out.append((new_top, total, acc))
            return tuple(out)

        start = tuple(
            (jnp.full((SLAB, 1), LOW, F32), jnp.zeros((SLAB, 1), F32), jnp.zeros((SLAB, SLAB), F32)) for _ in range(3)
        )

        def prompt(c, state):
            return fold(state, [meta[s * 24 + c * 4 + a, 0] for a in range(4)], c * 512)

        def own(c, state):
            return fold(state, [meta[s * 24 + 16, 0], meta[s * 24 + 17, 0]], 2048)

        state = lax.fori_loop(0, meta[s * 24 + 18, 0], prompt, start)
        state = lax.fori_loop(0, meta[s * 24 + 19, 0], own, state)
        heads = [acc / total for _, total, acc in state]
        out_ref[s, :, 0:128] = jnp.where(lane < 64, pltpu.roll(heads[0], 64, 1), heads[1]).astype(BF16)
        out_ref[s, :, 128:256] = jnp.where(lane < 64, pltpu.roll(heads[2], 64, 1), 0.0).astype(BF16)
        logs = [top + jnp.log(total) for top, total, _ in state]
        lse_ref[s] = jnp.where(lane == 0, logs[0], jnp.where(lane == 1, logs[1], logs[2]))
        return carry

    lax.fori_loop(0, 4, slab, 0)


def attend(meta, q, kv):
    return pl.pallas_call(
        attend_kernel,
        out_shape=(jax.ShapeDtypeStruct((4, SLAB, 256), BF16), jax.ShapeDtypeStruct((4, SLAB, SLAB), F32)),
        in_specs=[SMEM, VMEM, VMEM],
        out_specs=(VMEM, VMEM),
        compiler_params=pltpu.CompilerParams(vmem_limit_bytes=60 * MIB),
        name="attend",
    )(meta, q, kv)


def attend_back_kernel(meta, q_ref, kv_ref, grad_ref, out_ref, lse_ref, dq_ref, dkv_ref, acc_ref):
    lane = lax.broadcasted_iota(jnp.int32, (SLAB, SLAB), 1)
    which = lax.broadcasted_iota(jnp.int32, (8, SLAB), 0)
    unit = (lax.broadcasted_iota(jnp.int32, (8, SLAB), 1) == which).astype(F32)
    at_lane = lax.broadcasted_iota(jnp.int32, (8, 256), 1)
    pick = (lax.div(at_lane, HD) == lax.broadcasted_iota(jnp.int32, (8, 256), 0)).astype(F32)

    def clear(k, carry):
        acc_ref[k] = jnp.zeros((SLAB, 384), F32)
        return carry

    lax.fori_loop(0, 64, clear, 0)

    def slab(s, carry):
        pos_q = meta[s * 24 + 20, 0] + lax.broadcasted_iota(jnp.int32, (1, SLAB), 1)
        first = grad_ref[s, :, 0:128].astype(F32)
        last = grad_ref[s, :, 128:256].astype(F32)
        inner = grad_ref[s].astype(F32) * out_ref[s].astype(F32)
        deltas = lax.dot_general(pick, inner, LANES, precision=HIGHEST, preferred_element_type=F32)
        logs = lax.dot_general(unit, lse_ref[s], LANES, precision=HIGHEST, preferred_element_type=F32)
        logs = [jnp.sum(jnp.where(which == k, logs, 0.0), axis=0, keepdims=True) for k in range(3)]
        deltas = [jnp.sum(jnp.where(which == k, deltas, 0.0), axis=0, keepdims=True) for k in range(3)]
        right = [pltpu.roll(first, 64, 1), first, pltpu.roll(last, 64, 1)]
        pairs = []
        for j in range(3):
            grads = jnp.where(lane < 64, 0.0, right[j]).astype(BF16)
            pairs.append(jnp.concatenate([q_ref[s, :, pl.ds(j * 128, 128)], grads], 0))
        for j in range(3):
            dq_ref[s, :, pl.ds(j * 128, 128)] = jnp.zeros((SLAB, SLAB), F32)

        def fold(places, first_key):
            width = len(places) * SLAB
            pos_k = first_key + lax.broadcasted_iota(jnp.int32, (width, 1), 0)
            allowed = pos_k <= pos_q
            for j in range(3):
                keys = jnp.concatenate([kv_ref[at, :, pl.ds(j * 128, 128)] for at in places], 0)
                both = lax.dot_general(keys, pairs[j], (((1,), (1,)), ((), ())), preferred_element_type=F32)
                weights = jnp.where(allowed, jnp.exp(both[:, :128] - logs[j]), 0.0)
                slopes = (weights * (both[:, 128:] - deltas[j])).astype(BF16)
                terms = jnp.dot(
                    jnp.concatenate([slopes, weights.astype(BF16)], 1), pairs[j], preferred_element_type=F32
                )
                for n, at in enumerate(places):
                    acc_ref[at, :, pl.ds(j * 128, 128)] += terms[n * 128 : (n + 1) * 128]
                dq_ref[s, :, pl.ds(j * 128, 128)] += lax.dot_general(
                    slopes, keys, (((0,), (0,)), ((), ())), preferred_element_type=F32
                )

        def prompt(c, state):
            fold([meta[s * 24 + c * 4 + a, 0] for a in range(4)], c * 512)
            return state

        def own(c, state):
            fold([meta[s * 24 + 16, 0], meta[s * 24 + 17, 0]], 2048)
            return state

        lax.fori_loop(0, meta[s * 24 + 18, 0], prompt, 0)
        lax.fori_loop(0, meta[s * 24 + 19, 0], own, 0)
        return carry

    lax.fori_loop(0, 4, slab, 0)

    def store(k, carry):
        dkv_ref[k] = acc_ref[k].astype(BF16)
        return carry

    lax.fori_loop(0, 64, store, 0)


def attend_back(meta, q, kv, grads, out, lse):
    return pl.pallas_call(
        attend_back_kernel,
        out_shape=(jax.ShapeDtypeStruct((4, SLAB, 384), F32), jax.ShapeDtypeStruct((64, SLAB, 384), BF16)),
        in_specs=[SMEM, VMEM, VMEM, VMEM, VMEM, VMEM],
        out_specs=(VMEM, VMEM),
        scratch_shapes=[pltpu.VMEM((64, SLAB, 384), F32)],
        compiler_params=pltpu.CompilerParams(vmem_limit_bytes=60 * MIB),
        name="attend_back",
    )(meta, q, kv, grads, out, lse)


def split_columns(w):
    rows = w.shape[0]
    return w.reshape(rows, 2, 16, 2, 48).transpose(3, 1, 0, 2, 4).reshape(4, rows, 768)


def join_columns(w):
    rows = w.shape[1]
    return w.reshape(2, 2, rows, 16, 48).transpose(2, 1, 3, 0, 4).reshape(rows, 3072)


def per_device(
    tokens, gain_one, w_query, w_key, w_value, w_out, gain_two, w_gate, w_up, w_down, cotangent, segment_ids, positions
):
    blk, head = lax.axis_index("blk"), lax.axis_index("head")
    z, own = head * 2 + blk // 16, blk % 16
    perm = jnp.asarray(TO_PERM, BF16)
    perm_att = jnp.asarray(np.pad(TO_PERM.reshape(4, 192, 768), ((0, 0), (0, 64), (0, 0))).reshape(1024, 768), BF16)
    turn = jnp.asarray(OFFSET_TURNS, F32)
    first_gain, second_gain = gain_one.astype(F32)[:, None], gain_two.astype(F32)[:, None]

    seg = segment_ids.reshape(2, SLAB)[head, 0].astype(F32)
    base = positions.reshape(2, SLAB)[head, 0].astype(F32)
    angles = base * jnp.asarray(FREQUENCY, F32)[None]
    row = lax.broadcasted_iota(jnp.int32, (8, SLAB), 0)
    lane = lax.broadcasted_iota(jnp.int32, (8, SLAB), 1)
    here = lane == own * 4 + z
    desc = jnp.where(
        row == 0,
        jnp.cos(angles),
        jnp.where(
            row == 1,
            jnp.sin(angles),
            jnp.where(here & (row == 2), seg, jnp.where(here & (row == 3), base, 0.0)),
        ),
    )
    w_attention = jnp.pad(jnp.concatenate([w_query, w_key, w_value, w_out], 1), ((0, 4), (0, 0)))
    w_ff = jnp.pad(jnp.concatenate([w_gate, w_up], 1), ((0, 4), (0, 0)))
    gain_a = jnp.broadcast_to(jnp.pad(first_gain, ((0, 4), (0, 0))), (16, SLAB))
    gain_b = jnp.broadcast_to(jnp.pad(second_gain, ((0, 4), (0, 0))), (16, SLAB))

    kv, q, w_qkv, w_o, line_one, meta, line = front(0, tokens, w_attention, gain_a, perm, turn, desc)
    kv = kv.reshape(64, SLAB, 384)
    heads_out, lse = attend(meta, q, kv)
    output, grad_middle, grad_heads, ff_sum, og_sum = middle(
        1, heads_out, tokens, cotangent, w_o, w_ff, gain_b, w_down, perm, perm_att
    )
    dq, dkv = attend_back(meta, q, kv, grad_heads, heads_out, lse)
    input_grad, got_ff, got_qkv = back(
        2, dq, dkv.reshape(4, 4, 512, 384), w_qkv, line_one, line, turn, grad_middle, tokens, perm, ff_sum, og_sum
    )

    got_out = got_ff[:, :12, 1536:].astype(F32)
    got_ff = got_ff[:, :12, :1536].astype(F32)
    got_qkv = got_qkv[:, :12].astype(F32)
    by_kind = got_qkv.reshape(4, 12, 3, 4, HD).transpose(3, 1, 0, 2, 4).reshape(4, 12, 768)
    gate_grad, up_grad = join_columns(got_ff[:, :, :768]), join_columns(got_ff[:, :, 768:])
    gain_one_grad = jnp.sum(by_kind[0] * w_query + by_kind[2] * w_key + by_kind[3] * w_value, axis=1)
    gain_two_grad = jnp.sum(gate_grad * w_gate + up_grad * w_up, axis=1)
    return (
        output,
        input_grad,
        gain_one_grad,
        by_kind[0] * first_gain,
        by_kind[2] * first_gain,
        by_kind[3] * first_gain,
        jnp.sum(got_out, axis=0),
        gain_two_grad,
        gate_grad * second_gain,
        up_grad * second_gain,
        ff_sum[0, :, 1536:],
    )


def solution(mesh):
    rows = P(("grp", "blk", "head"), None)
    flat = P(("grp", "blk", "head"))
    weight = P(("blk", "head"), None)
    gain = P(("blk", "head"))
    ids = P(("grp", "blk"))
    in_specs = (rows, gain, weight, weight, weight, weight, gain, weight, weight, weight, rows, ids, ids)
    out_specs = (rows, rows, flat, rows, rows, rows, rows, flat, rows, rows, rows)
    return jax.shard_map(per_device, mesh=mesh, in_specs=in_specs, out_specs=out_specs, check_vma=False)
```

time: 395 us -> 293 us (0.74)
  matrix products: 34.9 us -> 0 us
  local copies, waits for them, and re-layouts: 39.1 us -> 8.03 us
  Pallas kernels: 291 us -> 267 us
  other arithmetic: 27.1 us -> 14.3 us
    dot_general x17 -> x0, matrix products: 34.9 us -> none  [the longest x6 13.7 us: dot_right_t(): lax.dot_general(left, right, (((1,), (1,)), ((), ())), preferred_element_...]
    pallas_call x9 -> x3, Pallas kernels: 254 us -> 230 us  [the longest x1 86.5 us: middle(): pl.pallas_call(middle_kernel, out_shape=(jax.ShapeDtypeStruct((SLAB, 768)...]
    concatenate x11 -> x0, local copies, waits for them, and re-layouts: 8.92 us -> none  [the longest x2 4.69 us: per_device(): jnp.concatenate([dq.reshape(512, 3, 1, 128) * 0.125, dkv_own.reshape(512,...]
    dot_general x4 -> x0, local copies, waits for them, and re-layouts: 5.4 us -> none  [the longest x2 3 us: dot(): return jnp.dot(left, right, preferred_element_type=F32)]
where the time goes in v2:
time: 293 us; the launch traced here: 291 us
  Pallas kernels  267 us (91%)
  other arithmetic  14.3 us (5%)
  local copies, waits for them, and re-layouts  8.03 us (3%)
    pallas_call x1, Pallas kernels, middle(): pl.pallas_call(middle_kernel, out_shape=(jax.ShapeDtypeStruct((SLAB, 768)...  86.5 us
    pallas_call x1, Pallas kernels, front(): pl.pallas_call(front_kernel, out_shape=(jax.ShapeDtypeStruct((4, 4, 512,...  78.4 us
    pallas_call x1, Pallas kernels, back(): pl.pallas_call(back_kernel, out_shape=(jax.ShapeDtypeStruct((SLAB, 768),...  64.9 us
    pallas_call x1, Pallas kernels, attend_back(): pl.pallas_call(attend_back_kernel, out_shape=(jax.ShapeDtypeStruct((4, SL...  21.1 us
    pallas_call x1, Pallas kernels, attend(): pl.pallas_call(attend_kernel, out_shape=(jax.ShapeDtypeStruct((4, SLAB, 2...  16.4 us

profile of v2, /device:TPU:0, one launch (start us, length us, event | category | flops | bytes accessed | tf_op | source)
XLA Modules:
  0.0 290.6 jit_solution(277581098622930510)
XLA Ops:
  0.7 1.2 fusion.13
  1.9 1.3 multiply_cosine_fusion
  3.2 0.7 fusion.12
  3.9 0.7 fusion.11
  4.6 2.0 select_select_fusion.desc_ref
  6.6 0.7 broadcast_in_dim.56.gain_ref
  7.2 0.7 broadcast_in_dim.48.gain_ref
  7.9 1.5 fusion.9.w_ref
  9.3 1.6 fusion.2.w_ref
  11.0 78.4 %front.1 = (bf16[4,4,512,384]{3,2,1,0:T(8,128)(2,1)}, bf16[4,128,384]{2,1,0:T(8,128)(2,1)}, bf16[4,4,48,768]{3,2,1,0:T(8,128)(2,1)}, bf16[4,4,48,768]{3,2,1,0:T(...) custom-call(bf16[128,768]{1,0:T(8,128)(2,1)} %tok_ref.5, ...), custom_call_target="tpu_custom_call" | custom-call | tf_op jit(solution)/shard_map/front/pallas_call | solution.py:475
  89.5 16.4 %attend.1 = (bf16[4,128,256]{2,1,0:T(8,128)(2,1)}, f32[4,128,128]{2,1,0:T(8,128)}) custom-call(s32[96,128]{1,0:T(8,128)} %get-tuple-element.30.meta, bf16[4,128,384]{2,1,0:T(8,128)(2,1)} %get-tuple-element.31.q_ref, bf16[64,128,384]{2,1,0:T(8,128)(2,1)} %bitcast.25), custom_call_target="tpu_custom_call" | custom-call | tf_op jit(solution)/shard_map/attend/pallas_call | solution.py:822
  105.9 86.5 %middle.1 = (bf16[128,768]{1,0:T(8,128)(2,1)}, f32[128,768]{1,0:T(8,128)}, bf16[4,128,256]{2,1,0:T(8,128)(2,1)}, f32[1,48,2304]{2,1,0:T(8,128)}, f32[1,48,768]{2,1,0:T(8,128)}) custom-call(bf16[4,128,256]{2,1,0:T(8,128)(2,1)} %get-tuple-element.33.att_ref.out_ref, bf16[128,768]{1,0:T(8,128)(2,1)} %tok_ref.5, bf16[128,768]{1,0:T(8,128)(2,1)} %cot_ref.1, ...), custom_call_target="tpu_custom_call" | custom-call | tf_op jit(solution)/shard_map/middle/pallas_call | solution.py:629
  192.4 21.1 %attend_back.1 = (f32[4,128,384]{2,1,0:T(8,128)}, bf16[64,128,384]{2,1,0:T(8,128)(2,1)}) custom-call(s32[96,128]{1,0:T(8,128)} %get-tuple-element.30.meta, bf16[4,128,384]{2,1,0:T(8,128)(2,1)} %get-tuple-element.31.q_ref, bf16[64,128,384]{2,1,0:T(8,128)(2,1)} %bitcast.26, bf16[4,128,256]{2,1,0:T(8,128)(2,1)} %get-tuple-element.36.grad_ref, ...), custom_call_target="tpu_custom_call" | custom-call | tf_op jit(solution)/shard_map/attend_back/pallas_call | solution.py:902
  213.5 64.9 %back.1 = (f32[128,768]{1,0:T(8,128)}, bf16[4,16,2304]{2,1,0:T(8,128)(2,1)}, bf16[4,16,768]{2,1,0:T(8,128)(2,1)}) custom-call(f32[4,128,384]{2,1,0:T(8,128)} %get-tuple-element.38.dq_ref, bf16[4,4,512,384]{3,2,1,0:T(8,128)(2,1)} %bitcast.27, bf16[4,4,48,768]{3,2,1,0:T(8,128)(2,1)} %get-tuple-element.40.wqkv_ref, ...), custom_call_target="tpu_custom_call" | custom-call | tf_op jit(solution)/shard_map/back/pallas_call | solution.py:742
  278.5 0.0 copy-start.7
  278.5 1.6 slice_bitcast_fusion
  280.1 1.5 convert_reduce_fusion
  281.6 1.0 slice_convert_fusion
  282.6 0.0 copy-start.4
  282.6 0.0 copy-start.5
  282.6 0.0 copy-start.6
  282.6 0.1 copy.37
  282.7 0.1 copy.39
  282.8 0.0 copy-done.7
  282.9 0.1 copy.36
  283.0 0.2 reshape.75
  283.2 0.7 slice_reduce_fusion.2
  283.8 0.1 squeeze.8
  284.0 0.1 squeeze.19
  284.1 0.1 squeeze.18
  284.2 0.0 copy-done.4
  284.2 0.0 copy-done.5
  284.2 0.0 copy-done.6
  284.2 1.4 broadcast_multiply_fusion.2
  285.6 0.2 reshape.73
  285.8 0.0 copy-start.1
  285.8 0.0 copy-start.2
  285.8 0.3 copy.40
  286.1 0.5 reshape.74
  286.6 0.0 copy-start.3
  286.6 0.0 copy-start
  286.6 0.2 reshape.71
  286.9 0.3 copy.38
  287.2 0.5 reshape.72
  287.7 0.0 copy-done.1
  287.7 0.0 copy-done.2
  287.7 1.5 broadcast_multiply_fusion
  289.2 0.0 copy-done.3
  289.2 0.7 copy.43
  289.8 0.0 copy-done
  289.9 0.7 copy.44
  (7 shorter events, 0.1 us)
Async XLA Ops:
  278.5 4.4 %copy-start.7 = (bf16[4,16,768]{2,1,0:T(8,128)(2,1)S(1)}, bf16[4,16,768]{2,1,0:T(8,128)(2,1)}, u32[]{:S(2)}) copy-start(bf16[4,16,768]{2,1,0:T(8,128)(2,1)} %get-tuple-element.47) | copy-start | bytes 294916
  282.6 1.6 copy-start.4
  282.6 1.6 copy-start.5
  282.6 1.6 copy-start.6
  285.8 1.9 copy-start.1
  285.8 1.9 copy-start.2
  286.6 2.5 copy-start.3
  286.6 3.2 %copy-start = (f32[128,768]{1,0:T(8,128)S(1)}, f32[128,768]{1,0:T(8,128)}, u32[]{:S(2)}) copy-start(f32[128,768]{1,0:T(8,128)} %get-tuple-element.85) | copy-start | bytes 1179652

commit v3 on v2

v3 whole, which is shorter than its diff:
```python
import math

import jax
import jax.numpy as jnp
import numpy as np
from jax import lax
from jax.experimental import pallas as pl
from jax.experimental.pallas import tpu as pltpu
from jax.sharding import PartitionSpec as P

MESH = pl.DeviceIdType.MESH
F32 = jnp.float32
BF16 = jnp.bfloat16
HD = 64
CONTS = 8
SLAB = 128
LOW = -1e30
EPS = 1e-05
LANES = (((1,), (1,)), ((), ()))
HIGHEST = lax.Precision.HIGHEST
MIB = 1 << 20
VMEM = pl.BlockSpec(memory_space=pltpu.VMEM)
SMEM = pl.BlockSpec(memory_space=pltpu.SMEM)


def feature_order():
    place = np.arange(768)
    p, z, r = place // 48, place // 12 % 4, place % 12
    t = (z % 2) * 32 + p * 2 + z // 2
    return t * 12 + r


ORDER = feature_order()
TO_PERM = np.zeros((768, 768), np.float32)
TO_PERM[ORDER, np.arange(768)] = 1.0


ATT_PERM = np.pad(TO_PERM.reshape(4, 192, 768), ((0, 0), (0, 64), (0, 0))).reshape(1024, 768)
OUT_PERM = np.pad(ATT_PERM.reshape(1024, 16, 4, 12).transpose(0, 2, 1, 3), ((0, 0), (0, 0), (0, 0), (0, 4))).reshape(1024, 1024)
LANE_FREQUENCY = 10000.0 ** (-(np.arange(128) % 32) * 2.0 / HD) * (np.arange(128) < HD)
FREQUENCY = LANE_FREQUENCY.astype(np.float32)
OFFSET_ANGLES = np.arange(SLAB)[:, None] * LANE_FREQUENCY[None]
OFFSET_TURNS = np.stack([np.cos(OFFSET_ANGLES), np.sin(OFFSET_ANGLES)]).astype(np.float32)


class Place:
    def __init__(self):
        self.core = lax.axis_index("grp")
        blk = lax.axis_index("blk")
        self.blk, self.head = blk, lax.axis_index("head")
        self.x = lax.rem(blk, 4)
        self.y = lax.rem(lax.div(blk, 4), 4)
        self.z = self.head * 2 + lax.div(blk, 16)

    def other_core(self):
        return (1 - self.core, self.blk, self.head)

    def device(self, x=None, y=None, z=None):
        x = self.x if x is None else x
        y = self.y if y is None else y
        z = self.z if z is None else z
        return (self.core, lax.rem(z, 2) * 16 + y * 4 + x, lax.div(z, 2))

    def ring(self, axis):
        return Ring(self, axis)


class Ring:
    def __init__(self, place, axis):
        self.place, self.axis = place, axis
        self.own = getattr(place, axis)
        self.next = lax.rem(self.own + 1, 4)
        self.prev = lax.rem(self.own + 3, 4)
        self.far = lax.rem(self.own + 2, 4)

    def device(self, index):
        return self.place.device(**{self.axis: index})


def enter(place, axes, far=False):
    barrier = pltpu.get_barrier_semaphore()
    partners = []
    for axis in axes:
        if axis == "core":
            partners.append(place.other_core())
            continue
        ring = place.ring(axis)
        partners += [ring.device(ring.next), ring.device(ring.prev)]
        if axis == "z" or far:
            partners.append(ring.device(ring.far))
    for partner in partners:
        pl.semaphore_signal(barrier, inc=1, device_id=partner, device_id_type=MESH)
    pl.semaphore_wait(barrier, len(partners))


class Links:
    def __init__(self, send, recv):
        self.send, self.recv, self.used, self.sent = send, recv, 0, []

    def copy(self, source, target, device):
        k = self.used
        self.used += 1
        copy = pltpu.make_async_remote_copy(
            src_ref=source,
            dst_ref=target,
            send_sem=self.send.at[k],
            recv_sem=self.recv.at[k],
            device_id=device,
            device_id_type=MESH,
        )
        copy.start()
        self.sent.append(copy)
        return copy

    def finish(self, count=None):
        count = len(self.sent) if count is None else count
        for copy in self.sent[:count]:
            copy.wait_send()
        del self.sent[:count]


def together(steps):
    steps = list(steps)
    while steps:
        left = []
        for step in steps:
            try:
                next(step)
                left.append(step)
            except StopIteration:
                pass
        steps = left


def ring_gather(links, ring, slot):
    right = links.copy(slot(ring.own, None), slot(ring.own, None), ring.device(ring.next))
    left = links.copy(slot(ring.own, None), slot(ring.own, None), ring.device(ring.prev))
    yield
    right.wait_recv()
    on_right = links.copy(slot(ring.prev, 0), slot(ring.prev, 0), ring.device(ring.next))
    left.wait_recv()
    on_left = links.copy(slot(ring.next, 1), slot(ring.next, 1), ring.device(ring.prev))
    yield
    on_right.wait_recv()
    on_left.wait_recv()


def add_into(target, terms, kind):
    *lead, rows, columns = target.shape
    step = 16
    for size in (128, 64, 48, 32):
        if rows % size == 0 and size * columns <= 48 * 1024:
            step = size
            break
    count = rows // step

    def body(k, carry):
        at, rest = [], lax.div(k, count)
        for size in reversed(lead):
            at.insert(0, lax.rem(rest, size))
            rest = lax.div(rest, size)
        at = (*at, pl.ds(pl.multiple_of(lax.rem(k, count) * step, step), step), slice(None))
        total = terms[0][at].astype(F32)
        for term in terms[1:]:
            total = total + term[at].astype(F32)
        target[at] = total.astype(kind)
        return carry

    lax.fori_loop(0, math.prod(lead) * count, body, 0)


def ring_scatter(links, ring, part, room, target, kind):
    low, high, sum_low, sum_high, from_prev, from_next = room
    nxt, prv = ring.device(ring.next), ring.device(ring.prev)
    far_low = links.copy(part(ring.far, 0), low, nxt)
    far_high = links.copy(part(ring.far, 1), high, prv)
    next_high = links.copy(part(ring.next, 1), from_prev(1), nxt)
    prev_low = links.copy(part(ring.prev, 0), from_next(0), prv)
    yield
    far_low.wait_recv()
    add_into(sum_low, [part(ring.next, 0), low], BF16)
    next_low = links.copy(sum_low, from_prev(0), nxt)
    far_high.wait_recv()
    add_into(sum_high, [part(ring.prev, 1), high], BF16)
    prev_high = links.copy(sum_high, from_next(1), prv)
    yield
    for copy in (next_high, prev_low, next_low, prev_high):
        copy.wait_recv()
    add_into(target, [part(ring.own, None), from_prev(None), from_next(None)], kind)


def lead_part(part):
    return pl.ds(0, 4) if part is None else pl.ds(2 * part, 2)


def row_part(rows, part):
    first = (rows // 2 + 15) // 16 * 16
    if part is None:
        return 0, rows
    return (0, first) if part == 0 else (first, rows - first)


def regions(rows, columns, by_rows):
    if by_rows:
        return [(0, rows // 2, 0, columns), (rows // 2, rows // 2, 0, columns)]
    return [(0, rows, 0, columns // 2), (0, rows, columns // 2, columns // 2)]


def plane_gather(links, place, buf, by_rows):
    rows, columns = buf.shape[2:]

    def half(region, x_first):
        r0, rn, c0, cn = region

        def one(k, part):
            off, size = row_part(rn, part)
            y, x = (place.y, k) if x_first else (k, place.x)
            return buf.at[y, x, pl.ds(r0 + off, size), pl.ds(c0, cn)]

        def line(k, part):
            y, x = (k, lead_part(part)) if x_first else (lead_part(part), k)
            return buf.at[y, x, pl.ds(r0, rn), pl.ds(c0, cn)]

        yield from ring_gather(links, place.ring("x" if x_first else "y"), one)
        yield from ring_gather(links, place.ring("y" if x_first else "x"), line)

    a, b = regions(rows, columns, by_rows)
    return half(a, True), half(b, False)


def plane_scatter_room(rows, columns, by_rows):
    rooms = []
    for _, rn, _, cn in regions(rows, columns, by_rows):
        rooms += [pltpu.VMEM((2, rn, cn), BF16)] * 4 + [pltpu.VMEM((4, rn, cn), BF16)] * 3
        low, high = row_part(rn, 0)[1], row_part(rn, 1)[1]
        rooms += [pltpu.VMEM((1, low, cn), BF16), pltpu.VMEM((1, high, cn), BF16)] * 2
        rooms += [pltpu.VMEM((1, rn, cn), BF16)] * 2
    return rooms


def plane_scatter(links, place, buf, rooms, target, by_rows):
    rows, columns = buf.shape[2:]

    def half(region, room, x_first):
        r0, rn, c0, cn = region
        low, high, sum_low, sum_high, prev, nxt, lined = room[:7]
        low1, high1, sum_low1, sum_high1, prev1, nxt1 = room[7:]

        def line(k, part):
            y, x = (lead_part(part), k) if x_first else (k, lead_part(part))
            return buf.at[y, x, pl.ds(r0, rn), pl.ds(c0, cn)]

        def one(k, part):
            off, size = row_part(rn, part)
            return lined.at[pl.ds(k, 1), pl.ds(off, size), :]

        def lined_part(ref):
            return lambda part: ref.at[lead_part(part)]

        def one_part(ref):
            def view(part):
                off, size = row_part(rn, part)
                return ref.at[:, pl.ds(off, size), :]

            return view

        room_a = (low, high, sum_low, sum_high, lined_part(prev), lined_part(nxt))
        room_b = (low1, high1, sum_low1, sum_high1, one_part(prev1), one_part(nxt1))
        yield from ring_scatter(links, place.ring("x" if x_first else "y"), line, room_a, lined, BF16)
        out = target.at[:, pl.ds(r0, rn), pl.ds(c0, cn)]
        yield from ring_scatter(links, place.ring("y" if x_first else "x"), one, room_b, out, F32)

    a, b = regions(rows, columns, by_rows)
    return half(a, rooms[:13], False), half(b, rooms[13:], True)


SMALL_ROOM = [pltpu.VMEM((3, 4, 16, 384), BF16), pltpu.VMEM((4, 16, 384), BF16), pltpu.VMEM((3, 1, 16, 384), BF16)] * 2


def direct_scatter(links, ring, part, room, target, kind):
    copies = []
    for k, to in enumerate((ring.next, ring.prev, ring.far)):
        copies.append(links.copy(part(to), room.at[k], ring.device(to)))
    yield
    for copy in copies:
        copy.wait_recv()
    add_into(target, [part(ring.own), room.at[0], room.at[1], room.at[2]], kind)


def small_scatter(links, place, buf, rooms, target):
    def half(c0, room, x_first):
        columns = pl.ds(c0, 384)
        firsts, lined, lasts = room

        def line(k):
            return buf.at[:, k, :, columns] if x_first else buf.at[k, :, :, columns]

        yield from direct_scatter(links, place.ring("x" if x_first else "y"), line, firsts, lined, BF16)
        out = target.at[:, :, columns]
        yield from direct_scatter(
            links, place.ring("y" if x_first else "x"), lambda k: lined.at[pl.ds(k, 1)], lasts, out, F32
        )

    return half(0, rooms[:3], False), half(384, rooms[3:], True)


def line_scatter_room(rows, columns):
    low, high = row_part(rows, 0)[1], row_part(rows, 1)[1]
    return [pltpu.VMEM((1, low, columns), BF16), pltpu.VMEM((1, high, columns), BF16)] * 2 + [
        pltpu.VMEM((1, rows, columns), BF16)
    ] * 2


def line_scatter(links, place, buf, room, target):
    rows = buf.shape[1]

    def part(k, half):
        off, size = row_part(rows, half)
        return buf.at[pl.ds(k, 1), pl.ds(off, size), :]

    def view(ref):
        def cut(half):
            off, size = row_part(rows, half)
            return ref.at[:, pl.ds(off, size), :]

        return cut

    low, high, sum_low, sum_high, prev, nxt = room
    yield from ring_scatter(
        links, place.ring("z"), part, (low, high, sum_low, sum_high, view(prev), view(nxt)), target, F32
    )


def line_gather(links, place, buf):
    rows = buf.shape[1]

    def slot(k, half):
        off, size = row_part(rows, half)
        return buf.at[k, pl.ds(off, size)]

    yield from ring_gather(links, place.ring("z"), slot)


def line_swap(links, place, source, target):
    ring = place.ring("z")
    copies = []
    for other in (ring.next, ring.prev, ring.far):
        copies.append(links.copy(source.at[other], target.at[ring.own], ring.device(other)))
    target[ring.own] = source[ring.own]
    yield
    for copy in copies:
        copy.wait_recv()


def small_gather(links, ring, slot):
    right = links.copy(slot(ring.own), slot(ring.own), ring.device(ring.next))
    left = links.copy(slot(ring.own), slot(ring.own), ring.device(ring.prev))
    yield
    right.wait_recv()
    left.wait_recv()
    on = links.copy(slot(ring.prev), slot(ring.prev), ring.device(ring.next))
    yield
    on.wait_recv()


def shared_gather(links, place, buf):
    half = buf.shape[3] // 2
    flip = place.core == 1
    columns = pl.ds(pl.multiple_of(place.core * half, 128), half)
    first, second = jnp.where(flip, place.y, place.x), jnp.where(flip, place.x, place.y)
    first_next, first_prev, first_far = [lax.rem(first + k, 4) for k in (1, 3, 2)]
    second_next, second_prev, second_far = [lax.rem(second + k, 4) for k in (1, 3, 2)]

    def block(s, f, part=None):
        y, x = jnp.where(flip, f, s), jnp.where(flip, s, f)
        rows = pl.ds(0, 48) if part is None else (pl.ds(0, 32) if part == 0 else pl.ds(32, 16))
        return buf.at[y, x, rows, columns]

    def device(s, f):
        return place.device(x=jnp.where(flip, s, f), y=jnp.where(flip, f, s))

    def send(s, f, to, part=None):
        return links.copy(block(s, f, part), block(s, f, part), to)

    handed = []

    def hand(s, f):
        handed.append(links.copy(block(s, f), block(s, f), place.other_core()))

    on_right, on_left = device(second, first_next), device(second, first_prev)
    up, down = device(second_next, first), device(second_prev, first)
    order = (first, first_prev, first_next, first_far)
    ups, downs = [], []

    def line(k):
        ups.append(send(second, order[k], up))
        downs.append(send(second, order[k], down))

    right = send(second, first, on_right)
    left = send(second, first, on_left)
    line(0)
    yield
    right.wait_recv()
    far_low = send(second, first_prev, on_right, 0)
    line(1)
    left.wait_recv()
    far_high = send(second, first_next, on_left, 1)
    line(2)
    hand(second, first_prev)
    hand(second, first_next)
    yield
    far_low.wait_recv()
    far_high.wait_recv()
    line(3)
    hand(second, first_far)
    yield
    far = []
    for k in range(4):
        ups[k].wait_recv()
        if k < 2:
            far.append(send(second_prev, order[k], up))
        hand(second_prev, order[k])
        downs[k].wait_recv()
        if k >= 2:
            far.append(send(second_next, order[k], down))
        hand(second_next, order[k])
    yield
    for k in range(4):
        far[k].wait_recv()
        hand(second_far, order[k])
    yield
    for copy in handed:
        copy.wait_recv()


def advance(*steps):
    for step in steps:
        next(step, None)


def finish(*steps):
    together(steps)


def dot(left, right):
    return jnp.dot(left, right, preferred_element_type=F32)


def dot_right_t(left, right):
    return lax.dot_general(left, right, LANES, preferred_element_type=F32)


def pack_rows():
    i = lax.broadcasted_iota(jnp.int32, (48, 64), 0)
    k = lax.broadcasted_iota(jnp.int32, (48, 64), 1)
    return (k == lax.div(i, 12) * 16 + lax.rem(i, 12)).astype(BF16)


def spread_rows():
    k = lax.broadcasted_iota(jnp.int32, (64, 48), 0)
    i = lax.broadcasted_iota(jnp.int32, (64, 48), 1)
    return (k == lax.div(i, 12) * 16 + lax.rem(i, 12)).astype(BF16)


def merged(ref):
    rows, columns = ref.shape[0] * ref.shape[1] * ref.shape[2], ref.shape[3]
    return ref[...].reshape(rows, columns)


def mean_square(values):
    return jnp.mean(values * values, axis=-1, keepdims=True)


def norm_back(grad, normed, scale):
    return scale * (grad - normed * jnp.mean(grad * normed, axis=-1, keepdims=True))


def slab_turns(line_ref, turn_ref, s):
    rows = line_ref[s]
    cos_base, sin_base = rows[0:1], rows[1:2]
    cos_off, sin_off = turn_ref[0], turn_ref[1]
    lane = lax.broadcasted_iota(jnp.int32, (SLAB, SLAB), 1)
    sign = jnp.where(lane < 32, -1.0, jnp.where(lane < 64, 1.0, 0.0))
    return cos_base * cos_off - sin_base * sin_off, (sin_base * cos_off + cos_base * sin_off) * sign


def turned(field, cosine, sine):
    lane = lax.broadcasted_iota(jnp.int32, (SLAB, SLAB), 1)
    return field * cosine + jnp.where(lane < 32, pltpu.roll(field, 96, 1), pltpu.roll(field, 32, 1)) * sine


def half_rows(values, k):
    return values[k * SLAB : (k + 1) * SLAB]


def direct_gather(links, place, buf):
    half = buf.shape[3] // 2
    ring_x, ring_y = place.ring("x"), place.ring("y")
    a, b = pl.ds(0, half), pl.ds(half, half)

    def spread(ring, view):
        return [links.copy(view, view, ring.device(k)) for k in (ring.next, ring.prev, ring.far)]

    first = spread(ring_x, buf.at[place.y, place.x, :, a])
    second = spread(ring_y, buf.at[place.y, place.x, :, b])
    yield
    for copy in first:
        copy.wait_recv()
    first = spread(ring_y, buf.at[place.y, :, :, a])
    for copy in second:
        copy.wait_recv()
    second = spread(ring_x, buf.at[:, place.x, :, b])
    yield
    for copy in first + second:
        copy.wait_recv()


def slab_place(at):
    return lax.div(at, 16), lax.rem(lax.div(at, 4), 4), lax.rem(at, 4)


def slab_gather(links, place, buf):
    def half(z0, x_first):
        def one(k, part):
            y, x = (place.y, k) if x_first else (k, place.x)
            return buf.at[y, x, pl.ds(z0, 2) if part is None else pl.ds(z0 + part, 1)]

        def line(k, part):
            y, x = (k, lead_part(part)) if x_first else (lead_part(part), k)
            return buf.at[y, x, pl.ds(z0, 2)]

        yield from ring_gather(links, place.ring("x" if x_first else "y"), one)
        yield from ring_gather(links, place.ring("y" if x_first else "x"), line)

    return half(0, True), half(2, False)


def slab_scatter_room():
    few, many = pltpu.VMEM((2, 2, SLAB, SLAB), BF16), pltpu.VMEM((4, 2, SLAB, SLAB), BF16)
    one, two = pltpu.VMEM((1, SLAB, SLAB), BF16), pltpu.VMEM((2, SLAB, SLAB), BF16)
    return ([few] * 4 + [many] * 3 + [one] * 4 + [two] * 2) * 2


def slab_scatter(links, place, buf, rooms, target):
    def half(z0, room, x_first):
        low, high, sum_low, sum_high, prev, nxt, lined = room[:7]
        low1, high1, sum_low1, sum_high1, prev1, nxt1 = room[7:]

        def line(k, part):
            y, x = (lead_part(part), k) if x_first else (k, lead_part(part))
            return buf.at[y, x, pl.ds(z0, 2)]

        def one(k, part):
            return lined.at[k] if part is None else lined.at[k, pl.ds(part, 1)]

        def lined_part(ref):
            return lambda part: ref.at[lead_part(part)]

        def one_part(ref):
            return lambda part: ref.at[pl.ds(0, 2) if part is None else pl.ds(part, 1)]

        room_a = (low, high, sum_low, sum_high, lined_part(prev), lined_part(nxt))
        room_b = (low1, high1, sum_low1, sum_high1, one_part(prev1), one_part(nxt1))
        yield from ring_scatter(links, place.ring("x" if x_first else "y"), line, room_a, lined, BF16)
        out = target.at[pl.ds(z0, 2)]
        yield from ring_scatter(links, place.ring("y" if x_first else "x"), one, room_b, out, F32)

    return half(0, rooms[:13], False), half(2, rooms[13:], True)


def keys_of(kv_ref, table, s, first, count):
    places = [slab_place(jnp.clip(table[s * 24 + first + k, 0], 0, 63)) for k in range(count)]
    return jnp.concatenate([kv_ref[y, x, z] for y, x, z in places], 0)


def query_positions(table, s, shape, axis):
    return table[s * 24 + 20, 0] + lax.broadcasted_iota(jnp.int32, shape, axis)


def attend_head(j, table, q_ref, kv_ref, top_ref, sum_ref, acc_ref, between):
    def fold(s, first, count, first_key):
        keys = keys_of(kv_ref, table, s, first, count)
        width = count * SLAB
        pos_q = query_positions(table, s, (SLAB, 1), 0)
        pos_k = first_key + lax.broadcasted_iota(jnp.int32, (1, width), 1)
        scores = dot_right_t(q_ref[s, :, pl.ds(j * 128, 128)], keys)
        scores = jnp.where(pos_k <= pos_q, scores, LOW)
        top = top_ref[s]
        new_top = jnp.maximum(top, jnp.max(scores, axis=1, keepdims=True))
        weights = jnp.exp(scores - new_top[:, 0:1])
        decay = jnp.exp(top - new_top)
        sum_ref[s] = sum_ref[s] * decay + jnp.sum(weights, axis=1, keepdims=True)
        acc_ref[s] = acc_ref[s] * decay + dot(weights.astype(BF16), keys)
        top_ref[s] = new_top

    for s in range(4):
        top_ref[s] = jnp.full((SLAB, SLAB), LOW, F32)
        sum_ref[s] = jnp.zeros((SLAB, SLAB), F32)
        acc_ref[s] = jnp.zeros((SLAB, SLAB), F32)

    def prompt(c, carry):
        for s in range(4):
            fold(s, c * 4, 4, c * 512)
        return carry

    lax.fori_loop(0, 2, prompt, 0)
    between(0)
    lax.fori_loop(2, 4, prompt, 0)
    between(1)
    for s in range(4):
        fold(s, 16, 2, 2048)


def attend_back_head(j, table, q_ref, kv_ref, grad_ref, logs, deltas, dq_ref, terms_ref, pair_ref, between):
    lane = lax.broadcasted_iota(jnp.int32, (SLAB, SLAB), 1)
    for s in range(4):
        grads = grad_ref[s, :, pl.ds(128 * (j // 2), 128)].astype(F32)
        if j != 1:
            grads = pltpu.roll(grads, 64, 1)
        pair_ref[s, pl.ds(0, SLAB)] = q_ref[s, :, pl.ds(j * 128, 128)]
        pair_ref[s, pl.ds(SLAB, SLAB)] = jnp.where(lane < 64, 0.0, grads).astype(BF16)
        dq_ref[s] = jnp.zeros((SLAB, SLAB), F32)

    def fold(s, first, count, first_key):
        keys = keys_of(kv_ref, table, s, first, count)
        width = count * SLAB
        pos_q = query_positions(table, s, (1, SLAB), 1)
        pos_k = first_key + lax.broadcasted_iota(jnp.int32, (width, 1), 0)
        pair = pair_ref[s]
        both = dot_right_t(keys, pair)
        weights = jnp.where(pos_k <= pos_q, jnp.exp(both[:, :SLAB] - logs[s]), 0.0)
        slopes = (weights * (both[:, SLAB:] - deltas[s])).astype(BF16)
        terms = dot(jnp.concatenate([slopes, weights.astype(BF16)], 1), pair)
        terms_ref[s, pl.ds(first, count)] = terms.astype(BF16).reshape(count, SLAB, SLAB)
        dq_ref[s] += lax.dot_general(slopes, keys, (((0,), (0,)), ((), ())), preferred_element_type=F32)

    def prompt(c, carry):
        for s in range(4):
            fold(s, c * 4, 4, c * 512)
        return carry

    lax.fori_loop(0, 2, prompt, 0)
    between(0)
    lax.fori_loop(2, 4, prompt, 0)
    between(1)
    for s in range(4):
        fold(s, 16, 2, 2048)


def sum_terms(table, terms_ref, part_ref):
    def slab(t, carry):
        places = [jnp.clip(table[96 + s, t], 0, 18) for s in range(4)]
        total = terms_ref[0, places[0]].astype(F32)
        for s in range(1, 4):
            total = total + terms_ref[s, places[s]].astype(F32)
        y, x, z = slab_place(t)
        part_ref[y, x, z] = total.astype(BF16)
        return carry

    lax.fori_loop(0, 64, slab, 0)


def lookups(total, own, meta_ref):
    seg, base = total[2:3], total[3:4]
    lane = lax.broadcasted_iota(jnp.int32, (1, SLAB), 1)
    lane_at = lane.astype(F32)
    n = lax.broadcasted_iota(jnp.int32, (24, 1), 0)
    back_rows = jnp.zeros((8, SLAB), F32)
    back_row = lax.broadcasted_iota(jnp.int32, (8, 1), 0)
    for s in range(4):
        mine = lane == own * 4 + s
        seg_q = jnp.sum(jnp.where(mine, seg, 0.0), axis=1, keepdims=True)
        base_q = jnp.sum(jnp.where(mine, base, 0.0), axis=1, keepdims=True)
        prompt = jnp.where(seg_q >= CONTS + 1.0, CONTS + 1.0, 0.0)
        want = jnp.where(n < 16, prompt, seg_q)
        hit = (seg == want) & (base == n.astype(F32) * SLAB) & (lane < 64)
        places = jnp.max(jnp.where(hit, lane_at, 0.0), axis=1, keepdims=True)
        listed = jnp.where(n == 20, base_q, places)
        meta_ref[pl.ds(s * 24, 24), :] = jnp.broadcast_to(listed, (24, SLAB)).astype(jnp.int32)
        visible = (seg == prompt) | (seg == seg_q)
        places = jnp.where(visible, jnp.minimum(base * (1.0 / SLAB), 17.0), 18.0)
        back_rows = jnp.where(back_row == s, places, back_rows)
    meta_ref[pl.ds(96, 8), :] = back_rows.astype(jnp.int32)


def layer_kernel(
    tok_ref, cot_ref, w_ref, ff_ref, down_ref, gain_ref, perm_ref, turn_ref, desc_ref, perm_att_hbm, out_perm_hbm,
    out_ref, in_ref, down_sum_ref, got_ff_ref, got_ref, got_out_ref,
    perm_att, out_perm, const_sem, line_ref, descs, meta_ref, table, table_sem,
    for_line, for_line_ff, rows, rows_o, rows_ff, one, cots, wqkv, wo, wff, q_ref, kv0, kv1, kv2,
    tops, sums, accs, att_ref, lse_ref, atts, att_s, mid_s, gm_s, two, act, pre, turn_t, part, part_out, sum_z, sum_out,
    to_heads, grads_ref, terms, pairs, kv_own, d_s, qkv_sum, ff_sum,
    og_part, og_sum, og_next, *rest,
):
    send, recv = rest[-2:]
    rooms = list(rest[:-2])

    def take(count):
        out = rooms[:count]
        del rooms[:count]
        return out

    back_room, ff_room, out_room = take(6), take(26), take(6)
    kv_rooms = [take(26) for _ in range(3)]
    qkv_room, in_room, og_line_room, og_room = take(26), take(6), take(6), take(6)
    kvs = (kv0, kv1, kv2)

    const_copies = [
        pltpu.make_async_copy(perm_att_hbm, perm_att, const_sem.at[0]),
        pltpu.make_async_copy(out_perm_hbm, out_perm, const_sem.at[1]),
    ]
    for copy in const_copies:
        copy.start()
    place = Place()
    enter(place, ("x", "y", "z", "core"), True)
    links = Links(send, recv)
    own = place.y * 4 + place.x

    line_ref[place.z] = desc_ref[...]
    lined = small_gather(links, place.ring("z"), lambda k: line_ref.at[k])
    w = w_ref[...].astype(F32)
    gain = gain_ref[:, 0:1]
    none = jnp.zeros((16, HD), F32)
    for z in range(4):
        pieces = []
        for j in range(3):
            c = 192 * z + 64 * j
            pieces += [w[:, c : c + 64] * gain, none, w[:, 768 + c : 832 + c] * gain, w[:, 1536 + c : 1600 + c] * gain]
        for_line[z] = jnp.concatenate(pieces, 1).astype(BF16)
    swap = line_swap(links, place, for_line, rows)
    advance(swap, lined)
    x = dot(tok_ref[...], perm_ref[...])
    one[place.z] = (x * lax.rsqrt(mean_square(x) + EPS)).astype(BF16)
    ones = line_gather(links, place, one)
    advance(ones)
    finish(swap)
    wqkv[place.y, place.x] = dot(pack_rows(), rows[...].reshape(64, 768)).astype(BF16)
    qkv = direct_gather(links, place, wqkv)
    advance(qkv)
    gain = gain_ref[:, 1:2]
    for z in range(4):
        for k in range(2):
            pieces = []
            for p in range(16):
                c = 3072 * k + ((z % 2) * 32 + p * 2 + z // 2) * 48
                pieces.append(ff_ref[:, c : c + 48].astype(F32) * gain)
            for_line_ff[z, :, pl.ds(768 * k, 768)] = jnp.concatenate(pieces, 1).astype(BF16)
    advance(lined, ones)
    advance(qkv)
    finish(lined)
    descs[place.y, place.x] = line_ref[0] + line_ref[1] + line_ref[2] + line_ref[3]
    desc_x = small_gather(links, place.ring("x"), lambda k: descs.at[place.y, k])
    desc_y = small_gather(links, place.ring("y"), lambda k: descs.at[k])
    advance(desc_x)
    finish(ones)
    rows_o[place.z] = w_ref[:, pl.ds(2304, 768)]
    o_line = small_gather(links, place.ring("z"), lambda k: rows_o.at[k])
    ff_swap = line_swap(links, place, for_line_ff, rows_ff)
    cots[place.z] = cot_ref[...]
    cot_gather = line_gather(links, place, cots)
    advance(o_line, ff_swap, cot_gather)
    finish(qkv)

    lines = one[...].reshape(512, 768)
    gathers = []
    for j in range(3):
        field = dot(lines, wqkv[:, :, :, pl.ds(256 * j, 256)].reshape(768, 256))
        for s in range(4):
            cosine, sine = slab_turns(line_ref, turn_ref, s)
            query = turned(half_rows(field[:, 0:128], s), cosine, sine)
            q_ref[s, :, pl.ds(128 * j, 128)] = (query * 0.125).astype(BF16)
            pair = turned(half_rows(field[:, 128:256], s), cosine, sine)
            kvs[j][place.y, place.x, s] = pair.astype(BF16)
        gathers.append(slab_gather(links, place, kvs[j]))
        advance(*gathers[j])
    advance(desc_x)
    for j in range(3):
        advance(*gathers[j])
    finish(desc_x)
    advance(desc_y)
    advance(*gathers[0])
    advance(desc_y, o_line)
    advance(*gathers[0])
    advance(*gathers[1])
    finish(desc_y)
    total = jnp.zeros((8, SLAB), F32)
    for y in range(4):
        for k in range(4):
            total = total + descs[y, k]
    lookups(total, own, meta_ref)
    copy = pltpu.make_async_copy(meta_ref, table, table_sem)
    copy.start()
    copy.wait()
    finish(ff_swap, o_line)
    wo[place.y, place.x] = dot(pack_rows(), rows_o[...].reshape(64, 768)).astype(BF16)
    for c in range(0, 1536, 768):
        wff[place.y, place.x, :, pl.ds(c, 768)] = dot(
            pack_rows(), rows_ff[:, :, pl.ds(c, 768)].reshape(64, 768)
        ).astype(BF16)
    wff[place.y, place.x, :, pl.ds(1536, 768)] = down_ref[...]
    advance(cot_gather)
    for copy in const_copies:
        copy.wait()

    lane = lax.broadcasted_iota(jnp.int32, (SLAB, SLAB), 1)
    o_gather = direct_gather(links, place, wo)
    w_gather = shared_gather(links, place, wff)
    for j in range(3):
        finish(*gathers[j])

        def between(k, j=j):
            if j == 0 and k == 1:
                advance(*gathers[1])
                advance(*gathers[2])
            if j == 1 and k == 0:
                advance(cot_gather)
            if j == 1 and k == 1:
                advance(*gathers[2])
            if j == 2:
                advance(o_gather)
                advance(w_gather)

        if j == 2:
            advance(o_gather)
            advance(w_gather)
        attend_head(j, table, q_ref, kvs[j], tops, sums, accs, between)
        for s in range(4):
            head = accs[s] / sums[s]
            if j == 0:
                att_ref[s, :, 0:128] = jnp.where(lane < 64, pltpu.roll(head, 64, 1), 0.0).astype(BF16)
            elif j == 1:
                att_ref[s, :, 0:128] = jnp.where(lane < 64, att_ref[s, :, 0:128].astype(F32), head).astype(BF16)
            else:
                att_ref[s, :, 128:256] = jnp.where(lane < 64, pltpu.roll(head, 64, 1), 0.0).astype(BF16)
            logs = tops[s] + jnp.log(sums[s])
            lse_ref[s] = logs if j == 0 else jnp.where(lane == j, logs, lse_ref[s])
    att_swap = line_swap(links, place, att_ref, atts)
    advance(att_swap)
    finish(cot_gather, o_gather)
    advance(w_gather)
    finish(att_swap)

    att = dot(atts[0], perm_att[pl.ds(0, 256), :])
    for z in range(1, 4):
        att = att + dot(atts[z], perm_att[pl.ds(256 * z, 256), :])
    att_s[...] = att.astype(BF16)
    mid_s[...] = tok_ref[...].astype(F32) + dot(att_s[...], merged(wo))
    middle = mid_s[...]
    scale_two = lax.rsqrt(mean_square(middle) + EPS)
    two[place.z] = dot((middle * scale_two).astype(BF16), perm_ref[...]).astype(BF16)
    two_gather = line_gather(links, place, two)
    advance(two_gather)
    advance(w_gather)
    att = dot(atts[0], out_perm[pl.ds(0, 256), :])
    for z in range(1, 4):
        att = att + dot(atts[z], out_perm[pl.ds(256 * z, 256), :])
    att_by_z = att.astype(BF16).T
    advance(two_gather)
    together([w_gather, two_gather])

    def block(r, carry):
        at = pl.ds(pl.multiple_of(r * 256, 256), 256)
        two_b = two[pl.ds(r * 2, 2)].reshape(256, 768)
        cot_b = cots[pl.ds(r * 2, 2)].reshape(256, 768)
        gate_w = wff[:, :, :, pl.ds(0, 768)].reshape(768, 768)
        up_w = wff[:, :, :, pl.ds(768, 768)].reshape(768, 768)
        down_w = wff[:, :, :, pl.ds(1536, 768)].reshape(768, 768)
        gate = dot(two_b, gate_w)
        up = dot(two_b, up_w)
        sig = 1.0 / (1.0 + jnp.exp(-gate))
        silu = gate * sig
        act_b = (silu * up).astype(BF16)
        act[at, :] = act_b
        grad_act = dot_right_t(cot_b, down_w)
        grad_gate = (grad_act * up * (sig * (1.0 + gate * (1.0 - sig)))).astype(BF16)
        grad_up = (grad_act * silu).astype(BF16)
        pre[at, pl.ds(0, 768)] = grad_gate
        pre[at, pl.ds(768, 768)] = grad_up
        back = dot_right_t(grad_gate, gate_w) + dot_right_t(grad_up, up_w)
        part[pl.ds(r * 2, 2)] = back.astype(BF16).reshape(2, SLAB, 768)
        part_out[pl.ds(r * 2, 2)] = dot(act_b, down_w).astype(BF16).reshape(2, SLAB, 768)
        return carry

    lax.fori_loop(0, 2, block, 0)
    links.finish()
    back_sum = line_scatter(links, place, part, back_room, sum_z)
    advance(back_sum)
    turn_t[...] = two[...].reshape(512, 768).T

    def first_grads(c, carry):
        at = pl.ds(pl.multiple_of(c * 256, 256), 256)
        wff[:, :, :, at] = dot(turn_t[...], pre[:, at]).astype(BF16).reshape(4, 4, 48, 256)
        return carry

    def last_grads(c, carry):
        at = pl.ds(pl.multiple_of(c * 256, 256), 256)
        to = pl.ds(pl.multiple_of(1536 + c * 256, 256), 256)
        cot_all = cots[:, :, at].reshape(512, 256)
        wff[:, :, :, to] = dot(turn_t[...], cot_all).astype(BF16).reshape(4, 4, 48, 256)
        return carry

    lax.fori_loop(0, 6, first_grads, 0)
    advance(back_sum)
    turn_t[...] = act[...].T
    lax.fori_loop(0, 3, last_grads, 0)
    ff = plane_scatter(links, place, wff, ff_room, ff_sum, False)
    advance(*ff)
    finish(back_sum)
    links.finish(6)

    grad = dot_right_t(sum_z[0].astype(BF16), perm_ref[...])
    middle = mid_s[...]
    scale_two = lax.rsqrt(mean_square(middle) + EPS)
    gm_s[...] = cot_ref[...].astype(F32) + norm_back(grad, middle * scale_two, scale_two)
    low = gm_s[...].astype(BF16)
    grad_att = dot_right_t(low, merged(wo)).astype(BF16)
    for z in range(4):
        to_heads[z] = dot_right_t(grad_att, perm_att[pl.ds(256 * z, 256), :]).astype(BF16)
    heads_swap = line_swap(links, place, to_heads, grads_ref)
    advance(heads_swap)
    out_sum = line_scatter(links, place, part_out, out_room, sum_out)
    advance(out_sum)
    turn_t[...] = one[...].reshape(512, 768).T
    og_part[...] = dot(att_by_z, low).astype(BF16).reshape(4, 256, 768)
    for s in range(4):
        terms[s, 18] = jnp.zeros((SLAB, SLAB), BF16)
    finish(heads_swap)
    advance(*ff)

    which = lax.broadcasted_iota(jnp.int32, (8, SLAB), 0)
    unit = (lax.broadcasted_iota(jnp.int32, (8, SLAB), 1) == which).astype(F32)
    at_lane = lax.broadcasted_iota(jnp.int32, (8, 256), 1)
    pick = (lax.div(at_lane, HD) == lax.broadcasted_iota(jnp.int32, (8, 256), 0)).astype(F32)
    logs, deltas = [], []
    for s in range(4):
        inner = grads_ref[s].astype(F32) * att_ref[s].astype(F32)
        delta = lax.dot_general(pick, inner, LANES, precision=HIGHEST, preferred_element_type=F32)
        log = lax.dot_general(unit, lse_ref[s], LANES, precision=HIGHEST, preferred_element_type=F32)
        logs.append([jnp.sum(jnp.where(which == k, log, 0.0), axis=0, keepdims=True) for k in range(3)])
        deltas.append([jnp.sum(jnp.where(which == k, delta, 0.0), axis=0, keepdims=True) for k in range(3)])

    scatters = []

    def keys_back(j):
        for s in range(4):
            cosine, sine = slab_turns(line_ref, turn_ref, s)
            grad = kv_own[j, s]
            d_s[pl.ds(s * SLAB, SLAB), pl.ds(256 * j + 128, 128)] = turned(grad, cosine, -sine).astype(BF16)
        at = pl.ds(256 * j, 256)
        wo[:, :, :, at] = dot(turn_t[...], d_s[:, at]).astype(BF16).reshape(4, 4, 48, 256)

    og_line = line_scatter(links, place, og_part, og_line_room, og_sum)
    spread = spread_rows()
    for j in range(3):

        def between(k, j=j):
            if j == 0:
                advance(*ff)
                if k == 0:
                    advance(out_sum)
            if j == 1:
                advance(*scatters[0])
            if j == 2 and k == 0:
                advance(*scatters[0])
                advance(*scatters[1])
            if j == 2 and k == 1:
                finish(*scatters[0])
                advance(*scatters[1])

        attend_back_head(
            j, table, q_ref, kvs[j], grads_ref, [v[j] for v in logs], [v[j] for v in deltas], accs, terms, pairs, between
        )
        sum_terms(table, terms, kvs[j])
        scatters.append(slab_scatter(links, place, kvs[j], kv_rooms[j], kv_own.at[j]))
        advance(*scatters[j])
        for s in range(4):
            cosine, sine = slab_turns(line_ref, turn_ref, s)
            grad = jnp.where(lane < 64, accs[s] * 0.125, 0.0)
            d_s[pl.ds(s * SLAB, SLAB), pl.ds(256 * j, 128)] = turned(grad, cosine, -sine).astype(BF16)
        if j == 0:
            finish(out_sum)
            advance(og_line)
            out_ref[...] = (mid_s[...] + sum_out[0]).astype(BF16)
            finish(*ff)
            down_sum_ref[...] = ff_sum[0, :, pl.ds(1536, 768)]
            for c in range(0, 1536, 768):
                for_line_ff[:, :, pl.ds(c, 768)] = (
                    dot(spread, ff_sum[0, :, pl.ds(c, 768)].astype(BF16)).astype(BF16).reshape(4, 16, 768)
                )
            grads_swap = line_swap(links, place, for_line_ff, got_ff_ref)
            advance(grads_swap)
        if j == 1:
            advance(og_line)

    advance(*scatters[2])
    advance(*scatters[1])
    keys_back(0)
    finish(og_line, grads_swap)
    og_next[...] = og_sum[0].astype(BF16).reshape(4, 4, 16, 768)
    finish(*scatters[1])
    advance(*scatters[2])
    keys_back(1)
    og = small_scatter(links, place, og_next, og_room, got_out_ref)
    advance(*scatters[2])
    advance(*og)
    finish(*scatters[2])
    for s in range(4):
        cosine, sine = slab_turns(line_ref, turn_ref, s)
        grad = kv_own[2, s]
        d_s[pl.ds(s * SLAB, SLAB), pl.ds(640, 128)] = turned(grad, cosine, -sine).astype(BF16)

    def last_block(r, carry):
        at = pl.ds(pl.multiple_of(r * 256, 256), 256)
        part[pl.ds(r * 2, 2)] = dot_right_t(d_s[at, :], merged(wqkv)).astype(BF16).reshape(2, SLAB, 768)
        return carry

    lax.fori_loop(0, 2, last_block, 0)
    in_sum = line_scatter(links, place, part, in_room, sum_z)
    advance(in_sum)
    at = pl.ds(512, 256)
    wo[:, :, :, at] = dot(turn_t[...], d_s[:, at]).astype(BF16).reshape(4, 4, 48, 256)
    qkv = plane_scatter(links, place, wo, qkv_room, qkv_sum, False)
    advance(*qkv)
    advance(*og)
    advance(*qkv)
    advance(in_sum)
    advance(*qkv)
    advance(*og)
    finish(in_sum)
    grad = dot_right_t(sum_z[0].astype(BF16), perm_ref[...])
    x = tok_ref[...].astype(F32)
    scale = lax.rsqrt(mean_square(x) + EPS)
    in_ref[...] = gm_s[...] + norm_back(grad, x * scale, scale)
    finish(*qkv)
    for_line[...] = dot(spread, qkv_sum[0].astype(BF16)).astype(BF16).reshape(4, 16, 768)
    last = line_swap(links, place, for_line, got_ref)
    advance(last)
    finish(*og)
    finish(last)
    links.finish()


LINE = pltpu.VMEM((4, SLAB, 768), BF16)
KV = pltpu.VMEM((4, 4, 4, SLAB, SLAB), BF16)
OUTS = [
    ((SLAB, 768), BF16),
    ((SLAB, 768), F32),
    ((48, 768), F32),
    ((4, 16, 1536), BF16),
    ((4, 16, 768), BF16),
    ((1, 16, 768), F32),
]
ROOM = (
    [
        pltpu.VMEM((1024, 768), BF16),
        pltpu.VMEM((1024, 1024), BF16),
        pltpu.SemaphoreType.DMA((2,)),
        pltpu.VMEM((4, 8, SLAB), F32),
        pltpu.VMEM((4, 4, 8, SLAB), F32),
        pltpu.VMEM((104, SLAB), jnp.int32),
        pltpu.SMEM((104, SLAB), jnp.int32),
        pltpu.SemaphoreType.DMA,
        pltpu.VMEM((4, 16, 768), BF16),
        pltpu.VMEM((4, 16, 1536), BF16),
        pltpu.VMEM((4, 16, 768), BF16),
        pltpu.VMEM((4, 16, 768), BF16),
        pltpu.VMEM((4, 16, 1536), BF16),
        LINE,
        LINE,
        pltpu.VMEM((4, 4, 48, 768), BF16),
        pltpu.VMEM((4, 4, 48, 768), BF16),
        pltpu.VMEM((4, 4, 48, 2304), BF16),
        pltpu.VMEM((4, SLAB, 384), BF16),
        KV,
        KV,
        KV,
        pltpu.VMEM((4, SLAB, SLAB), F32),
        pltpu.VMEM((4, SLAB, SLAB), F32),
        pltpu.VMEM((4, SLAB, SLAB), F32),
        pltpu.VMEM((4, SLAB, 256), BF16),
        pltpu.VMEM((4, SLAB, SLAB), F32),
        pltpu.VMEM((4, SLAB, 256), BF16),
        pltpu.VMEM((SLAB, 768), BF16),
        pltpu.VMEM((SLAB, 768), F32),
        pltpu.VMEM((SLAB, 768), F32),
        LINE,
        pltpu.VMEM((512, 768), BF16),
        pltpu.VMEM((512, 1536), BF16),
        pltpu.VMEM((768, 512), BF16),
        LINE,
        LINE,
        pltpu.VMEM((1, SLAB, 768), F32),
        pltpu.VMEM((1, SLAB, 768), F32),
        pltpu.VMEM((4, SLAB, 256), BF16),
        pltpu.VMEM((4, SLAB, 256), BF16),
        pltpu.VMEM((4, 19, SLAB, SLAB), BF16),
        pltpu.VMEM((4, 256, SLAB), BF16),
        pltpu.VMEM((3, 4, SLAB, SLAB), F32),
        pltpu.VMEM((512, 768), BF16),
        pltpu.VMEM((1, 48, 768), F32),
        pltpu.VMEM((1, 48, 2304), F32),
        pltpu.VMEM((4, 256, 768), BF16),
        pltpu.VMEM((1, 256, 768), F32),
        pltpu.VMEM((4, 4, 16, 768), BF16),
    ]
    + line_scatter_room(SLAB, 768)
    + plane_scatter_room(48, 2304, False)
    + line_scatter_room(SLAB, 768)
    + slab_scatter_room() * 3
    + plane_scatter_room(48, 768, False)
    + line_scatter_room(SLAB, 768)
    + line_scatter_room(256, 768)
    + SMALL_ROOM
)


def join_columns(w):
    rows = w.shape[1]
    return w.reshape(2, 2, rows, 16, 48).transpose(2, 1, 3, 0, 4).reshape(rows, 3072)


def per_device(
    tokens, gain_one, w_query, w_key, w_value, w_out, gain_two, w_gate, w_up, w_down, cotangent, segment_ids, positions
):
    blk, head = lax.axis_index("blk"), lax.axis_index("head")
    z, own = head * 2 + blk // 16, blk % 16
    perm = jnp.asarray(TO_PERM, BF16)
    perm_att = jnp.asarray(ATT_PERM, BF16)
    out_perm = jnp.asarray(OUT_PERM, BF16)
    turn = jnp.asarray(OFFSET_TURNS, F32)
    first_gain, second_gain = gain_one.astype(F32)[:, None], gain_two.astype(F32)[:, None]

    seg = segment_ids.reshape(2, SLAB)[head, 0].astype(F32)
    base = positions.reshape(2, SLAB)[head, 0].astype(F32)
    angles = base * jnp.asarray(FREQUENCY, F32)[None]
    row = lax.broadcasted_iota(jnp.int32, (8, SLAB), 0)
    lane = lax.broadcasted_iota(jnp.int32, (8, SLAB), 1)
    here = lane == own * 4 + z
    desc = jnp.where(
        row == 0,
        jnp.cos(angles),
        jnp.where(
            row == 1,
            jnp.sin(angles),
            jnp.where(here & (row == 2), seg, jnp.where(here & (row == 3), base, 0.0)),
        ),
    )
    w_attention = jnp.pad(jnp.concatenate([w_query, w_key, w_value, w_out], 1), ((0, 4), (0, 0)))
    w_ff = jnp.pad(jnp.concatenate([w_gate, w_up], 1), ((0, 4), (0, 0)))
    gains = jnp.pad(jnp.concatenate([first_gain, second_gain], 1), ((0, 4), (0, SLAB - 2)))

    output, input_grad, down_grad, got_ff, got_qkv, got_out = pl.pallas_call(
        layer_kernel,
        out_shape=tuple(jax.ShapeDtypeStruct(shape, kind) for shape, kind in OUTS),
        in_specs=[VMEM] * 9 + [pl.BlockSpec(memory_space=pl.ANY)] * 2,
        out_specs=tuple([VMEM] * len(OUTS)),
        scratch_shapes=ROOM + [pltpu.SemaphoreType.DMA((320,))] * 2,
        compiler_params=pltpu.CompilerParams(collective_id=0, has_side_effects=True, vmem_limit_bytes=62 * MIB),
        name="layer",
    )(tokens, cotangent, w_attention, w_ff, w_down, gains, perm, turn, desc, perm_att, out_perm)

    got_ff = got_ff[:, :12].astype(F32)
    got_qkv = got_qkv[:, :12].astype(F32)
    by_kind = got_qkv.reshape(4, 12, 3, 4, HD).transpose(3, 1, 0, 2, 4).reshape(4, 12, 768)
    gate_grad, up_grad = join_columns(got_ff[:, :, :768]), join_columns(got_ff[:, :, 768:])
    gain_one_grad = jnp.sum(by_kind[0] * w_query + by_kind[2] * w_key + by_kind[3] * w_value, axis=1)
    gain_two_grad = jnp.sum(gate_grad * w_gate + up_grad * w_up, axis=1)
    return (
        output,
        input_grad,
        gain_one_grad,
        by_kind[0] * first_gain,
        by_kind[2] * first_gain,
        by_kind[3] * first_gain,
        got_out[0, :12],
        gain_two_grad,
        gate_grad * second_gain,
        up_grad * second_gain,
        down_grad,
    )


def solution(mesh):
    rows = P(("grp", "blk", "head"), None)
    flat = P(("grp", "blk", "head"))
    weight = P(("blk", "head"), None)
    gain = P(("blk", "head"))
    ids = P(("grp", "blk"))
    in_specs = (rows, gain, weight, weight, weight, weight, gain, weight, weight, weight, rows, ids, ids)
    out_specs = (rows, rows, flat, rows, rows, rows, rows, flat, rows, rows, rows)
    return jax.shard_map(per_device, mesh=mesh, in_specs=in_specs, out_specs=out_specs, check_vma=False)
```

time: 293 us -> 235 us (0.80)
  Pallas kernels: 267 us -> 211 us
    pallas_call x5 -> x1, Pallas kernels: 267 us -> 211 us  [per_device(): pl.pallas_call(layer_kernel, out_shape=tuple((jax.ShapeDtypeStruct(shape,...]
where the time goes in v3:
time: 235 us; the launch traced here: 232 us
  Pallas kernels  211 us (90%)
  other arithmetic  12.1 us (5%)
  local copies, waits for them, and re-layouts  7.06 us (3%)
    pallas_call x1, Pallas kernels, per_device(): pl.pallas_call(layer_kernel, out_shape=tuple((jax.ShapeDtypeStruct(shape,...  211 us

profile of v3, /device:TPU:0, one launch (start us, length us, event | category | flops | bytes accessed | tf_op | source)
XLA Modules:
  0.0 231.8 jit_solution(7504321246945663224)
XLA Ops:
  0.7 1.2 fusion.13
  1.9 1.3 multiply_cosine_fusion
  3.3 2.0 select_select_fusion.desc_ref
  5.2 0.7 fusion.11
  5.9 0.1 copy.48
  6.0 0.6 pad.14.gain_ref
  6.6 1.6 fusion.2.ff_ref
  8.3 1.5 fusion.9.w_ref
  9.7 211.3 %layer.1 = (bf16[128,768]{1,0:T(8,128)(2,1)}, f32[128,768]{1,0:T(8,128)}, f32[48,768]{1,0:T(8,128)}, bf16[4,16,1536]{2,1,0:T(8,128)(2,1)}, bf16[4,16,768]{2,1,0:T(8,128)(2,1)}, /*index=5*/f32[1,16,768]{2,1,0:T(8,128)}) custom-call(bf16[128,768]{1,0:T(8,128)(2,1)} %tok_ref.1, bf16[128,768]{1,0:T(8,128)(2,1)} %cot_ref.1, bf16[16,3072]{1,0:T(8,128)(2,1)} %fusion.9.w_ref, ...), custom_call_target="tpu_custom_call" | custom-call | tf_op jit(solution)/shard_map/layer/pallas_call | solution.py:1152
  221.1 1.0 slice_convert_fusion
  222.1 0.1 copy.50
  222.2 0.2 reshape.63
  222.4 0.3 copy.51
  222.7 0.0 copy-start.1
  222.7 0.0 copy-start.2
  222.7 0.5 reshape.64
  223.3 0.0 copy-start.8
  223.3 0.1 copy.52
  223.4 0.2 reshape.65
  223.6 0.3 copy.53
  223.9 0.5 reshape.66
  224.4 0.0 copy-start.5
  224.4 0.0 copy-start.6
  224.4 0.0 copy-start.7
  224.4 0.0 copy-done.1
  224.4 0.0 copy-done.2
  224.5 0.0 copy-start.9
  224.5 0.0 copy-start.3
  224.5 1.5 broadcast_multiply_fusion
  225.9 0.0 copy-start
  225.9 0.0 copy-done.8
  226.0 0.1 copy.49
  226.1 0.0 copy-start.4
  226.1 0.2 reshape.67
  226.3 0.7 slice_reduce_fusion.2
  226.9 0.1 squeeze.18
  227.1 0.1 squeeze.19
  227.2 0.1 squeeze.8
  227.3 0.0 copy-done.5
  227.3 0.0 copy-done.6
  227.3 0.0 copy-done.7
  227.3 1.4 broadcast_multiply_fusion.2
  228.6 0.0 copy-done.9
  228.6 0.6 slice_bitcast_fusion
  229.3 0.0 copy-done.3
  229.3 0.7 copy.57
  230.0 0.0 copy-done
  230.0 0.7 copy.58
  230.7 0.0 copy-done.4
  230.7 0.7 copy.59
  (6 shorter events, 0.1 us)
Async XLA Ops:
  222.7 1.7 copy-start.1
  222.7 1.7 copy-start.2
  223.3 2.7 %copy-start.8 = (bf16[4,16,768]{2,1,0:T(8,128)(2,1)S(1)}, bf16[4,16,768]{2,1,0:T(8,128)(2,1)}, u32[]{:S(2)}) copy-start(bf16[4,16,768]{2,1,0:T(8,128)(2,1)} %get-tuple-element.19) | copy-start | bytes 294916
  224.4 2.9 %copy-start.5 = (bf16[12,768]{1,0:T(8,128)(2,1)S(1)}, bf16[12,768]{1,0:T(8,128)(2,1)}, u32[]{:S(2)}) copy-start(bf16[12,768]{1,0:T(8,128)(2,1)} %param.22) | copy-start | bytes 55300
  224.4 2.9 %copy-start.6 = (bf16[12,768]{1,0:T(8,128)(2,1)S(1)}, bf16[12,768]{1,0:T(8,128)(2,1)}, u32[]{:S(2)}) copy-start(bf16[12,768]{1,0:T(8,128)(2,1)} %param.21) | copy-start | bytes 55300
  224.4 2.9 %copy-start.7 = (bf16[12,768]{1,0:T(8,128)(2,1)S(1)}, bf16[12,768]{1,0:T(8,128)(2,1)}, u32[]{:S(2)}) copy-start(bf16[12,768]{1,0:T(8,128)(2,1)} %param.20) | copy-start | bytes 55300
  224.5 4.2 %copy-start.9 = (f32[1,16,768]{2,1,0:T(8,128)S(1)}, f32[1,16,768]{2,1,0:T(8,128)}, u32[]{:S(2)}) copy-start(f32[1,16,768]{2,1,0:T(8,128)} %get-tuple-element.20) | copy-start | bytes 147460
  224.5 4.8 %copy-start.3 = (bf16[128,768]{1,0:T(8,128)(2,1)S(1)}, bf16[128,768]{1,0:T(8,128)(2,1)}, u32[]{:S(2)}) copy-start(bf16[128,768]{1,0:T(8,128)(2,1)} %get-tuple-element.60) | copy-start | bytes 589828
  225.9 4.0 %copy-start = (f32[128,768]{1,0:T(8,128)S(1)}, f32[128,768]{1,0:T(8,128)}, u32[]{:S(2)}) copy-start(f32[128,768]{1,0:T(8,128)} %get-tuple-element.61) | copy-start | bytes 1179652
  226.1 4.6 %copy-start.4 = (f32[48,768]{1,0:T(8,128)S(1)}, f32[48,768]{1,0:T(8,128)}, u32[]{:S(2)}) copy-start(f32[48,768]{1,0:T(8,128)} %get-tuple-element.70) | copy-start | bytes 442372

commit v4 on v3

--- a/solution.py
+++ b/solution.py
@@ -38,8 +38,9 @@
 ATT_PERM = np.pad(TO_PERM.reshape(4, 192, 768), ((0, 0), (0, 64), (0, 0))).reshape(1024, 768)
 OUT_PERM = np.pad(ATT_PERM.reshape(1024, 16, 4, 12).transpose(0, 2, 1, 3), ((0, 0), (0, 0), (0, 0), (0, 4))).reshape(1024, 1024)
 LANE_FREQUENCY = 10000.0 ** (-(np.arange(128) % 32) * 2.0 / HD) * (np.arange(128) < HD)
-FREQUENCY = LANE_FREQUENCY.astype(np.float32)
 OFFSET_ANGLES = np.arange(SLAB)[:, None] * LANE_FREQUENCY[None]
+BASE_ANGLES = SLAB * np.arange(24)[:, None] * LANE_FREQUENCY[None]
+BASE_TURNS = np.stack([np.cos(BASE_ANGLES), np.sin(BASE_ANGLES)]).astype(np.float32)
 OFFSET_TURNS = np.stack([np.cos(OFFSET_ANGLES), np.sin(OFFSET_ANGLES)]).astype(np.float32)
 
 
@@ -77,20 +78,19 @@
         return self.place.device(**{self.axis: index})
 
 
-def enter(place, axes, far=False):
+def announce(place):
+    partners = [place.other_core()]
+    for axis in ("x", "y", "z"):
+        ring = place.ring(axis)
+        partners += [ring.device(ring.next), ring.device(ring.prev), ring.device(ring.far)]
     barrier = pltpu.get_barrier_semaphore()
-    partners = []
-    for axis in axes:
-        if axis == "core":
-            partners.append(place.other_core())
-            continue
-        ring = place.ring(axis)
-        partners += [ring.device(ring.next), ring.device(ring.prev)]
-        if axis == "z" or far:
-            partners.append(ring.device(ring.far))
     for partner in partners:
         pl.semaphore_signal(barrier, inc=1, device_id=partner, device_id_type=MESH)
-    pl.semaphore_wait(barrier, len(partners))
+    return len(partners)
+
+
+def enter(partners):
+    pl.semaphore_wait(pltpu.get_barrier_semaphore(), partners)
 
 
 class Links:
@@ -160,13 +160,14 @@
             at.insert(0, lax.rem(rest, size))
             rest = lax.div(rest, size)
         at = (*at, pl.ds(pl.multiple_of(lax.rem(k, count) * step, step), step), slice(None))
-        total = terms[0][at].astype(F32)
+        total = terms[0][at].astype(kind)
         for term in terms[1:]:
-            total = total + term[at].astype(F32)
-        target[at] = total.astype(kind)
+            total = total + term[at].astype(kind)
+        target[at] = total
         return carry
 
-    lax.fori_loop(0, math.prod(lead) * count, body, 0)
+    trips = math.prod(lead) * count
+    lax.fori_loop(0, trips, body, 0, unroll=2 if trips % 2 == 0 else 1)
 
 
 def ring_scatter(links, ring, part, room, target, kind):
@@ -274,7 +275,13 @@
     return half(a, rooms[:13], False), half(b, rooms[13:], True)
 
 
-SMALL_ROOM = [pltpu.VMEM((3, 4, 16, 384), BF16), pltpu.VMEM((4, 16, 384), BF16), pltpu.VMEM((3, 1, 16, 384), BF16)] * 2
+def small_scatter_room(rows, columns):
+    half = columns // 2
+    return [
+        pltpu.VMEM((3, 4, rows, half), BF16),
+        pltpu.VMEM((4, rows, half), BF16),
+        pltpu.VMEM((3, 1, rows, half), BF16),
+    ] * 2
 
 
 def direct_scatter(links, ring, part, room, target, kind):
@@ -287,9 +294,11 @@
     add_into(target, [part(ring.own), room.at[0], room.at[1], room.at[2]], kind)
 
 
-def small_scatter(links, place, buf, rooms, target):
-    def half(c0, room, x_first):
-        columns = pl.ds(c0, 384)
+def small_scatter(links, place, buf, c0, width, rooms, target):
+    size = width // 2
+
+    def half(first, room, x_first):
+        columns = pl.ds(first, size)
         firsts, lined, lasts = room
 
         def line(k):
@@ -301,7 +310,7 @@
             links, place.ring("y" if x_first else "x"), lambda k: lined.at[pl.ds(k, 1)], lasts, out, F32
         )
 
-    return half(0, rooms[:3], False), half(384, rooms[3:], True)
+    return half(c0, rooms[:3], False), half(c0 + size, rooms[3:], True)
 
 
 def line_scatter_room(rows, columns):
@@ -493,25 +502,24 @@
     return values[k * SLAB : (k + 1) * SLAB]
 
 
-def direct_gather(links, place, buf):
-    half = buf.shape[3] // 2
+def direct_gather(links, place, buf, first, second):
     ring_x, ring_y = place.ring("x"), place.ring("y")
-    a, b = pl.ds(0, half), pl.ds(half, half)
+    a, b = pl.ds(*first), pl.ds(*second)
 
     def spread(ring, view):
         return [links.copy(view, view, ring.device(k)) for k in (ring.next, ring.prev, ring.far)]
 
-    first = spread(ring_x, buf.at[place.y, place.x, :, a])
-    second = spread(ring_y, buf.at[place.y, place.x, :, b])
-    yield
-    for copy in first:
+    over_x = spread(ring_x, buf.at[place.y, place.x, :, a])
+    over_y = spread(ring_y, buf.at[place.y, place.x, :, b])
+    yield
+    for copy in over_x:
         copy.wait_recv()
-    first = spread(ring_y, buf.at[place.y, :, :, a])
-    for copy in second:
+    over_x = spread(ring_y, buf.at[place.y, :, :, a])
+    for copy in over_y:
         copy.wait_recv()
-    second = spread(ring_x, buf.at[:, place.x, :, b])
-    yield
-    for copy in first + second:
+    over_y = spread(ring_x, buf.at[:, place.x, :, b])
+    yield
+    for copy in over_x + over_y:
         copy.wait_recv()
 
 
@@ -519,20 +527,56 @@
     return lax.div(at, 16), lax.rem(lax.div(at, 4), 4), lax.rem(at, 4)
 
 
+def flow_gather(links, over, along, block):
+    s, f = along.own, over.own
+    on_right, on_left = over.device(over.next), over.device(over.prev)
+    up, down = along.device(along.next), along.device(along.prev)
+    order = (f, over.prev, over.next, over.far)
+    ups, downs, far = [], [], []
+
+    def send(s, f, to, part=None):
+        return links.copy(block(s, f, part), block(s, f, part), to)
+
+    def line(k):
+        ups.append(send(s, order[k], up))
+        downs.append(send(s, order[k], down))
+
+    right, left = send(s, f, on_right), send(s, f, on_left)
+    line(0)
+    yield
+    right.wait_recv()
+    far_low = send(s, over.prev, on_right, 0)
+    left.wait_recv()
+    far_high = send(s, over.next, on_left, 1)
+    line(1)
+    line(2)
+    yield
+    far_low.wait_recv()
+    far_high.wait_recv()
+    line(3)
+    yield
+    for k in range(4):
+        ups[k].wait_recv()
+        if k < 2:
+            far.append(send(along.prev, order[k], up))
+        downs[k].wait_recv()
+        if k >= 2:
+            far.append(send(along.next, order[k], down))
+    yield
+    for copy in far:
+        copy.wait_recv()
+
+
 def slab_gather(links, place, buf):
-    def half(z0, x_first):
-        def one(k, part):
-            y, x = (place.y, k) if x_first else (k, place.x)
-            return buf.at[y, x, pl.ds(z0, 2) if part is None else pl.ds(z0 + part, 1)]
-
-        def line(k, part):
-            y, x = (k, lead_part(part)) if x_first else (lead_part(part), k)
-            return buf.at[y, x, pl.ds(z0, 2)]
-
-        yield from ring_gather(links, place.ring("x" if x_first else "y"), one)
-        yield from ring_gather(links, place.ring("y" if x_first else "x"), line)
-
-    return half(0, True), half(2, False)
+    ring_x, ring_y = place.ring("x"), place.ring("y")
+
+    def slabs(z0, part):
+        return pl.ds(z0, 2) if part is None else pl.ds(z0 + part, 1)
+
+    return (
+        flow_gather(links, ring_x, ring_y, lambda s, f, part: buf.at[s, f, slabs(0, part)]),
+        flow_gather(links, ring_y, ring_x, lambda s, f, part: buf.at[f, s, slabs(2, part)]),
+    )
 
 
 def slab_scatter_room():
@@ -657,7 +701,7 @@
         part_ref[y, x, z] = total.astype(BF16)
         return carry
 
-    lax.fori_loop(0, 64, slab, 0)
+    lax.fori_loop(0, 64, slab, 0, unroll=4)
 
 
 def lookups(total, own, meta_ref):
@@ -683,8 +727,71 @@
     meta_ref[pl.ds(96, 8), :] = back_rows.astype(jnp.int32)
 
 
+def column_of(gain_ref):
+    i = lax.broadcasted_iota(jnp.int32, (12, 12), 0)
+    k = lax.broadcasted_iota(jnp.int32, (12, 12), 1)
+    return jnp.sum(jnp.where(i == k, gain_ref[...].astype(F32), 0.0), axis=1, keepdims=True)
+
+
+def plane_columns(z):
+    return [((z % 2) * 32 + p * 2 + z // 2) * 48 for p in range(16)]
+
+
+def own_slab(place, at, seg_ref, pos_ref, base_ref):
+    lane = lax.broadcasted_iota(jnp.int32, (1, SLAB), 1)
+    high = place.head == 1
+    seg = jnp.where(high, seg_ref[1:2], seg_ref[0:1]).astype(F32)
+    base = (jnp.where(high, pos_ref[1:2], pos_ref[0:1]) - lane).astype(F32)
+    m = lax.broadcasted_iota(jnp.int32, (24, SLAB), 0).astype(F32)
+    cosine, sine = [
+        jnp.sum(jnp.where(m == base * (1.0 / SLAB), base_ref[k], 0.0), axis=0, keepdims=True) for k in range(2)
+    ]
+    row = lax.broadcasted_iota(jnp.int32, (8, SLAB), 0)
+    here = (lane == at) & (row >= 2)
+    facts = jnp.where(here, jnp.where(row == 2, seg, jnp.where(row == 3, base, 0.0)), 0.0)
+    return jnp.where(row == 0, cosine, jnp.where(row == 1, sine, facts))
+
+
+def finish_kernel(
+    ff_ref, qkv_ref, og_ref, wq_ref, wk_ref, wv_ref, gate_ref, up_ref, gain1_ref, gain2_ref, out_in, grad_in, down_in,
+    out_ref, grad_ref, dgain1_ref, dq_ref, dk_ref, dv_ref, do_ref, dgain2_ref, dgate_ref, dup_ref, down_ref,
+):
+    out_ref[...] = out_in[...]
+    grad_ref[...] = grad_in[...]
+    down_ref[...] = down_in[...]
+    i = lax.broadcasted_iota(jnp.int32, (12, 12), 0)
+    k = lax.broadcasted_iota(jnp.int32, (12, 12), 1)
+
+    def row_of(column):
+        return jnp.sum(jnp.where(i == k, column, 0.0), axis=0, keepdims=True)
+
+    gain = column_of(gain1_ref)
+    grads = [qkv_ref[z].astype(F32)[:12] for z in range(4)]
+    total = jnp.zeros((12, 1), F32)
+    for c, w_ref, to_ref in ((128, wq_ref, dq_ref), (0, wk_ref, dk_ref), (64, wv_ref, dv_ref)):
+        grad = jnp.concatenate([grads[z][:, 256 * j + c : 256 * j + c + HD] for z in range(4) for j in range(3)], 1)
+        total = total + jnp.sum(grad * w_ref[...].astype(F32), axis=1, keepdims=True)
+        to_ref[...] = grad * gain
+    dgain1_ref[...] = row_of(total)
+    do_ref[...] = og_ref[0, pl.ds(0, 12)]
+
+    gain = column_of(gain2_ref)
+    total = jnp.zeros((12, 1), F32)
+    for k_at, w_ref, to_ref in ((0, gate_ref, dgate_ref), (768, up_ref, dup_ref)):
+        pieces = {}
+        for z in range(4):
+            grad = ff_ref[z, :, pl.ds(k_at, 768)].astype(F32)[:12]
+            for p, c in enumerate(plane_columns(z)):
+                pieces[c] = grad[:, 48 * p : 48 * p + 48]
+        grad = jnp.concatenate([pieces[c] for c in sorted(pieces)], 1)
+        total = total + jnp.sum(grad * w_ref[...].astype(F32), axis=1, keepdims=True)
+        to_ref[...] = grad * gain
+    dgain2_ref[...] = row_of(total)
+
+
 def layer_kernel(
-    tok_ref, cot_ref, w_ref, ff_ref, down_ref, gain_ref, perm_ref, turn_ref, desc_ref, perm_att_hbm, out_perm_hbm,
+    tok_ref, cot_ref, wq_ref, wk_ref, wv_ref, wo_ref, gate_ref, up_ref, down_ref, gain1_ref, gain2_ref, seg_ref, pos_ref,
+    perm_ref, turn_ref, base_ref, perm_att_hbm, out_perm_hbm,
     out_ref, in_ref, down_sum_ref, got_ff_ref, got_ref, got_out_ref,
     perm_att, out_perm, const_sem, line_ref, descs, meta_ref, table, table_sem,
     for_line, for_line_ff, rows, rows_o, rows_ff, one, cots, wqkv, wo, wff, q_ref, kv0, kv1, kv2,
@@ -702,7 +809,8 @@
 
     back_room, ff_room, out_room = take(6), take(26), take(6)
     kv_rooms = [take(26) for _ in range(3)]
-    qkv_room, in_room, og_line_room, og_room = take(26), take(6), take(6), take(6)
+    qkv_rooms = [take(6) for _ in range(3)]
+    in_room, og_line_room, og_room = take(6), take(6), take(6)
     kvs = (kv0, kv1, kv2)
 
     const_copies = [
@@ -712,74 +820,80 @@
     for copy in const_copies:
         copy.start()
     place = Place()
-    enter(place, ("x", "y", "z", "core"), True)
+    partners = announce(place)
     links = Links(send, recv)
     own = place.y * 4 + place.x
 
-    line_ref[place.z] = desc_ref[...]
+    line_ref[place.z] = own_slab(place, own * 4 + place.z, seg_ref, pos_ref, base_ref)
     lined = small_gather(links, place.ring("z"), lambda k: line_ref.at[k])
-    w = w_ref[...].astype(F32)
-    gain = gain_ref[:, 0:1]
-    none = jnp.zeros((16, HD), F32)
+    gain = column_of(gain1_ref)
+    w_q, w_k, w_v = [ref[...].astype(F32) * gain for ref in (wq_ref, wk_ref, wv_ref)]
+    none, blank = jnp.zeros((12, HD), F32), jnp.zeros((4, 768), F32)
     for z in range(4):
-        pieces = []
+        pieces, last = [], []
         for j in range(3):
-            c = 192 * z + 64 * j
-            pieces += [w[:, c : c + 64] * gain, none, w[:, 768 + c : 832 + c] * gain, w[:, 1536 + c : 1600 + c] * gain]
-        for_line[z] = jnp.concatenate(pieces, 1).astype(BF16)
+            at = slice(192 * z + 64 * j, 192 * z + 64 * j + 64)
+            pieces += [w_k[:, at], w_v[:, at]]
+            last += [w_q[:, at], none]
+        pieces += last
+        for_line[z] = jnp.concatenate([jnp.concatenate(pieces, 1), blank], 0).astype(BF16)
+    x = dot(tok_ref[...], perm_ref[...])
+    one[place.z] = (x * lax.rsqrt(mean_square(x) + EPS)).astype(BF16)
+    enter(partners)
     swap = line_swap(links, place, for_line, rows)
     advance(swap, lined)
-    x = dot(tok_ref[...], perm_ref[...])
-    one[place.z] = (x * lax.rsqrt(mean_square(x) + EPS)).astype(BF16)
     ones = line_gather(links, place, one)
     advance(ones)
     finish(swap)
     wqkv[place.y, place.x] = dot(pack_rows(), rows[...].reshape(64, 768)).astype(BF16)
-    qkv = direct_gather(links, place, wqkv)
-    advance(qkv)
-    gain = gain_ref[:, 1:2]
-    for z in range(4):
-        for k in range(2):
-            pieces = []
-            for p in range(16):
-                c = 3072 * k + ((z % 2) * 32 + p * 2 + z // 2) * 48
-                pieces.append(ff_ref[:, c : c + 48].astype(F32) * gain)
-            for_line_ff[z, :, pl.ds(768 * k, 768)] = jnp.concatenate(pieces, 1).astype(BF16)
-    advance(lined, ones)
-    advance(qkv)
+    kv_gather = direct_gather(links, place, wqkv, (0, 256), (256, 128))
+    q_gather = direct_gather(links, place, wqkv, (512, 256), (384, 128))
+    advance(kv_gather)
+    gain = column_of(gain2_ref)
+    for k, ref in enumerate((gate_ref, up_ref)):
+        w = ref[...].astype(F32) * gain
+        for z in range(4):
+            pieces = [w[:, c : c + 48] for c in plane_columns(z)]
+            for_line_ff[z, :, pl.ds(768 * k, 768)] = jnp.concatenate([jnp.concatenate(pieces, 1), blank], 0).astype(BF16)
+    advance(lined, kv_gather, ones)
+    advance(q_gather)
     finish(lined)
     descs[place.y, place.x] = line_ref[0] + line_ref[1] + line_ref[2] + line_ref[3]
     desc_x = small_gather(links, place.ring("x"), lambda k: descs.at[place.y, k])
     desc_y = small_gather(links, place.ring("y"), lambda k: descs.at[k])
     advance(desc_x)
-    finish(ones)
-    rows_o[place.z] = w_ref[:, pl.ds(2304, 768)]
+    finish(ones, kv_gather)
+    rows_o[place.z] = jnp.concatenate([wo_ref[...].astype(F32), blank], 0).astype(BF16)
     o_line = small_gather(links, place.ring("z"), lambda k: rows_o.at[k])
     ff_swap = line_swap(links, place, for_line_ff, rows_ff)
     cots[place.z] = cot_ref[...]
     cot_gather = line_gather(links, place, cots)
-    advance(o_line, ff_swap, cot_gather)
-    finish(qkv)
 
     lines = one[...].reshape(512, 768)
-    gathers = []
+    gathers = [slab_gather(links, place, kv) for kv in kvs]
     for j in range(3):
-        field = dot(lines, wqkv[:, :, :, pl.ds(256 * j, 256)].reshape(768, 256))
+        field = dot(lines, wqkv[:, :, :, pl.ds(128 * j, 128)].reshape(768, 128))
         for s in range(4):
             cosine, sine = slab_turns(line_ref, turn_ref, s)
-            query = turned(half_rows(field[:, 0:128], s), cosine, sine)
-            q_ref[s, :, pl.ds(128 * j, 128)] = (query * 0.125).astype(BF16)
-            pair = turned(half_rows(field[:, 128:256], s), cosine, sine)
-            kvs[j][place.y, place.x, s] = pair.astype(BF16)
-        gathers.append(slab_gather(links, place, kvs[j]))
-        advance(*gathers[j])
-    advance(desc_x)
-    for j in range(3):
-        advance(*gathers[j])
+            kvs[j][place.y, place.x, s] = turned(half_rows(field, s), cosine, sine).astype(BF16)
+        if j < 2:
+            advance(*gathers[j])
+    advance(o_line, ff_swap, cot_gather)
+    advance(q_gather, desc_x)
+    advance(*gathers[0])
+    advance(*gathers[0])
     finish(desc_x)
     advance(desc_y)
-    advance(*gathers[0])
+    advance(*gathers[1])
+    advance(*gathers[2])
     advance(desc_y, o_line)
+    finish(q_gather)
+    field = dot(lines, wqkv[:, :, :, pl.ds(384, 384)].reshape(768, 384))
+    for s in range(4):
+        cosine, sine = slab_turns(line_ref, turn_ref, s)
+        for j in range(3):
+            query = turned(half_rows(field[:, 128 * j : 128 * j + 128], s), cosine, sine)
+            q_ref[s, :, pl.ds(128 * j, 128)] = (query * 0.125).astype(BF16)
     advance(*gathers[0])
     advance(*gathers[1])
     finish(desc_y)
@@ -803,20 +917,25 @@
         copy.wait()
 
     lane = lax.broadcasted_iota(jnp.int32, (SLAB, SLAB), 1)
-    o_gather = direct_gather(links, place, wo)
+    o_gather = direct_gather(links, place, wo, (0, 384), (384, 384))
     w_gather = shared_gather(links, place, wff)
     for j in range(3):
         finish(*gathers[j])
 
         def between(k, j=j):
+            if j == 0 and k == 0:
+                advance(*gathers[1])
+                advance(*gathers[2])
             if j == 0 and k == 1:
-                advance(*gathers[1])
                 advance(*gathers[2])
             if j == 1 and k == 0:
                 advance(cot_gather)
+                links.finish(40)
             if j == 1 and k == 1:
                 advance(*gathers[2])
-            if j == 2:
+            if j == 2 and k == 0:
+                links.finish(40)
+            if j == 2 and k == 1:
                 advance(o_gather)
                 advance(w_gather)
 
@@ -836,9 +955,10 @@
             lse_ref[s] = logs if j == 0 else jnp.where(lane == j, logs, lse_ref[s])
     att_swap = line_swap(links, place, att_ref, atts)
     advance(att_swap)
-    finish(cot_gather, o_gather)
     advance(w_gather)
-    finish(att_swap)
+    finish(cot_gather)
+    links.finish(40)
+    finish(att_swap, o_gather)
 
     att = dot(atts[0], perm_att[pl.ds(0, 256), :])
     for z in range(1, 4):
@@ -878,13 +998,19 @@
         pre[at, pl.ds(768, 768)] = grad_up
         back = dot_right_t(grad_gate, gate_w) + dot_right_t(grad_up, up_w)
         part[pl.ds(r * 2, 2)] = back.astype(BF16).reshape(2, SLAB, 768)
-        part_out[pl.ds(r * 2, 2)] = dot(act_b, down_w).astype(BF16).reshape(2, SLAB, 768)
+        return carry
+
+    def out_block(r, carry):
+        at = pl.ds(pl.multiple_of(r * 256, 256), 256)
+        down_w = wff[:, :, :, pl.ds(1536, 768)].reshape(768, 768)
+        part_out[pl.ds(r * 2, 2)] = dot(act[at, :], down_w).astype(BF16).reshape(2, SLAB, 768)
         return carry
 
     lax.fori_loop(0, 2, block, 0)
     links.finish()
     back_sum = line_scatter(links, place, part, back_room, sum_z)
     advance(back_sum)
+    lax.fori_loop(0, 2, out_block, 0)
     turn_t[...] = two[...].reshape(512, 768).T
 
     def first_grads(c, carry):
@@ -941,13 +1067,17 @@
 
     scatters = []
 
-    def keys_back(j):
+    def keys_turn(j):
         for s in range(4):
             cosine, sine = slab_turns(line_ref, turn_ref, s)
-            grad = kv_own[j, s]
-            d_s[pl.ds(s * SLAB, SLAB), pl.ds(256 * j + 128, 128)] = turned(grad, cosine, -sine).astype(BF16)
-        at = pl.ds(256 * j, 256)
-        wo[:, :, :, at] = dot(turn_t[...], d_s[:, at]).astype(BF16).reshape(4, 4, 48, 256)
+            d_s[pl.ds(s * SLAB, SLAB), pl.ds(128 * j, 128)] = turned(kv_own[j, s], cosine, -sine).astype(BF16)
+
+    def keys_grads(j):
+        pair = jnp.concatenate([d_s[:, pl.ds(128 * j, 128)], d_s[:, pl.ds(384 + 128 * j, 128)]], 1)
+        wo[:, :, :, pl.ds(256 * j, 256)] = dot(turn_t[...], pair).astype(BF16).reshape(4, 4, 48, 256)
+        scatter = small_scatter(links, place, wo, 256 * j, 256, qkv_rooms[j], qkv_sum)
+        advance(*scatter)
+        return scatter
 
     og_line = line_scatter(links, place, og_part, og_line_room, og_sum)
     spread = spread_rows()
@@ -976,7 +1106,7 @@
         for s in range(4):
             cosine, sine = slab_turns(line_ref, turn_ref, s)
             grad = jnp.where(lane < 64, accs[s] * 0.125, 0.0)
-            d_s[pl.ds(s * SLAB, SLAB), pl.ds(256 * j, 128)] = turned(grad, cosine, -sine).astype(BF16)
+            d_s[pl.ds(s * SLAB, SLAB), pl.ds(384 + 128 * j, 128)] = turned(grad, cosine, -sine).astype(BF16)
         if j == 0:
             finish(out_sum)
             advance(og_line)
@@ -994,20 +1124,22 @@
 
     advance(*scatters[2])
     advance(*scatters[1])
-    keys_back(0)
+    keys_turn(0)
+    qkv = list(keys_grads(0))
     finish(og_line, grads_swap)
     og_next[...] = og_sum[0].astype(BF16).reshape(4, 4, 16, 768)
+    links.finish(60)
     finish(*scatters[1])
     advance(*scatters[2])
-    keys_back(1)
-    og = small_scatter(links, place, og_next, og_room, got_out_ref)
+    keys_turn(1)
+    qkv += keys_grads(1)
+    og = small_scatter(links, place, og_next, 0, 768, og_room, got_out_ref)
+    advance(*og)
     advance(*scatters[2])
-    advance(*og)
+    links.finish(60)
+    advance(*qkv)
     finish(*scatters[2])
-    for s in range(4):
-        cosine, sine = slab_turns(line_ref, turn_ref, s)
-        grad = kv_own[2, s]
-        d_s[pl.ds(s * SLAB, SLAB), pl.ds(640, 128)] = turned(grad, cosine, -sine).astype(BF16)
+    keys_turn(2)
 
     def last_block(r, carry):
         at = pl.ds(pl.multiple_of(r * 256, 256), 256)
@@ -1017,27 +1149,24 @@
     lax.fori_loop(0, 2, last_block, 0)
     in_sum = line_scatter(links, place, part, in_room, sum_z)
     advance(in_sum)
-    at = pl.ds(512, 256)
-    wo[:, :, :, at] = dot(turn_t[...], d_s[:, at]).astype(BF16).reshape(4, 4, 48, 256)
-    qkv = plane_scatter(links, place, wo, qkv_room, qkv_sum, False)
-    advance(*qkv)
+    last_qkv = keys_grads(2)
+    finish(*qkv)
     advance(*og)
-    advance(*qkv)
     advance(in_sum)
-    advance(*qkv)
-    advance(*og)
+    advance(*last_qkv)
+    finish(*og)
+    links.finish(len(links.sent) - 12)
+    finish(*last_qkv)
+    for_line[...] = dot(spread, qkv_sum[0].astype(BF16)).astype(BF16).reshape(4, 16, 768)
+    last = line_swap(links, place, for_line, got_ref)
+    advance(last)
     finish(in_sum)
     grad = dot_right_t(sum_z[0].astype(BF16), perm_ref[...])
     x = tok_ref[...].astype(F32)
     scale = lax.rsqrt(mean_square(x) + EPS)
     in_ref[...] = gm_s[...] + norm_back(grad, x * scale, scale)
-    finish(*qkv)
-    for_line[...] = dot(spread, qkv_sum[0].astype(BF16)).astype(BF16).reshape(4, 16, 768)
-    last = line_swap(links, place, for_line, got_ref)
-    advance(last)
-    finish(*og)
+    links.finish()
     finish(last)
-    links.finish()
 
 
 LINE = pltpu.VMEM((4, SLAB, 768), BF16)
@@ -1107,76 +1236,42 @@
     + plane_scatter_room(48, 2304, False)
     + line_scatter_room(SLAB, 768)
     + slab_scatter_room() * 3
-    + plane_scatter_room(48, 768, False)
+    + small_scatter_room(48, 256) * 3
     + line_scatter_room(SLAB, 768)
     + line_scatter_room(256, 768)
-    + SMALL_ROOM
+    + small_scatter_room(16, 768)
 )
-
-
-def join_columns(w):
-    rows = w.shape[1]
-    return w.reshape(2, 2, rows, 16, 48).transpose(2, 1, 3, 0, 4).reshape(rows, 3072)
 
 
 def per_device(
     tokens, gain_one, w_query, w_key, w_value, w_out, gain_two, w_gate, w_up, w_down, cotangent, segment_ids, positions
 ):
-    blk, head = lax.axis_index("blk"), lax.axis_index("head")
-    z, own = head * 2 + blk // 16, blk % 16
-    perm = jnp.asarray(TO_PERM, BF16)
-    perm_att = jnp.asarray(ATT_PERM, BF16)
-    out_perm = jnp.asarray(OUT_PERM, BF16)
-    turn = jnp.asarray(OFFSET_TURNS, F32)
-    first_gain, second_gain = gain_one.astype(F32)[:, None], gain_two.astype(F32)[:, None]
-
-    seg = segment_ids.reshape(2, SLAB)[head, 0].astype(F32)
-    base = positions.reshape(2, SLAB)[head, 0].astype(F32)
-    angles = base * jnp.asarray(FREQUENCY, F32)[None]
-    row = lax.broadcasted_iota(jnp.int32, (8, SLAB), 0)
-    lane = lax.broadcasted_iota(jnp.int32, (8, SLAB), 1)
-    here = lane == own * 4 + z
-    desc = jnp.where(
-        row == 0,
-        jnp.cos(angles),
-        jnp.where(
-            row == 1,
-            jnp.sin(angles),
-            jnp.where(here & (row == 2), seg, jnp.where(here & (row == 3), base, 0.0)),
-        ),
-    )
-    w_attention = jnp.pad(jnp.concatenate([w_query, w_key, w_value, w_out], 1), ((0, 4), (0, 0)))
-    w_ff = jnp.pad(jnp.concatenate([w_gate, w_up], 1), ((0, 4), (0, 0)))
-    gains = jnp.pad(jnp.concatenate([first_gain, second_gain], 1), ((0, 4), (0, SLAB - 2)))
-
+    gains = (gain_one.reshape(1, 12), gain_two.reshape(1, 12))
     output, input_grad, down_grad, got_ff, got_qkv, got_out = pl.pallas_call(
         layer_kernel,
         out_shape=tuple(jax.ShapeDtypeStruct(shape, kind) for shape, kind in OUTS),
-        in_specs=[VMEM] * 9 + [pl.BlockSpec(memory_space=pl.ANY)] * 2,
+        in_specs=[VMEM] * 16 + [pl.BlockSpec(memory_space=pl.ANY)] * 2,
         out_specs=tuple([VMEM] * len(OUTS)),
-        scratch_shapes=ROOM + [pltpu.SemaphoreType.DMA((320,))] * 2,
+        scratch_shapes=ROOM + [pltpu.SemaphoreType.DMA((400,))] * 2,
         compiler_params=pltpu.CompilerParams(collective_id=0, has_side_effects=True, vmem_limit_bytes=62 * MIB),
         name="layer",
-    )(tokens, cotangent, w_attention, w_ff, w_down, gains, perm, turn, desc, perm_att, out_perm)
-
-    got_ff = got_ff[:, :12].astype(F32)
-    got_qkv = got_qkv[:, :12].astype(F32)
-    by_kind = got_qkv.reshape(4, 12, 3, 4, HD).transpose(3, 1, 0, 2, 4).reshape(4, 12, 768)
-    gate_grad, up_grad = join_columns(got_ff[:, :, :768]), join_columns(got_ff[:, :, 768:])
-    gain_one_grad = jnp.sum(by_kind[0] * w_query + by_kind[2] * w_key + by_kind[3] * w_value, axis=1)
-    gain_two_grad = jnp.sum(gate_grad * w_gate + up_grad * w_up, axis=1)
+    )(
+        tokens, cotangent, w_query, w_key, w_value, w_out, w_gate, w_up, w_down, *gains,
+        segment_ids.reshape(2, SLAB), positions.reshape(2, SLAB),
+        jnp.asarray(TO_PERM, BF16), jnp.asarray(OFFSET_TURNS, F32), jnp.asarray(BASE_TURNS, F32),
+        jnp.asarray(ATT_PERM, BF16), jnp.asarray(OUT_PERM, BF16),
+    )
+    small, square, wide = [jax.ShapeDtypeStruct((rows, columns), F32) for rows, columns in ((1, 12), (12, 768), (12, 3072))]
+    output, input_grad, gain_one_grad, dq, dk, dv, do, gain_two_grad, dgate, dup, down_grad = pl.pallas_call(
+        finish_kernel,
+        out_shape=(*[jax.ShapeDtypeStruct(*OUTS[k]) for k in range(2)], small, square, square, square, square, small, wide, wide,
+                   jax.ShapeDtypeStruct(*OUTS[2])),
+        in_specs=[VMEM] * 13,
+        out_specs=(VMEM,) * 11,
+        name="finish",
+    )(got_ff, got_qkv, got_out, w_query, w_key, w_value, w_gate, w_up, *gains, output, input_grad, down_grad)
     return (
-        output,
-        input_grad,
-        gain_one_grad,
-        by_kind[0] * first_gain,
-        by_kind[2] * first_gain,
-        by_kind[3] * first_gain,
-        got_out[0, :12],
-        gain_two_grad,
-        gate_grad * second_gain,
-        up_grad * second_gain,
-        down_grad,
+        output, input_grad, gain_one_grad.reshape(12), dq, dk, dv, do, gain_two_grad.reshape(12), dgate, dup, down_grad
     )
 
 

time: 235 us -> 201 us (0.86); the launches traced: 232 us -> 201 us
  other arithmetic: 12.1 us -> 0 us
  Pallas kernels: 211 us -> 200 us
  local copies, waits for them, and re-layouts: 7.06 us -> 0 us
    pallas_call x1, Pallas kernels: 211 us -> 197 us  [per_device(): pl.pallas_call(layer_kernel, out_shape=tuple((jax.ShapeDtypeStruct(shape,...]
    concatenate x3 -> x0, other arithmetic: 3.11 us -> none  [the longest x1 1.65 us: per_device(): w_ff = jnp.pad(jnp.concatenate([w_gate, w_up], 1), ((0, 4), (0, 0)))]
    convert_element_type x3 -> x0, other arithmetic: 2.85 us -> none  [the longest x1 1.22 us: per_device(): base = positions.reshape(2, SLAB)[head, 0].astype(F32)]
    pallas_call x0 -> x1, Pallas kernels: none -> 2.83 us  [per_device(): pl.pallas_call(finish_kernel, out_shape=(*[jax.ShapeDtypeStruct(*OUTS[k])...]
    mul x2 -> x0, other arithmetic: 2.81 us -> none  [the longest x1 1.46 us: per_device(): up_grad * second_gain]
where the time goes in v4:
time: 201 us
  Pallas kernels  200 us (100%)
    pallas_call x1, Pallas kernels, per_device(): pl.pallas_call(layer_kernel, out_shape=tuple((jax.ShapeDtypeStruct(shape,...  197 us

profile of v4, /device:TPU:0, one launch (start us, length us, event | category | flops | bytes accessed | tf_op | source)
XLA Modules:
  0.0 201.0 jit_solution(13253682948383604057)
XLA Ops:
  0.6 197.4 %layer.1 = (bf16[128,768]{1,0:T(8,128)(2,1)}, f32[128,768]{1,0:T(8,128)}, f32[48,768]{1,0:T(8,128)}, bf16[4,16,1536]{2,1,0:T(8,128)(2,1)}, bf16[4,16,768]{2,1,0:T(8,128)(2,1)}, /*index=5*/f32[1,16,768]{2,1,0:T(8,128)}) custom-call(bf16[128,768]{1,0:T(8,128)(2,1)} %tok_ref.1, bf16[128,768]{1,0:T(8,128)(2,1)} %cot_ref.1, bf16[12,768]{1,0:T(8,128)(2,1)} %wq_ref.3, ...), custom_call_target="tpu_custom_call" | custom-call | tf_op jit(solution)/shard_map/layer/pallas_call | solution.py:1250
  198.1 2.8 %finish.1 = (bf16[128,768]{1,0:T(8,128)(2,1)}, f32[128,768]{1,0:T(8,128)}, f32[1,12]{1,0:T(1,128)}, f32[12,768]{1,0:T(8,128)}, f32[12,768]{1,0:T(8,128)}, /*inde...) custom-call(bf16[4,16,1536]{2,1,0:T(8,128)(2,1)} %get-tuple-element., ...), custom_call_target="tpu_custom_call" | custom-call | tf_op jit(solution)/shard_map/finish/pallas_call | solution.py:1265

commit v5 on v4

--- a/solution.py
+++ b/solution.py
@@ -95,27 +95,43 @@
 
 class Links:
     def __init__(self, send, recv):
-        self.send, self.recv, self.used, self.sent = send, recv, 0, []
-
-    def copy(self, source, target, device):
-        k = self.used
-        self.used += 1
+        self.send, self.recv, self.sends, self.recvs, self.sent = send, recv, 0, 0, []
+
+    def send_slot(self):
+        self.sends += 1
+        return self.send.at[self.sends - 1]
+
+    def recv_slot(self):
+        self.recvs += 1
+        return self.recv.at[self.recvs - 1]
+
+    def start(self, source, target, device, send, recv):
         copy = pltpu.make_async_remote_copy(
-            src_ref=source,
-            dst_ref=target,
-            send_sem=self.send.at[k],
-            recv_sem=self.recv.at[k],
-            device_id=device,
-            device_id_type=MESH,
+            src_ref=source, dst_ref=target, send_sem=send, recv_sem=recv, device_id=device, device_id_type=MESH
         )
         copy.start()
-        self.sent.append(copy)
         return copy
+
+    def copy(self, source, target, device):
+        copy = self.start(source, target, device, self.send_slot(), self.recv_slot())
+        self.sent.append(copy.wait_send)
+        return copy
+
+    def group(self, copies, view, recv=None):
+        send = self.send_slot()
+        slots = [self.recv_slot()] * len(copies) if recv is None else recv
+        for (source, target, device), slot in zip(copies, slots):
+            self.start(source, target, device, send, slot)
+        self.sent.append(lambda: self.arrived(view, send))
+        return lambda: self.arrived(view, slots[0])
+
+    def arrived(self, view, semaphore):
+        pltpu.make_async_copy(view, view, semaphore).wait()
 
     def finish(self, count=None):
         count = len(self.sent) if count is None else count
-        for copy in self.sent[:count]:
-            copy.wait_send()
+        for wait in self.sent[:count]:
+            wait()
         del self.sent[:count]
 
 
@@ -275,30 +291,28 @@
     return half(a, rooms[:13], False), half(b, rooms[13:], True)
 
 
-def small_scatter_room(rows, columns):
-    half = columns // 2
-    return [
-        pltpu.VMEM((3, 4, rows, half), BF16),
-        pltpu.VMEM((4, rows, half), BF16),
-        pltpu.VMEM((3, 1, rows, half), BF16),
-    ] * 2
+def small_scatter_room(rows, *sizes):
+    rooms = []
+    for size in sizes:
+        rooms += [
+            pltpu.VMEM((3, 4, rows, size), BF16),
+            pltpu.VMEM((4, rows, size), BF16),
+            pltpu.VMEM((3, 1, rows, size), BF16),
+        ]
+    return rooms
 
 
 def direct_scatter(links, ring, part, room, target, kind):
-    copies = []
-    for k, to in enumerate((ring.next, ring.prev, ring.far)):
-        copies.append(links.copy(part(to), room.at[k], ring.device(to)))
-    yield
-    for copy in copies:
-        copy.wait_recv()
+    copies = [(part(to), room.at[k], ring.device(to)) for k, to in enumerate((ring.next, ring.prev, ring.far))]
+    arrived = links.group(copies, room)
+    yield
+    arrived()
     add_into(target, [part(ring.own), room.at[0], room.at[1], room.at[2]], kind)
 
 
-def small_scatter(links, place, buf, c0, width, rooms, target):
-    size = width // 2
-
-    def half(first, room, x_first):
-        columns = pl.ds(first, size)
+def small_scatter(links, place, buf, first, second, rooms, target):
+    def half(region, room, x_first):
+        columns = pl.ds(*region)
         firsts, lined, lasts = room
 
         def line(k):
@@ -310,7 +324,7 @@
             links, place.ring("y" if x_first else "x"), lambda k: lined.at[pl.ds(k, 1)], lasts, out, F32
         )
 
-    return half(c0, rooms[:3], False), half(c0 + size, rooms[3:], True)
+    return half(first, rooms[:3], False), half(second, rooms[3:], True)
 
 
 def line_scatter_room(rows, columns):
@@ -361,21 +375,17 @@
         copy.wait_recv()
 
 
-def small_gather(links, ring, slot):
-    right = links.copy(slot(ring.own), slot(ring.own), ring.device(ring.next))
-    left = links.copy(slot(ring.own), slot(ring.own), ring.device(ring.prev))
-    yield
-    right.wait_recv()
-    left.wait_recv()
-    on = links.copy(slot(ring.prev), slot(ring.prev), ring.device(ring.next))
-    yield
-    on.wait_recv()
-
-
-def shared_gather(links, place, buf):
-    half = buf.shape[3] // 2
+def small_gather(links, ring, slot, three):
+    own = slot(ring.own)
+    arrived = links.group([(own, own, ring.device(k)) for k in (ring.next, ring.prev, ring.far)], three)
+    yield
+    arrived()
+
+
+def shared_gather(links, place, buf, start, size):
+    half = size // 2
     flip = place.core == 1
-    columns = pl.ds(pl.multiple_of(place.core * half, 128), half)
+    columns = pl.ds(pl.multiple_of(start + place.core * half, 128), half)
     first, second = jnp.where(flip, place.y, place.x), jnp.where(flip, place.x, place.y)
     first_next, first_prev, first_far = [lax.rem(first + k, 4) for k in (1, 3, 2)]
     second_next, second_prev, second_far = [lax.rem(second + k, 4) for k in (1, 3, 2)]
@@ -393,8 +403,11 @@
 
     handed = []
 
-    def hand(s, f):
-        handed.append(links.copy(block(s, f), block(s, f), place.other_core()))
+    def hands(view):
+        pair = links.send_slot(), links.recv_slot()
+        links.sent.append(lambda: links.arrived(view, pair[0]))
+        handed.append(lambda: links.arrived(view, pair[1]))
+        return lambda s, f: links.start(block(s, f), block(s, f), place.other_core(), *pair)
 
     on_right, on_left = device(second, first_next), device(second, first_prev)
     up, down = device(second_next, first), device(second_prev, first)
@@ -415,15 +428,17 @@
     left.wait_recv()
     far_high = send(second, first_next, on_left, 1)
     line(2)
+    hand = hands(buf.at[0, pl.ds(0, 2), :, columns])
     hand(second, first_prev)
     hand(second, first_next)
     yield
     far_low.wait_recv()
     far_high.wait_recv()
     line(3)
-    hand(second, first_far)
+    hands(buf.at[0, 0, :, columns])(second, first_far)
     yield
     far = []
+    hand = hands(buf.at[pl.ds(0, 2), :, :, columns])
     for k in range(4):
         ups[k].wait_recv()
         if k < 2:
@@ -434,12 +449,13 @@
             far.append(send(second_next, order[k], down))
         hand(second_next, order[k])
     yield
+    hand = hands(buf.at[0, :, :, columns])
     for k in range(4):
         far[k].wait_recv()
         hand(second_far, order[k])
     yield
-    for copy in handed:
-        copy.wait_recv()
+    for wait in handed:
+        wait()
 
 
 def advance(*steps):
@@ -506,110 +522,124 @@
     ring_x, ring_y = place.ring("x"), place.ring("y")
     a, b = pl.ds(*first), pl.ds(*second)
 
-    def spread(ring, view):
-        return [links.copy(view, view, ring.device(k)) for k in (ring.next, ring.prev, ring.far)]
-
-    over_x = spread(ring_x, buf.at[place.y, place.x, :, a])
-    over_y = spread(ring_y, buf.at[place.y, place.x, :, b])
-    yield
-    for copy in over_x:
-        copy.wait_recv()
-    over_x = spread(ring_y, buf.at[place.y, :, :, a])
-    for copy in over_y:
-        copy.wait_recv()
-    over_y = spread(ring_x, buf.at[:, place.x, :, b])
-    yield
-    for copy in over_x + over_y:
-        copy.wait_recv()
+    def spread(ring, view, size):
+        return links.group([(view, view, ring.device(k)) for k in (ring.next, ring.prev, ring.far)], size)
+
+    over_x = spread(ring_x, buf.at[place.y, place.x, :, a], buf.at[0, pl.ds(0, 3), :, a])
+    over_y = spread(ring_y, buf.at[place.y, place.x, :, b], buf.at[0, pl.ds(0, 3), :, b])
+    yield
+    over_x()
+    over_x = spread(ring_y, buf.at[place.y, :, :, a], buf.at[pl.ds(0, 3), :, :, a])
+    over_y()
+    over_y = spread(ring_x, buf.at[:, place.x, :, b], buf.at[pl.ds(0, 3), :, :, b])
+    yield
+    over_x()
+    over_y()
+
+
+def turned_view(buf, flip):
+    def view(along, over):
+        first, second = (over, along) if flip else (along, over)
+        return buf.at[first, second, pl.ds(2 if flip else 0, 2)]
+
+    return view
+
+
+def slab_gather_half(links, along, over, view):
+    three, four = pl.ds(1, 3), pl.ds(0, 4)
+    own = view(0, 0)
+    over_arrived = links.group(
+        [
+            (own, view(0, 3), over.device(over.next)),
+            (own, view(0, 1), over.device(over.prev)),
+            (own, view(0, 2), over.device(over.far)),
+        ],
+        view(0, three),
+    )
+    up, down = along.device(along.next), along.device(along.prev)
+    lines = [links.recv_slot(), links.recv_slot()]
+    links.group([(own, view(3, 0), up), (own, view(1, 0), down)], view(0, pl.ds(0, 2)), lines)
+    yield
+    over_arrived()
+    rest = view(0, three)
+    links.group([(rest, view(3, three), up), (rest, view(1, three), down)], view(pl.ds(0, 2), three), lines)
+    yield
+    low, high = pl.ds(0, 2), pl.ds(2, 2)
+    links.arrived(view(3, four), lines[0])
+    far = [links.recv_slot()] * 2
+    send = links.send_slot()
+    links.start(view(3, low), view(2, low), up, send, far[0])
+    links.arrived(view(1, four), lines[1])
+    links.start(view(1, high), view(2, high), down, send, far[1])
+    links.sent.append(lambda: links.arrived(view(0, four), send))
+    yield
+    links.arrived(view(2, four), far[0])
+
+
+def slab_gather(links, place, buf):
+    ring_x, ring_y = place.ring("x"), place.ring("y")
+    return (
+        slab_gather_half(links, ring_y, ring_x, turned_view(buf, False)),
+        slab_gather_half(links, ring_x, ring_y, turned_view(buf, True)),
+    )
+
+
+def slab_scatter_room():
+    many, line = pltpu.VMEM((2, 2, SLAB, SLAB), BF16), pltpu.VMEM((4, 2, SLAB, SLAB), BF16)
+    return ([many] * 2 + [line] * 3 + [pltpu.VMEM((3, 2, SLAB, SLAB), BF16)]) * 2
+
+
+def slab_scatter_half(links, along, over, view, room, target):
+    low, high, prev, nxt, lined, lasts = room
+    lo, hi, four = pl.ds(0, 2), pl.ds(2, 2), pl.ds(0, 4)
+    up, down = along.device(along.next), along.device(along.prev)
+    slots = [links.recv_slot() for _ in range(4)]
+    links.group(
+        [
+            (view(2, lo), low, up),
+            (view(2, hi), high, down),
+            (view(1, hi), prev.at[hi], up),
+            (view(3, lo), nxt.at[lo], down),
+        ],
+        view(lo, four),
+        slots,
+    )
+    yield
+    links.arrived(low, slots[0])
+    add_into(view(1, lo), [view(1, lo), low], BF16)
+    send = links.send_slot()
+    links.start(view(1, lo), prev.at[lo], up, send, slots[2])
+    links.arrived(high, slots[1])
+    add_into(view(3, hi), [view(3, hi), high], BF16)
+    links.start(view(3, hi), nxt.at[hi], down, send, slots[3])
+    links.sent.append(lambda: links.arrived(view(0, four), send))
+    yield
+    links.arrived(prev, slots[2])
+    links.arrived(nxt, slots[3])
+    add_into(lined, [view(0, four), prev, nxt], BF16)
+    arrived = links.group(
+        [
+            (lined.at[1], lasts.at[0], over.device(over.next)),
+            (lined.at[3], lasts.at[1], over.device(over.prev)),
+            (lined.at[2], lasts.at[2], over.device(over.far)),
+        ],
+        lasts,
+    )
+    yield
+    arrived()
+    add_into(target, [lined.at[0], lasts.at[0], lasts.at[1], lasts.at[2]], F32)
+
+
+def slab_scatter(links, place, buf, rooms, target):
+    ring_x, ring_y = place.ring("x"), place.ring("y")
+    return (
+        slab_scatter_half(links, ring_y, ring_x, turned_view(buf, False), rooms[:6], target.at[pl.ds(0, 2)]),
+        slab_scatter_half(links, ring_x, ring_y, turned_view(buf, True), rooms[6:], target.at[pl.ds(2, 2)]),
+    )
 
 
 def slab_place(at):
     return lax.div(at, 16), lax.rem(lax.div(at, 4), 4), lax.rem(at, 4)
-
-
-def flow_gather(links, over, along, block):
-    s, f = along.own, over.own
-    on_right, on_left = over.device(over.next), over.device(over.prev)
-    up, down = along.device(along.next), along.device(along.prev)
-    order = (f, over.prev, over.next, over.far)
-    ups, downs, far = [], [], []
-
-    def send(s, f, to, part=None):
-        return links.copy(block(s, f, part), block(s, f, part), to)
-
-    def line(k):
-        ups.append(send(s, order[k], up))
-        downs.append(send(s, order[k], down))
-
-    right, left = send(s, f, on_right), send(s, f, on_left)
-    line(0)
-    yield
-    right.wait_recv()
-    far_low = send(s, over.prev, on_right, 0)
-    left.wait_recv()
-    far_high = send(s, over.next, on_left, 1)
-    line(1)
-    line(2)
-    yield
-    far_low.wait_recv()
-    far_high.wait_recv()
-    line(3)
-    yield
-    for k in range(4):
-        ups[k].wait_recv()
-        if k < 2:
-            far.append(send(along.prev, order[k], up))
-        downs[k].wait_recv()
-        if k >= 2:
-            far.append(send(along.next, order[k], down))
-    yield
-    for copy in far:
-        copy.wait_recv()
-
-
-def slab_gather(links, place, buf):
-    ring_x, ring_y = place.ring("x"), place.ring("y")
-
-    def slabs(z0, part):
-        return pl.ds(z0, 2) if part is None else pl.ds(z0 + part, 1)
-
-    return (
-        flow_gather(links, ring_x, ring_y, lambda s, f, part: buf.at[s, f, slabs(0, part)]),
-        flow_gather(links, ring_y, ring_x, lambda s, f, part: buf.at[f, s, slabs(2, part)]),
-    )
-
-
-def slab_scatter_room():
-    few, many = pltpu.VMEM((2, 2, SLAB, SLAB), BF16), pltpu.VMEM((4, 2, SLAB, SLAB), BF16)
-    one, two = pltpu.VMEM((1, SLAB, SLAB), BF16), pltpu.VMEM((2, SLAB, SLAB), BF16)
-    return ([few] * 4 + [many] * 3 + [one] * 4 + [two] * 2) * 2
-
-
-def slab_scatter(links, place, buf, rooms, target):
-    def half(z0, room, x_first):
-        low, high, sum_low, sum_high, prev, nxt, lined = room[:7]
-        low1, high1, sum_low1, sum_high1, prev1, nxt1 = room[7:]
-
-        def line(k, part):
-            y, x = (lead_part(part), k) if x_first else (k, lead_part(part))
-            return buf.at[y, x, pl.ds(z0, 2)]
-
-        def one(k, part):
-            return lined.at[k] if part is None else lined.at[k, pl.ds(part, 1)]
-
-        def lined_part(ref):
-            return lambda part: ref.at[lead_part(part)]
-
-        def one_part(ref):
-            return lambda part: ref.at[pl.ds(0, 2) if part is None else pl.ds(part, 1)]
-
-        room_a = (low, high, sum_low, sum_high, lined_part(prev), lined_part(nxt))
-        room_b = (low1, high1, sum_low1, sum_high1, one_part(prev1), one_part(nxt1))
-        yield from ring_scatter(links, place.ring("x" if x_first else "y"), line, room_a, lined, BF16)
-        out = target.at[pl.ds(z0, 2)]
-        yield from ring_scatter(links, place.ring("y" if x_first else "x"), one, room_b, out, F32)
-
-    return half(0, rooms[:13], False), half(2, rooms[13:], True)
 
 
 def keys_of(kv_ref, table, s, first, count):
@@ -625,21 +655,23 @@
     def fold(s, first, count, first_key):
         keys = keys_of(kv_ref, table, s, first, count)
         width = count * SLAB
-        pos_q = query_positions(table, s, (SLAB, 1), 0)
-        pos_k = first_key + lax.broadcasted_iota(jnp.int32, (1, width), 1)
-        scores = dot_right_t(q_ref[s, :, pl.ds(j * 128, 128)], keys)
+        pos_q = query_positions(table, s, (1, SLAB), 1)
+        pos_k = first_key + lax.broadcasted_iota(jnp.int32, (width, 1), 0)
+        scores = dot_right_t(keys, q_ref[s, :, pl.ds(j * 128, 128)])
         scores = jnp.where(pos_k <= pos_q, scores, LOW)
-        top = top_ref[s]
-        new_top = jnp.maximum(top, jnp.max(scores, axis=1, keepdims=True))
-        weights = jnp.exp(scores - new_top[:, 0:1])
+        top, total = top_ref[s][0:1], sum_ref[s][0:1]
+        new_top = jnp.maximum(top, jnp.max(scores, axis=0, keepdims=True))
+        weights = jnp.exp(scores - new_top)
         decay = jnp.exp(top - new_top)
-        sum_ref[s] = sum_ref[s] * decay + jnp.sum(weights, axis=1, keepdims=True)
-        acc_ref[s] = acc_ref[s] * decay + dot(weights.astype(BF16), keys)
-        top_ref[s] = new_top
+        total = total * decay + jnp.sum(weights, axis=0, keepdims=True)
+        sums = lax.dot_general(keys, weights.astype(BF16), (((0,), (0,)), ((), ())), preferred_element_type=F32)
+        acc_ref[s] = acc_ref[s] * decay + sums
+        top_ref[s] = jnp.broadcast_to(new_top, (8, SLAB))
+        sum_ref[s] = jnp.broadcast_to(total, (8, SLAB))
 
     for s in range(4):
-        top_ref[s] = jnp.full((SLAB, SLAB), LOW, F32)
-        sum_ref[s] = jnp.zeros((SLAB, SLAB), F32)
+        top_ref[s] = jnp.full((8, SLAB), LOW, F32)
+        sum_ref[s] = jnp.zeros((8, SLAB), F32)
         acc_ref[s] = jnp.zeros((SLAB, SLAB), F32)
 
     def prompt(c, carry):
@@ -689,25 +721,30 @@
     between(1)
     for s in range(4):
         fold(s, 16, 2, 2048)
-
-
-def sum_terms(table, terms_ref, part_ref):
-    def slab(t, carry):
-        places = [jnp.clip(table[96 + s, t], 0, 18) for s in range(4)]
-        total = terms_ref[0, places[0]].astype(F32)
-        for s in range(1, 4):
-            total = total + terms_ref[s, places[s]].astype(F32)
-        y, x, z = slab_place(t)
-        part_ref[y, x, z] = total.astype(BF16)
+    between(2)
+
+
+def sum_terms(place, table, terms_ref, part_ref):
+    def block(t, carry):
+        dy, dx = lax.div(t, 4), lax.rem(t, 4)
+        at = lax.rem(dy + place.y, 4) * 16 + lax.rem(dx + place.x, 4) * 4
+        for dz in range(4):
+            places = [jnp.clip(table[96 + s, at + dz], 0, 18) for s in range(4)]
+            total = terms_ref[0, places[0]].astype(F32)
+            for s in range(1, 4):
+                total = total + terms_ref[s, places[s]].astype(F32)
+            part_ref[dy, dx, dz] = total.astype(BF16)
         return carry
 
-    lax.fori_loop(0, 64, slab, 0, unroll=4)
-
-
-def lookups(total, own, meta_ref):
+    lax.fori_loop(0, 16, block, 0)
+
+
+def lookups(total, place, meta_ref):
     seg, base = total[2:3], total[3:4]
     lane = lax.broadcasted_iota(jnp.int32, (1, SLAB), 1)
-    lane_at = lane.astype(F32)
+    from_here = lax.rem(lax.div(lane, 16) + 4 - place.y, 4) * 16 + lax.rem(lax.rem(lax.div(lane, 4), 4) + 4 - place.x, 4) * 4
+    lane_at = (from_here + lax.rem(lane, 4)).astype(F32)
+    own = place.y * 4 + place.x
     n = lax.broadcasted_iota(jnp.int32, (24, 1), 0)
     back_rows = jnp.zeros((8, SLAB), F32)
     back_row = lax.broadcasted_iota(jnp.int32, (8, 1), 0)
@@ -768,8 +805,9 @@
     gain = column_of(gain1_ref)
     grads = [qkv_ref[z].astype(F32)[:12] for z in range(4)]
     total = jnp.zeros((12, 1), F32)
-    for c, w_ref, to_ref in ((128, wq_ref, dq_ref), (0, wk_ref, dk_ref), (64, wv_ref, dv_ref)):
-        grad = jnp.concatenate([grads[z][:, 256 * j + c : 256 * j + c + HD] for z in range(4) for j in range(3)], 1)
+    for c, w_ref, to_ref in ((384, wq_ref, dq_ref), (0, wk_ref, dk_ref), (64, wv_ref, dv_ref)):
+        step = 64 if c == 384 else 128
+        grad = jnp.concatenate([grads[z][:, step * j + c : step * j + c + HD] for z in range(4) for j in range(3)], 1)
         total = total + jnp.sum(grad * w_ref[...].astype(F32), axis=1, keepdims=True)
         to_ref[...] = grad * gain
     dgain1_ref[...] = row_of(total)
@@ -795,7 +833,7 @@
     out_ref, in_ref, down_sum_ref, got_ff_ref, got_ref, got_out_ref,
     perm_att, out_perm, const_sem, line_ref, descs, meta_ref, table, table_sem,
     for_line, for_line_ff, rows, rows_o, rows_ff, one, cots, wqkv, wo, wff, q_ref, kv0, kv1, kv2,
-    tops, sums, accs, att_ref, lse_ref, atts, att_s, mid_s, gm_s, two, act, pre, turn_t, part, part_out, sum_z, sum_out,
+    tops, sums, accs, heads, att_ref, lse_ref, atts, att_s, mid_s, gm_s, two, act, pre, turn_t, part, part_out, sum_z, sum_out,
     to_heads, grads_ref, terms, pairs, kv_own, d_s, qkv_sum, ff_sum,
     og_part, og_sum, og_next, *rest,
 ):
@@ -808,8 +846,8 @@
         return out
 
     back_room, ff_room, out_room = take(6), take(26), take(6)
-    kv_rooms = [take(26) for _ in range(3)]
-    qkv_rooms = [take(6) for _ in range(3)]
+    kv_rooms = [take(12) for _ in range(3)]
+    qkv_rooms = [take(6) for _ in range(2)]
     in_room, og_line_room, og_room = take(6), take(6), take(6)
     kvs = (kv0, kv1, kv2)
 
@@ -825,7 +863,7 @@
     own = place.y * 4 + place.x
 
     line_ref[place.z] = own_slab(place, own * 4 + place.z, seg_ref, pos_ref, base_ref)
-    lined = small_gather(links, place.ring("z"), lambda k: line_ref.at[k])
+    lined = small_gather(links, place.ring("z"), lambda k: line_ref.at[k], line_ref.at[pl.ds(0, 3)])
     gain = column_of(gain1_ref)
     w_q, w_k, w_v = [ref[...].astype(F32) * gain for ref in (wq_ref, wk_ref, wv_ref)]
     none, blank = jnp.zeros((12, HD), F32), jnp.zeros((4, 768), F32)
@@ -834,40 +872,57 @@
         for j in range(3):
             at = slice(192 * z + 64 * j, 192 * z + 64 * j + 64)
             pieces += [w_k[:, at], w_v[:, at]]
-            last += [w_q[:, at], none]
-        pieces += last
-        for_line[z] = jnp.concatenate([jnp.concatenate(pieces, 1), blank], 0).astype(BF16)
+            last.append(w_q[:, at])
+        pieces += [*last, none]
+        for_line[z] = jnp.concatenate([jnp.concatenate(pieces, 1), blank[:, :640]], 0).astype(BF16)
     x = dot(tok_ref[...], perm_ref[...])
     one[place.z] = (x * lax.rsqrt(mean_square(x) + EPS)).astype(BF16)
     enter(partners)
     swap = line_swap(links, place, for_line, rows)
     advance(swap, lined)
+    rows_o[place.z] = jnp.concatenate([wo_ref[...].astype(F32), blank], 0).astype(BF16)
+    o_line = small_gather(links, place.ring("z"), lambda k: rows_o.at[k], rows_o.at[pl.ds(0, 3)])
+    advance(o_line)
     ones = line_gather(links, place, one)
+    finish(swap)
     advance(ones)
-    finish(swap)
-    wqkv[place.y, place.x] = dot(pack_rows(), rows[...].reshape(64, 768)).astype(BF16)
+    wqkv[place.y, place.x] = dot(pack_rows(), rows[...].reshape(64, 640)).astype(BF16)
     kv_gather = direct_gather(links, place, wqkv, (0, 256), (256, 128))
-    q_gather = direct_gather(links, place, wqkv, (512, 256), (384, 128))
+    q_gather = shared_gather(links, place, wqkv, 384, 256)
     advance(kv_gather)
+    finish(lined, o_line)
+    wo[place.y, place.x] = dot(pack_rows(), rows_o[...].reshape(64, 768)).astype(BF16)
+    o_gather = shared_gather(links, place, wo, 0, 768)
+    descs[place.y, place.x] = line_ref[0] + line_ref[1] + line_ref[2] + line_ref[3]
+    desc_x = small_gather(links, place.ring("x"), lambda k: descs.at[place.y, k], descs.at[0, pl.ds(0, 3)])
+    desc_y = small_gather(links, place.ring("y"), lambda k: descs.at[k], descs.at[pl.ds(0, 3)])
+    advance(desc_x)
     gain = column_of(gain2_ref)
     for k, ref in enumerate((gate_ref, up_ref)):
         w = ref[...].astype(F32) * gain
         for z in range(4):
             pieces = [w[:, c : c + 48] for c in plane_columns(z)]
             for_line_ff[z, :, pl.ds(768 * k, 768)] = jnp.concatenate([jnp.concatenate(pieces, 1), blank], 0).astype(BF16)
-    advance(lined, kv_gather, ones)
+    advance(kv_gather)
+    finish(desc_x)
+    advance(desc_y)
     advance(q_gather)
-    finish(lined)
-    descs[place.y, place.x] = line_ref[0] + line_ref[1] + line_ref[2] + line_ref[3]
-    desc_x = small_gather(links, place.ring("x"), lambda k: descs.at[place.y, k])
-    desc_y = small_gather(links, place.ring("y"), lambda k: descs.at[k])
-    advance(desc_x)
-    finish(ones, kv_gather)
-    rows_o[place.z] = jnp.concatenate([wo_ref[...].astype(F32), blank], 0).astype(BF16)
-    o_line = small_gather(links, place.ring("z"), lambda k: rows_o.at[k])
+    advance(o_gather)
+    advance(ones)
     ff_swap = line_swap(links, place, for_line_ff, rows_ff)
     cots[place.z] = cot_ref[...]
     cot_gather = line_gather(links, place, cots)
+    finish(desc_y)
+    total = jnp.zeros((8, SLAB), F32)
+    for y in range(4):
+        for k in range(4):
+            total = total + descs[y, k]
+    lookups(total, place, meta_ref)
+    table_copy = pltpu.make_async_copy(meta_ref, table, table_sem)
+    table_copy.start()
+    finish(ones, kv_gather)
+    advance(q_gather)
+    advance(o_gather)
 
     lines = one[...].reshape(512, 768)
     gathers = [slab_gather(links, place, kv) for kv in kvs]
@@ -875,90 +930,74 @@
         field = dot(lines, wqkv[:, :, :, pl.ds(128 * j, 128)].reshape(768, 128))
         for s in range(4):
             cosine, sine = slab_turns(line_ref, turn_ref, s)
-            kvs[j][place.y, place.x, s] = turned(half_rows(field, s), cosine, sine).astype(BF16)
+            kvs[j][0, 0, s] = turned(half_rows(field, s), cosine, sine).astype(BF16)
         if j < 2:
             advance(*gathers[j])
-    advance(o_line, ff_swap, cot_gather)
-    advance(q_gather, desc_x)
+    advance(ff_swap, cot_gather)
+    advance(o_gather)
+    advance(q_gather)
     advance(*gathers[0])
-    advance(*gathers[0])
-    finish(desc_x)
-    advance(desc_y)
-    advance(*gathers[1])
     advance(*gathers[2])
-    advance(desc_y, o_line)
+    advance(q_gather)
     finish(q_gather)
-    field = dot(lines, wqkv[:, :, :, pl.ds(384, 384)].reshape(768, 384))
+    field = dot(lines, wqkv[:, :, :, pl.ds(384, 256)].reshape(768, 256))
+    lane = lax.broadcasted_iota(jnp.int32, (SLAB, SLAB), 1)
     for s in range(4):
         cosine, sine = slab_turns(line_ref, turn_ref, s)
-        for j in range(3):
-            query = turned(half_rows(field[:, 128 * j : 128 * j + 128], s), cosine, sine)
-            q_ref[s, :, pl.ds(128 * j, 128)] = (query * 0.125).astype(BF16)
-    advance(*gathers[0])
+        first, last = half_rows(field[:, 0:128], s), half_rows(field[:, 128:256], s)
+        for j, query in enumerate((first, pltpu.roll(first, 64, 1), last)):
+            query = turned(jnp.where(lane < 64, query * 0.125, 0.0), cosine, sine)
+            q_ref[s, :, pl.ds(128 * j, 128)] = query.astype(BF16)
     advance(*gathers[1])
-    finish(desc_y)
-    total = jnp.zeros((8, SLAB), F32)
-    for y in range(4):
-        for k in range(4):
-            total = total + descs[y, k]
-    lookups(total, own, meta_ref)
-    copy = pltpu.make_async_copy(meta_ref, table, table_sem)
-    copy.start()
-    copy.wait()
-    finish(ff_swap, o_line)
-    wo[place.y, place.x] = dot(pack_rows(), rows_o[...].reshape(64, 768)).astype(BF16)
+    advance(o_gather)
+    finish(ff_swap)
     for c in range(0, 1536, 768):
         wff[place.y, place.x, :, pl.ds(c, 768)] = dot(
             pack_rows(), rows_ff[:, :, pl.ds(c, 768)].reshape(64, 768)
         ).astype(BF16)
     wff[place.y, place.x, :, pl.ds(1536, 768)] = down_ref[...]
-    advance(cot_gather)
+    table_copy.wait()
     for copy in const_copies:
         copy.wait()
+    advance(*gathers[0])
+    advance(*gathers[2])
+    advance(cot_gather)
 
     lane = lax.broadcasted_iota(jnp.int32, (SLAB, SLAB), 1)
-    o_gather = direct_gather(links, place, wo, (0, 384), (384, 384))
-    w_gather = shared_gather(links, place, wff)
+    for s in range(4):
+        heads[s, pl.ds(192, 64), :] = jnp.zeros((64, SLAB), F32)
+    w_gather = shared_gather(links, place, wff, 0, 2304)
     for j in range(3):
         finish(*gathers[j])
 
         def between(k, j=j):
             if j == 0 and k == 0:
+                links.finish(8)
+            if j == 0 and k == 1:
                 advance(*gathers[1])
-                advance(*gathers[2])
-            if j == 0 and k == 1:
-                advance(*gathers[2])
             if j == 1 and k == 0:
-                advance(cot_gather)
-                links.finish(40)
+                finish(cot_gather)
+                links.finish(8)
             if j == 1 and k == 1:
-                advance(*gathers[2])
-            if j == 2 and k == 0:
-                links.finish(40)
-            if j == 2 and k == 1:
                 advance(o_gather)
-                advance(w_gather)
 
         if j == 2:
-            advance(o_gather)
             advance(w_gather)
         attend_head(j, table, q_ref, kvs[j], tops, sums, accs, between)
         for s in range(4):
-            head = accs[s] / sums[s]
-            if j == 0:
-                att_ref[s, :, 0:128] = jnp.where(lane < 64, pltpu.roll(head, 64, 1), 0.0).astype(BF16)
-            elif j == 1:
-                att_ref[s, :, 0:128] = jnp.where(lane < 64, att_ref[s, :, 0:128].astype(F32), head).astype(BF16)
-            else:
-                att_ref[s, :, 128:256] = jnp.where(lane < 64, pltpu.roll(head, 64, 1), 0.0).astype(BF16)
-            logs = tops[s] + jnp.log(sums[s])
-            lse_ref[s] = logs if j == 0 else jnp.where(lane == j, logs, lse_ref[s])
+            heads[s, pl.ds(64 * j, 64), :] = accs[s, pl.ds(64, 64), :] / sums[s][0:1]
+            lse_ref[j, s] = tops[s] + jnp.log(sums[s])
+        if j == 0:
+            advance(*gathers[2])
+    for s in range(4):
+        att_ref[s, :, 0:128] = heads[s, pl.ds(0, 128), :].T.astype(BF16)
+        att_ref[s, :, 128:256] = heads[s, pl.ds(128, 128), :].T.astype(BF16)
     att_swap = line_swap(links, place, att_ref, atts)
     advance(att_swap)
     advance(w_gather)
-    finish(cot_gather)
-    links.finish(40)
+    links.finish(20)
     finish(att_swap, o_gather)
+    advance(w_gather)
 
     att = dot(atts[0], perm_att[pl.ds(0, 256), :])
     for z in range(1, 4):
@@ -978,10 +1017,9 @@
     advance(two_gather)
     together([w_gather, two_gather])
 
-    def block(r, carry):
-        at = pl.ds(pl.multiple_of(r * 256, 256), 256)
-        two_b = two[pl.ds(r * 2, 2)].reshape(256, 768)
-        cot_b = cots[pl.ds(r * 2, 2)].reshape(256, 768)
+    def block():
+        two_b = two[...].reshape(512, 768)
+        cot_b = cots[...].reshape(512, 768)
         gate_w = wff[:, :, :, pl.ds(0, 768)].reshape(768, 768)
         up_w = wff[:, :, :, pl.ds(768, 768)].reshape(768, 768)
         down_w = wff[:, :, :, pl.ds(1536, 768)].reshape(768, 768)
@@ -990,15 +1028,14 @@
         sig = 1.0 / (1.0 + jnp.exp(-gate))
         silu = gate * sig
         act_b = (silu * up).astype(BF16)
-        act[at, :] = act_b
+        act[...] = act_b
         grad_act = dot_right_t(cot_b, down_w)
         grad_gate = (grad_act * up * (sig * (1.0 + gate * (1.0 - sig)))).astype(BF16)
         grad_up = (grad_act * silu).astype(BF16)
-        pre[at, pl.ds(0, 768)] = grad_gate
-        pre[at, pl.ds(768, 768)] = grad_up
+        pre[:, pl.ds(0, 768)] = grad_gate
+        pre[:, pl.ds(768, 768)] = grad_up
         back = dot_right_t(grad_gate, gate_w) + dot_right_t(grad_up, up_w)
-        part[pl.ds(r * 2, 2)] = back.astype(BF16).reshape(2, SLAB, 768)
-        return carry
+        part[...] = back.astype(BF16).reshape(4, SLAB, 768)
 
     def out_block(r, carry):
         at = pl.ds(pl.multiple_of(r * 256, 256), 256)
@@ -1006,7 +1043,7 @@
         part_out[pl.ds(r * 2, 2)] = dot(act[at, :], down_w).astype(BF16).reshape(2, SLAB, 768)
         return carry
 
-    lax.fori_loop(0, 2, block, 0)
+    block()
     links.finish()
     back_sum = line_scatter(links, place, part, back_room, sum_z)
     advance(back_sum)
@@ -1051,18 +1088,15 @@
     for s in range(4):
         terms[s, 18] = jnp.zeros((SLAB, SLAB), BF16)
     finish(heads_swap)
-    advance(*ff)
 
     which = lax.broadcasted_iota(jnp.int32, (8, SLAB), 0)
-    unit = (lax.broadcasted_iota(jnp.int32, (8, SLAB), 1) == which).astype(F32)
     at_lane = lax.broadcasted_iota(jnp.int32, (8, 256), 1)
     pick = (lax.div(at_lane, HD) == lax.broadcasted_iota(jnp.int32, (8, 256), 0)).astype(F32)
     logs, deltas = [], []
     for s in range(4):
         inner = grads_ref[s].astype(F32) * att_ref[s].astype(F32)
         delta = lax.dot_general(pick, inner, LANES, precision=HIGHEST, preferred_element_type=F32)
-        log = lax.dot_general(unit, lse_ref[s], LANES, precision=HIGHEST, preferred_element_type=F32)
-        logs.append([jnp.sum(jnp.where(which == k, log, 0.0), axis=0, keepdims=True) for k in range(3)])
+        logs.append([lse_ref[j, s][0:1] for j in range(3)])
         deltas.append([jnp.sum(jnp.where(which == k, delta, 0.0), axis=0, keepdims=True) for k in range(3)])
 
     scatters = []
@@ -1072,10 +1106,10 @@
             cosine, sine = slab_turns(line_ref, turn_ref, s)
             d_s[pl.ds(s * SLAB, SLAB), pl.ds(128 * j, 128)] = turned(kv_own[j, s], cosine, -sine).astype(BF16)
 
-    def keys_grads(j):
-        pair = jnp.concatenate([d_s[:, pl.ds(128 * j, 128)], d_s[:, pl.ds(384 + 128 * j, 128)]], 1)
-        wo[:, :, :, pl.ds(256 * j, 256)] = dot(turn_t[...], pair).astype(BF16).reshape(4, 4, 48, 256)
-        scatter = small_scatter(links, place, wo, 256 * j, 256, qkv_rooms[j], qkv_sum)
+    def qkv_grads(columns, first, second, room):
+        for c in columns:
+            wo[:, :, :, pl.ds(c, 128)] = dot(turn_t[...], d_s[:, pl.ds(c, 128)]).astype(BF16).reshape(4, 4, 48, 128)
+        scatter = small_scatter(links, place, wo, first, second, room, qkv_sum)
         advance(*scatter)
         return scatter
 
@@ -1084,60 +1118,64 @@
     for j in range(3):
 
         def between(k, j=j):
-            if j == 0:
+            if j == 0 and k == 0:
                 advance(*ff)
-                if k == 0:
-                    advance(out_sum)
-            if j == 1:
+                advance(out_sum)
+            if j == 1 and k == 0:
+                advance(*ff)
+                links.finish(8)
+            if j == 1 and k == 2:
                 advance(*scatters[0])
             if j == 2 and k == 0:
+                advance(*ff)
+                links.finish(4)
+            if j == 2 and k == 1:
                 advance(*scatters[0])
-                advance(*scatters[1])
-            if j == 2 and k == 1:
-                finish(*scatters[0])
+            if j == 2 and k == 2:
                 advance(*scatters[1])
 
         attend_back_head(
             j, table, q_ref, kvs[j], grads_ref, [v[j] for v in logs], [v[j] for v in deltas], accs, terms, pairs, between
         )
-        sum_terms(table, terms, kvs[j])
+        sum_terms(place, table, terms, kvs[j])
         scatters.append(slab_scatter(links, place, kvs[j], kv_rooms[j], kv_own.at[j]))
         advance(*scatters[j])
         for s in range(4):
             cosine, sine = slab_turns(line_ref, turn_ref, s)
-            grad = jnp.where(lane < 64, accs[s] * 0.125, 0.0)
-            d_s[pl.ds(s * SLAB, SLAB), pl.ds(384 + 128 * j, 128)] = turned(grad, cosine, -sine).astype(BF16)
+            grad = turned(jnp.where(lane < 64, accs[s] * 0.125, 0.0), cosine, -sine)
+            to = (pl.ds(s * SLAB, SLAB), pl.ds(384 + 128 * (j // 2), 128))
+            if j == 1:
+                grad = jnp.where(lane < 64, d_s[to].astype(F32), pltpu.roll(grad, 64, 1))
+            d_s[to] = grad.astype(BF16)
         if j == 0:
             finish(out_sum)
             advance(og_line)
             out_ref[...] = (mid_s[...] + sum_out[0]).astype(BF16)
-            finish(*ff)
-            down_sum_ref[...] = ff_sum[0, :, pl.ds(1536, 768)]
-            for c in range(0, 1536, 768):
-                for_line_ff[:, :, pl.ds(c, 768)] = (
-                    dot(spread, ff_sum[0, :, pl.ds(c, 768)].astype(BF16)).astype(BF16).reshape(4, 16, 768)
-                )
-            grads_swap = line_swap(links, place, for_line_ff, got_ff_ref)
-            advance(grads_swap)
         if j == 1:
             advance(og_line)
 
+    finish(*scatters[0])
+    finish(*ff)
+    down_sum_ref[...] = ff_sum[0, :, pl.ds(1536, 768)]
+    for c in range(0, 1536, 768):
+        for_line_ff[:, :, pl.ds(c, 768)] = (
+            dot(spread, ff_sum[0, :, pl.ds(c, 768)].astype(BF16)).astype(BF16).reshape(4, 16, 768)
+        )
+    finish(og_line)
+    grads_swap = line_swap(links, place, for_line_ff, got_ff_ref)
+    advance(grads_swap)
+    keys_turn(0)
+    og_next[...] = og_sum[0].astype(BF16).reshape(4, 4, 16, 768)
+    links.finish(12)
+    advance(*scatters[1])
     advance(*scatters[2])
-    advance(*scatters[1])
-    keys_turn(0)
-    qkv = list(keys_grads(0))
-    finish(og_line, grads_swap)
-    og_next[...] = og_sum[0].astype(BF16).reshape(4, 4, 16, 768)
-    links.finish(60)
     finish(*scatters[1])
+    keys_turn(1)
     advance(*scatters[2])
-    keys_turn(1)
-    qkv += keys_grads(1)
-    og = small_scatter(links, place, og_next, 0, 768, og_room, got_out_ref)
+    qkv = qkv_grads((0, 128, 384), (0, 256), (384, 128), qkv_rooms[0])
+    og = small_scatter(links, place, og_next, (0, 384), (384, 384), og_room, got_out_ref)
     advance(*og)
-    advance(*scatters[2])
-    links.finish(60)
-    advance(*qkv)
+    links.finish(12)
     finish(*scatters[2])
     keys_turn(2)
 
@@ -1149,17 +1187,19 @@
     lax.fori_loop(0, 2, last_block, 0)
     in_sum = line_scatter(links, place, part, in_room, sum_z)
     advance(in_sum)
-    last_qkv = keys_grads(2)
-    finish(*qkv)
-    advance(*og)
+    last_qkv = qkv_grads((256, 512), (256, 128), (512, 128), qkv_rooms[1])
+    advance(*qkv)
+    finish(grads_swap)
     advance(in_sum)
     advance(*last_qkv)
-    finish(*og)
-    links.finish(len(links.sent) - 12)
+    advance(*og)
+    finish(*qkv)
+    links.finish(len(links.sent) - 4)
     finish(*last_qkv)
-    for_line[...] = dot(spread, qkv_sum[0].astype(BF16)).astype(BF16).reshape(4, 16, 768)
+    for_line[...] = dot(spread, qkv_sum[0].astype(BF16)).astype(BF16).reshape(4, 16, 640)
     last = line_swap(links, place, for_line, got_ref)
     advance(last)
+    finish(*og)
     finish(in_sum)
     grad = dot_right_t(sum_z[0].astype(BF16), perm_ref[...])
     x = tok_ref[...].astype(F32)
@@ -1169,6 +1209,7 @@
     finish(last)
 
 
+SENDS, RECVS = 200, 212
 LINE = pltpu.VMEM((4, SLAB, 768), BF16)
 KV = pltpu.VMEM((4, 4, 4, SLAB, SLAB), BF16)
 OUTS = [
@@ -1176,7 +1217,7 @@
     ((SLAB, 768), F32),
     ((48, 768), F32),
     ((4, 16, 1536), BF16),
-    ((4, 16, 768), BF16),
+    ((4, 16, 640), BF16),
     ((1, 16, 768), F32),
 ]
 ROOM = (
@@ -1189,25 +1230,26 @@
         pltpu.VMEM((104, SLAB), jnp.int32),
         pltpu.SMEM((104, SLAB), jnp.int32),
         pltpu.SemaphoreType.DMA,
-        pltpu.VMEM((4, 16, 768), BF16),
+        pltpu.VMEM((4, 16, 640), BF16),
         pltpu.VMEM((4, 16, 1536), BF16),
-        pltpu.VMEM((4, 16, 768), BF16),
+        pltpu.VMEM((4, 16, 640), BF16),
         pltpu.VMEM((4, 16, 768), BF16),
         pltpu.VMEM((4, 16, 1536), BF16),
         LINE,
         LINE,
-        pltpu.VMEM((4, 4, 48, 768), BF16),
+        pltpu.VMEM((4, 4, 48, 640), BF16),
         pltpu.VMEM((4, 4, 48, 768), BF16),
         pltpu.VMEM((4, 4, 48, 2304), BF16),
         pltpu.VMEM((4, SLAB, 384), BF16),
         KV,
         KV,
         KV,
+        pltpu.VMEM((4, 8, SLAB), F32),
+        pltpu.VMEM((4, 8, SLAB), F32),
         pltpu.VMEM((4, SLAB, SLAB), F32),
-        pltpu.VMEM((4, SLAB, SLAB), F32),
-        pltpu.VMEM((4, SLAB, SLAB), F32),
+        pltpu.VMEM((4, 256, SLAB), F32),
         pltpu.VMEM((4, SLAB, 256), BF16),
-        pltpu.VMEM((4, SLAB, SLAB), F32),
+        pltpu.VMEM((3, 4, 8, SLAB), F32),
         pltpu.VMEM((4, SLAB, 256), BF16),
         pltpu.VMEM((SLAB, 768), BF16),
         pltpu.VMEM((SLAB, 768), F32),
@@ -1225,8 +1267,8 @@
         pltpu.VMEM((4, 19, SLAB, SLAB), BF16),
         pltpu.VMEM((4, 256, SLAB), BF16),
         pltpu.VMEM((3, 4, SLAB, SLAB), F32),
-        pltpu.VMEM((512, 768), BF16),
-        pltpu.VMEM((1, 48, 768), F32),
+        pltpu.VMEM((512, 640), BF16),
+        pltpu.VMEM((1, 48, 640), F32),
         pltpu.VMEM((1, 48, 2304), F32),
         pltpu.VMEM((4, 256, 768), BF16),
         pltpu.VMEM((1, 256, 768), F32),
@@ -1236,10 +1278,11 @@
     + plane_scatter_room(48, 2304, False)
     + line_scatter_room(SLAB, 768)
     + slab_scatter_room() * 3
-    + small_scatter_room(48, 256) * 3
+    + small_scatter_room(48, 256, 128)
+    + small_scatter_room(48, 128, 128)
     + line_scatter_room(SLAB, 768)
     + line_scatter_room(256, 768)
-    + small_scatter_room(16, 768)
+    + small_scatter_room(16, 384, 384)
 )
 
 
@@ -1252,7 +1295,8 @@
         out_shape=tuple(jax.ShapeDtypeStruct(shape, kind) for shape, kind in OUTS),
         in_specs=[VMEM] * 16 + [pl.BlockSpec(memory_space=pl.ANY)] * 2,
         out_specs=tuple([VMEM] * len(OUTS)),
-        scratch_shapes=ROOM + [pltpu.SemaphoreType.DMA((400,))] * 2,
+        scratch_shapes=ROOM
+        + [pltpu.SemaphoreType.DMA((SENDS,)), pltpu.SemaphoreType.DMA((RECVS,))],
         compiler_params=pltpu.CompilerParams(collective_id=0, has_side_effects=True, vmem_limit_bytes=62 * MIB),
         name="layer",
     )(

time: 201 us -> 183 us (0.910)
  Pallas kernels: 200 us -> 182 us
    pallas_call x1, Pallas kernels: 197 us -> 179 us  [per_device(): pl.pallas_call(layer_kernel, out_shape=tuple((jax.ShapeDtypeStruct(shape,...]
where the time goes in v5:
time: 183 us
  Pallas kernels  182 us (99%)
    pallas_call x1, Pallas kernels, per_device(): pl.pallas_call(layer_kernel, out_shape=tuple((jax.ShapeDtypeStruct(shape,...  179 us

profile of v5, /device:TPU:0, one launch (start us, length us, event | category | flops | bytes accessed | tf_op | source)
XLA Modules:
  0.0 182.9 jit_solution(5402492349169168192)
XLA Ops:
  0.6 179.3 %layer.1 = (bf16[128,768]{1,0:T(8,128)(2,1)}, f32[128,768]{1,0:T(8,128)}, f32[48,768]{1,0:T(8,128)}, bf16[4,16,1536]{2,1,0:T(8,128)(2,1)}, bf16[4,16,640]{2,1,0:T(8,128)(2,1)}, /*index=5*/f32[1,16,768]{2,1,0:T(8,128)}) custom-call(bf16[128,768]{1,0:T(8,128)(2,1)} %tok_ref.1, bf16[128,768]{1,0:T(8,128)(2,1)} %cot_ref.1, bf16[12,768]{1,0:T(8,128)(2,1)} %wq_ref.3, ...), custom_call_target="tpu_custom_call" | custom-call | tf_op jit(solution)/shard_map/layer/pallas_call | solution.py:1293
  180.0 2.8 %finish.1 = (bf16[128,768]{1,0:T(8,128)(2,1)}, f32[128,768]{1,0:T(8,128)}, f32[1,12]{1,0:T(1,128)}, f32[12,768]{1,0:T(8,128)}, f32[12,768]{1,0:T(8,128)}, /*inde...) custom-call(bf16[4,16,1536]{2,1,0:T(8,128)(2,1)} %get-tuple-element., ...), custom_call_target="tpu_custom_call" | custom-call | tf_op jit(solution)/shard_map/finish/pallas_call | solution.py:1309

commit v6 on v5

--- a/solution.py
+++ b/solution.py
@@ -366,13 +366,11 @@
 
 def line_swap(links, place, source, target):
     ring = place.ring("z")
-    copies = []
-    for other in (ring.next, ring.prev, ring.far):
-        copies.append(links.copy(source.at[other], target.at[ring.own], ring.device(other)))
+    copies = [(source.at[other], target.at[ring.own], ring.device(other)) for other in (ring.next, ring.prev, ring.far)]
+    arrived = links.group(copies, target.at[pl.ds(0, 3)])
     target[ring.own] = source[ring.own]
     yield
-    for copy in copies:
-        copy.wait_recv()
+    arrived()
 
 
 def small_gather(links, ring, slot, three):
@@ -828,10 +826,10 @@
 
 
 def layer_kernel(
-    tok_ref, cot_ref, wq_ref, wk_ref, wv_ref, wo_ref, gate_ref, up_ref, down_ref, gain1_ref, gain2_ref, seg_ref, pos_ref,
-    perm_ref, turn_ref, base_ref, perm_att_hbm, out_perm_hbm,
+    tok_ref, cot_hbm, wq_ref, wk_ref, wv_ref, wo_ref, gate_ref, up_ref, down_hbm, gain1_ref, gain2_ref, seg_ref, pos_ref,
+    perm_hbm, turn_hbm, base_ref, perm_att_hbm, out_perm_hbm,
     out_ref, in_ref, down_sum_ref, got_ff_ref, got_ref, got_out_ref,
-    perm_att, out_perm, const_sem, line_ref, descs, meta_ref, table, table_sem,
+    perm_ref, turn_ref, cot_ref, down_ref, perm_att, out_perm, const_sem, line_ref, descs, meta_ref, table, table_sem,
     for_line, for_line_ff, rows, rows_o, rows_ff, one, cots, wqkv, wo, wff, q_ref, kv0, kv1, kv2,
     tops, sums, accs, heads, att_ref, lse_ref, atts, att_s, mid_s, gm_s, two, act, pre, turn_t, part, part_out, sum_z, sum_out,
     to_heads, grads_ref, terms, pairs, kv_own, d_s, qkv_sum, ff_sum,
@@ -851,12 +849,13 @@
     in_room, og_line_room, og_room = take(6), take(6), take(6)
     kvs = (kv0, kv1, kv2)
 
-    const_copies = [
-        pltpu.make_async_copy(perm_att_hbm, perm_att, const_sem.at[0]),
-        pltpu.make_async_copy(out_perm_hbm, out_perm, const_sem.at[1]),
-    ]
-    for copy in const_copies:
-        copy.start()
+    pairs_in = (
+        (perm_hbm, perm_ref), (turn_hbm, turn_ref), (cot_hbm, cot_ref),
+        (down_hbm, down_ref), (perm_att_hbm, perm_att), (out_perm_hbm, out_perm),
+    )
+    loads = [pltpu.make_async_copy(source, target, const_sem.at[n]) for n, (source, target) in enumerate(pairs_in)]
+    for load in loads:
+        load.start()
     place = Place()
     partners = announce(place)
     links = Links(send, recv)
@@ -875,6 +874,7 @@
             last.append(w_q[:, at])
         pieces += [*last, none]
         for_line[z] = jnp.concatenate([jnp.concatenate(pieces, 1), blank[:, :640]], 0).astype(BF16)
+    loads[0].wait()
     x = dot(tok_ref[...], perm_ref[...])
     one[place.z] = (x * lax.rsqrt(mean_square(x) + EPS)).astype(BF16)
     enter(partners)
@@ -897,6 +897,8 @@
     desc_x = small_gather(links, place.ring("x"), lambda k: descs.at[place.y, k], descs.at[0, pl.ds(0, 3)])
     desc_y = small_gather(links, place.ring("y"), lambda k: descs.at[k], descs.at[pl.ds(0, 3)])
     advance(desc_x)
+    for load in loads[1:]:
+        load.wait()
     gain = column_of(gain2_ref)
     for k, ref in enumerate((gate_ref, up_ref)):
         w = ref[...].astype(F32) * gain
@@ -934,11 +936,13 @@
         if j < 2:
             advance(*gathers[j])
     advance(ff_swap, cot_gather)
-    advance(o_gather)
     advance(q_gather)
     advance(*gathers[0])
     advance(*gathers[2])
+    advance(*gathers[1])
     advance(q_gather)
+    advance(o_gather)
+    advance(*gathers[0])
     finish(q_gather)
     field = dot(lines, wqkv[:, :, :, pl.ds(384, 256)].reshape(768, 256))
     lane = lax.broadcasted_iota(jnp.int32, (SLAB, SLAB), 1)
@@ -948,8 +952,7 @@
         for j, query in enumerate((first, pltpu.roll(first, 64, 1), last)):
             query = turned(jnp.where(lane < 64, query * 0.125, 0.0), cosine, sine)
             q_ref[s, :, pl.ds(128 * j, 128)] = query.astype(BF16)
-    advance(*gathers[1])
-    advance(o_gather)
+    advance(*gathers[2])
     finish(ff_swap)
     for c in range(0, 1536, 768):
         wff[place.y, place.x, :, pl.ds(c, 768)] = dot(
@@ -957,10 +960,7 @@
         ).astype(BF16)
     wff[place.y, place.x, :, pl.ds(1536, 768)] = down_ref[...]
     table_copy.wait()
-    for copy in const_copies:
-        copy.wait()
-    advance(*gathers[0])
-    advance(*gathers[2])
+    advance(o_gather)
     advance(cot_gather)
 
     lane = lax.broadcasted_iota(jnp.int32, (SLAB, SLAB), 1)
@@ -1209,7 +1209,7 @@
     finish(last)
 
 
-SENDS, RECVS = 200, 212
+SENDS, RECVS = 188, 200
 LINE = pltpu.VMEM((4, SLAB, 768), BF16)
 KV = pltpu.VMEM((4, 4, 4, SLAB, SLAB), BF16)
 OUTS = [
@@ -1222,9 +1222,13 @@
 ]
 ROOM = (
     [
+        pltpu.VMEM((768, 768), BF16),
+        pltpu.VMEM((2, SLAB, SLAB), F32),
+        pltpu.VMEM((SLAB, 768), BF16),
+        pltpu.VMEM((48, 768), BF16),
         pltpu.VMEM((1024, 768), BF16),
         pltpu.VMEM((1024, 1024), BF16),
-        pltpu.SemaphoreType.DMA((2,)),
+        pltpu.SemaphoreType.DMA((6,)),
         pltpu.VMEM((4, 8, SLAB), F32),
         pltpu.VMEM((4, 4, 8, SLAB), F32),
         pltpu.VMEM((104, SLAB), jnp.int32),
@@ -1290,10 +1294,11 @@
     tokens, gain_one, w_query, w_key, w_value, w_out, gain_two, w_gate, w_up, w_down, cotangent, segment_ids, positions
 ):
     gains = (gain_one.reshape(1, 12), gain_two.reshape(1, 12))
+    anywhere = pl.BlockSpec(memory_space=pl.ANY)
     output, input_grad, down_grad, got_ff, got_qkv, got_out = pl.pallas_call(
         layer_kernel,
         out_shape=tuple(jax.ShapeDtypeStruct(shape, kind) for shape, kind in OUTS),
-        in_specs=[VMEM] * 16 + [pl.BlockSpec(memory_space=pl.ANY)] * 2,
+        in_specs=[anywhere if k in (1, 8, 13, 14, 16, 17) else VMEM for k in range(18)],
         out_specs=tuple([VMEM] * len(OUTS)),
         scratch_shapes=ROOM
         + [pltpu.SemaphoreType.DMA((SENDS,)), pltpu.SemaphoreType.DMA((RECVS,))],

time: 183 us -> 179 us (0.978)
  Pallas kernels: 182 us -> 178 us
    pallas_call x1, Pallas kernels: 179 us -> 176 us  [per_device(): pl.pallas_call(layer_kernel, out_shape=tuple((jax.ShapeDtypeStruct(shape,...]
where the time goes in v6:
time: 179 us
  Pallas kernels  178 us (99%)
    pallas_call x1, Pallas kernels, per_device(): pl.pallas_call(layer_kernel, out_shape=tuple((jax.ShapeDtypeStruct(shape,...  176 us

profile of v6, /device:TPU:0, one launch (start us, length us, event | category | flops | bytes accessed | tf_op | source)
XLA Modules:
  0.0 179.2 jit_solution(6360452094051558053)
XLA Ops:
  0.6 175.6 %layer.1 = (bf16[128,768]{1,0:T(8,128)(2,1)}, f32[128,768]{1,0:T(8,128)}, f32[48,768]{1,0:T(8,128)}, bf16[4,16,1536]{2,1,0:T(8,128)(2,1)}, bf16[4,16,640]{2,1,0:T(8,128)(2,1)}, /*index=5*/f32[1,16,768]{2,1,0:T(8,128)}) custom-call(bf16[128,768]{1,0:T(8,128)(2,1)} %tok_ref.1, bf16[128,768]{1,0:T(8,128)(2,1)} %cot_hbm.1, bf16[12,768]{1,0:T(8,128)(2,1)} %wq_ref.3, ...), custom_call_target="tpu_custom_call" | custom-call | tf_op jit(solution)/shard_map/layer/pallas_call | solution.py:1298
  176.3 2.8 %finish.1 = (bf16[128,768]{1,0:T(8,128)(2,1)}, f32[128,768]{1,0:T(8,128)}, f32[1,12]{1,0:T(1,128)}, f32[12,768]{1,0:T(8,128)}, f32[12,768]{1,0:T(8,128)}, /*inde...) custom-call(bf16[4,16,1536]{2,1,0:T(8,128)(2,1)} %get-tuple-element., ...), custom_call_target="tpu_custom_call" | custom-call | tf_op jit(solution)/shard_map/finish/pallas_call | solution.py:1314

commit v7 on v6

--- a/solution.py
+++ b/solution.py
@@ -831,7 +831,7 @@
     out_ref, in_ref, down_sum_ref, got_ff_ref, got_ref, got_out_ref,
     perm_ref, turn_ref, cot_ref, down_ref, perm_att, out_perm, const_sem, line_ref, descs, meta_ref, table, table_sem,
     for_line, for_line_ff, rows, rows_o, rows_ff, one, cots, wqkv, wo, wff, q_ref, kv0, kv1, kv2,
-    tops, sums, accs, heads, att_ref, lse_ref, atts, att_s, mid_s, gm_s, two, act, pre, turn_t, part, part_out, sum_z, sum_out,
+    tops, sums, accs, heads, att_ref, lse_ref, atts, wo_heads, mid_s, gm_s, two, act, pre, turn_t, part, part_out, sum_z, sum_out,
     to_heads, grads_ref, terms, pairs, kv_own, d_s, qkv_sum, ff_sum,
     og_part, og_sum, og_next, *rest,
 ):
@@ -905,12 +905,14 @@
         for z in range(4):
             pieces = [w[:, c : c + 48] for c in plane_columns(z)]
             for_line_ff[z, :, pl.ds(768 * k, 768)] = jnp.concatenate([jnp.concatenate(pieces, 1), blank], 0).astype(BF16)
+    advance(q_gather)
+    advance(o_gather)
     advance(kv_gather)
     finish(desc_x)
     advance(desc_y)
+    advance(ones)
     advance(q_gather)
     advance(o_gather)
-    advance(ones)
     ff_swap = line_swap(links, place, for_line_ff, rows_ff)
     cots[place.z] = cot_ref[...]
     cot_gather = line_gather(links, place, cots)
@@ -939,8 +941,8 @@
     advance(q_gather)
     advance(*gathers[0])
     advance(*gathers[2])
+    advance(q_gather)
     advance(*gathers[1])
-    advance(q_gather)
     advance(o_gather)
     advance(*gathers[0])
     finish(q_gather)
@@ -960,8 +962,8 @@
         ).astype(BF16)
     wff[place.y, place.x, :, pl.ds(1536, 768)] = down_ref[...]
     table_copy.wait()
-    advance(o_gather)
     advance(cot_gather)
+    advance(*gathers[1])
 
     lane = lax.broadcasted_iota(jnp.int32, (SLAB, SLAB), 1)
     for s in range(4):
@@ -974,7 +976,8 @@
             if j == 0 and k == 0:
                 links.finish(8)
             if j == 0 and k == 1:
-                advance(*gathers[1])
+                advance(*gathers[2])
+                advance(o_gather)
             if j == 1 and k == 0:
                 finish(cot_gather)
                 links.finish(8)
@@ -987,8 +990,6 @@
         for s in range(4):
             heads[s, pl.ds(64 * j, 64), :] = accs[s, pl.ds(64, 64), :] / sums[s][0:1]
             lse_ref[j, s] = tops[s] + jnp.log(sums[s])
-        if j == 0:
-            advance(*gathers[2])
     for s in range(4):
         att_ref[s, :, 0:128] = heads[s, pl.ds(0, 128), :].T.astype(BF16)
         att_ref[s, :, 128:256] = heads[s, pl.ds(128, 128), :].T.astype(BF16)
@@ -996,14 +997,16 @@
     advance(att_swap)
     advance(w_gather)
     links.finish(20)
-    finish(att_swap, o_gather)
+    finish(o_gather)
+    for z in range(4):
+        wo_heads[z] = dot(perm_att[pl.ds(256 * z, 256), :], merged(wo)).astype(BF16)
+    finish(att_swap)
     advance(w_gather)
 
-    att = dot(atts[0], perm_att[pl.ds(0, 256), :])
-    for z in range(1, 4):
-        att = att + dot(atts[z], perm_att[pl.ds(256 * z, 256), :])
-    att_s[...] = att.astype(BF16)
-    mid_s[...] = tok_ref[...].astype(F32) + dot(att_s[...], merged(wo))
+    middle = tok_ref[...].astype(F32)
+    for z in range(4):
+        middle = middle + dot(atts[z], wo_heads[z])
+    mid_s[...] = middle
     middle = mid_s[...]
     scale_two = lax.rsqrt(mean_square(middle) + EPS)
     two[place.z] = dot((middle * scale_two).astype(BF16), perm_ref[...]).astype(BF16)
@@ -1076,9 +1079,8 @@
     scale_two = lax.rsqrt(mean_square(middle) + EPS)
     gm_s[...] = cot_ref[...].astype(F32) + norm_back(grad, middle * scale_two, scale_two)
     low = gm_s[...].astype(BF16)
-    grad_att = dot_right_t(low, merged(wo)).astype(BF16)
     for z in range(4):
-        to_heads[z] = dot_right_t(grad_att, perm_att[pl.ds(256 * z, 256), :]).astype(BF16)
+        to_heads[z] = dot_right_t(low, wo_heads[z]).astype(BF16)
     heads_swap = line_swap(links, place, to_heads, grads_ref)
     advance(heads_swap)
     out_sum = line_scatter(links, place, part_out, out_room, sum_out)
@@ -1109,9 +1111,7 @@
     def qkv_grads(columns, first, second, room):
         for c in columns:
             wo[:, :, :, pl.ds(c, 128)] = dot(turn_t[...], d_s[:, pl.ds(c, 128)]).astype(BF16).reshape(4, 4, 48, 128)
-        scatter = small_scatter(links, place, wo, first, second, room, qkv_sum)
-        advance(*scatter)
-        return scatter
+        return small_scatter(links, place, wo, first, second, room, qkv_sum)
 
     og_line = line_scatter(links, place, og_part, og_line_room, og_sum)
     spread = spread_rows()
@@ -1174,9 +1174,9 @@
     advance(*scatters[2])
     qkv = qkv_grads((0, 128, 384), (0, 256), (384, 128), qkv_rooms[0])
     og = small_scatter(links, place, og_next, (0, 384), (384, 384), og_room, got_out_ref)
-    advance(*og)
     links.finish(12)
     finish(*scatters[2])
+    advance(*qkv)
     keys_turn(2)
 
     def last_block(r, carry):
@@ -1188,6 +1188,8 @@
     in_sum = line_scatter(links, place, part, in_room, sum_z)
     advance(in_sum)
     last_qkv = qkv_grads((256, 512), (256, 128), (512, 128), qkv_rooms[1])
+    advance(*last_qkv)
+    advance(*og)
     advance(*qkv)
     finish(grads_swap)
     advance(in_sum)
@@ -1255,7 +1257,7 @@
         pltpu.VMEM((4, SLAB, 256), BF16),
         pltpu.VMEM((3, 4, 8, SLAB), F32),
         pltpu.VMEM((4, SLAB, 256), BF16),
-        pltpu.VMEM((SLAB, 768), BF16),
+        pltpu.VMEM((4, 256, 768), BF16),
         pltpu.VMEM((SLAB, 768), F32),
         pltpu.VMEM((SLAB, 768), F32),
         LINE,

time: 179 us -> 176 us (0.983)
  Pallas kernels: 178 us -> 175 us
    pallas_call x1, Pallas kernels: 176 us -> 172 us  [per_device(): pl.pallas_call(layer_kernel, out_shape=tuple((jax.ShapeDtypeStruct(shape,...]
where the time goes in v7:
time: 176 us
  Pallas kernels  175 us (99%)
    pallas_call x1, Pallas kernels, per_device(): pl.pallas_call(layer_kernel, out_shape=tuple((jax.ShapeDtypeStruct(shape,...  172 us

profile of v7, /device:TPU:0, one launch (start us, length us, event | category | flops | bytes accessed | tf_op | source)
XLA Modules:
  0.0 175.5 jit_solution(8906742436424808747)
XLA Ops:
  0.6 171.9 %layer.1 = (bf16[128,768]{1,0:T(8,128)(2,1)}, f32[128,768]{1,0:T(8,128)}, f32[48,768]{1,0:T(8,128)}, bf16[4,16,1536]{2,1,0:T(8,128)(2,1)}, bf16[4,16,640]{2,1,0:T(8,128)(2,1)}, /*index=5*/f32[1,16,768]{2,1,0:T(8,128)}) custom-call(bf16[128,768]{1,0:T(8,128)(2,1)} %tok_ref.1, bf16[128,768]{1,0:T(8,128)(2,1)} %cot_hbm.1, bf16[12,768]{1,0:T(8,128)(2,1)} %wq_ref.3, ...), custom_call_target="tpu_custom_call" | custom-call | tf_op jit(solution)/shard_map/layer/pallas_call | solution.py:1300
  172.6 2.8 %finish.1 = (bf16[128,768]{1,0:T(8,128)(2,1)}, f32[128,768]{1,0:T(8,128)}, f32[1,12]{1,0:T(1,128)}, f32[12,768]{1,0:T(8,128)}, f32[12,768]{1,0:T(8,128)}, /*inde...) custom-call(bf16[4,16,1536]{2,1,0:T(8,128)(2,1)} %get-tuple-element., ...), custom_call_target="tpu_custom_call" | custom-call | tf_op jit(solution)/shard_map/finish/pallas_call | solution.py:1316

commit v8 on v7

--- a/solution.py
+++ b/solution.py
@@ -688,7 +688,7 @@
 def attend_back_head(j, table, q_ref, kv_ref, grad_ref, logs, deltas, dq_ref, terms_ref, pair_ref, between):
     lane = lax.broadcasted_iota(jnp.int32, (SLAB, SLAB), 1)
     for s in range(4):
-        grads = grad_ref[s, :, pl.ds(128 * (j // 2), 128)].astype(F32)
+        grads = grad_ref[j // 2, s].astype(F32)
         if j != 1:
             grads = pltpu.roll(grads, 64, 1)
         pair_ref[s, pl.ds(0, SLAB)] = q_ref[s, :, pl.ds(j * 128, 128)]
@@ -969,6 +969,7 @@
     for s in range(4):
         heads[s, pl.ds(192, 64), :] = jnp.zeros((64, SLAB), F32)
     w_gather = shared_gather(links, place, wff, 0, 2304)
+    att_swaps = []
     for j in range(3):
         finish(*gathers[j])
 
@@ -990,22 +991,22 @@
         for s in range(4):
             heads[s, pl.ds(64 * j, 64), :] = accs[s, pl.ds(64, 64), :] / sums[s][0:1]
             lse_ref[j, s] = tops[s] + jnp.log(sums[s])
-    for s in range(4):
-        att_ref[s, :, 0:128] = heads[s, pl.ds(0, 128), :].T.astype(BF16)
-        att_ref[s, :, 128:256] = heads[s, pl.ds(128, 128), :].T.astype(BF16)
-    att_swap = line_swap(links, place, att_ref, atts)
-    advance(att_swap)
+        if j:
+            for s in range(4):
+                att_ref[j - 1, s] = heads[s, pl.ds(128 * (j - 1), 128), :].T.astype(BF16)
+            att_swaps.append(line_swap(links, place, att_ref.at[j - 1], atts.at[j - 1]))
+            advance(att_swaps[j - 1])
     advance(w_gather)
     links.finish(20)
     finish(o_gather)
     for z in range(4):
         wo_heads[z] = dot(perm_att[pl.ds(256 * z, 256), :], merged(wo)).astype(BF16)
-    finish(att_swap)
+    finish(*att_swaps)
     advance(w_gather)
 
     middle = tok_ref[...].astype(F32)
     for z in range(4):
-        middle = middle + dot(atts[z], wo_heads[z])
+        middle = middle + dot(atts[0, z], wo_heads[z, pl.ds(0, 128)]) + dot(atts[1, z], wo_heads[z, pl.ds(128, 128)])
     mid_s[...] = middle
     middle = mid_s[...]
     scale_two = lax.rsqrt(mean_square(middle) + EPS)
@@ -1013,9 +1014,10 @@
     two_gather = line_gather(links, place, two)
     advance(two_gather)
     advance(w_gather)
-    att = dot(atts[0], out_perm[pl.ds(0, 256), :])
-    for z in range(1, 4):
-        att = att + dot(atts[z], out_perm[pl.ds(256 * z, 256), :])
+    att = jnp.zeros((SLAB, 1024), F32)
+    for z in range(4):
+        for t in range(2):
+            att = att + dot(atts[t, z], out_perm[pl.ds(256 * z + 128 * t, 128), :])
     att_by_z = att.astype(BF16).T
     advance(two_gather)
     together([w_gather, two_gather])
@@ -1079,27 +1081,31 @@
     scale_two = lax.rsqrt(mean_square(middle) + EPS)
     gm_s[...] = cot_ref[...].astype(F32) + norm_back(grad, middle * scale_two, scale_two)
     low = gm_s[...].astype(BF16)
-    for z in range(4):
-        to_heads[z] = dot_right_t(low, wo_heads[z]).astype(BF16)
-    heads_swap = line_swap(links, place, to_heads, grads_ref)
-    advance(heads_swap)
+    heads_swaps = []
+    for t in range(2):
+        for z in range(4):
+            to_heads[t, z] = dot_right_t(low, wo_heads[z, pl.ds(128 * t, 128)]).astype(BF16)
+        heads_swaps.append(line_swap(links, place, to_heads.at[t], grads_ref.at[t]))
+        advance(heads_swaps[t])
     out_sum = line_scatter(links, place, part_out, out_room, sum_out)
     advance(out_sum)
     turn_t[...] = one[...].reshape(512, 768).T
     og_part[...] = dot(att_by_z, low).astype(BF16).reshape(4, 256, 768)
     for s in range(4):
         terms[s, 18] = jnp.zeros((SLAB, SLAB), BF16)
-    finish(heads_swap)
+    finish(heads_swaps[0])
 
     which = lax.broadcasted_iota(jnp.int32, (8, SLAB), 0)
-    at_lane = lax.broadcasted_iota(jnp.int32, (8, 256), 1)
-    pick = (lax.div(at_lane, HD) == lax.broadcasted_iota(jnp.int32, (8, 256), 0)).astype(F32)
-    logs, deltas = [], []
-    for s in range(4):
-        inner = grads_ref[s].astype(F32) * att_ref[s].astype(F32)
-        delta = lax.dot_general(pick, inner, LANES, precision=HIGHEST, preferred_element_type=F32)
-        logs.append([lse_ref[j, s][0:1] for j in range(3)])
-        deltas.append([jnp.sum(jnp.where(which == k, delta, 0.0), axis=0, keepdims=True) for k in range(3)])
+    at_lane = lax.broadcasted_iota(jnp.int32, (8, SLAB), 1)
+    pick = (lax.div(at_lane, HD) == which).astype(F32)
+
+    def deltas_of(j):
+        rows = []
+        for s in range(4):
+            inner = grads_ref[j // 2, s].astype(F32) * att_ref[j // 2, s].astype(F32)
+            delta = lax.dot_general(pick, inner, LANES, precision=HIGHEST, preferred_element_type=F32)
+            rows.append(jnp.sum(jnp.where(which == j % 2, delta, 0.0), axis=0, keepdims=True))
+        return rows
 
     scatters = []
 
@@ -1134,9 +1140,10 @@
             if j == 2 and k == 2:
                 advance(*scatters[1])
 
-        attend_back_head(
-            j, table, q_ref, kvs[j], grads_ref, [v[j] for v in logs], [v[j] for v in deltas], accs, terms, pairs, between
-        )
+        if j == 2:
+            finish(heads_swaps[1])
+        logs = [lse_ref[j, s][0:1] for s in range(4)]
+        attend_back_head(j, table, q_ref, kvs[j], grads_ref, logs, deltas_of(j), accs, terms, pairs, between)
         sum_terms(place, table, terms, kvs[j])
         scatters.append(slab_scatter(links, place, kvs[j], kv_rooms[j], kv_own.at[j]))
         advance(*scatters[j])
@@ -1211,7 +1218,7 @@
     finish(last)
 
 
-SENDS, RECVS = 188, 200
+SENDS, RECVS = 190, 202
 LINE = pltpu.VMEM((4, SLAB, 768), BF16)
 KV = pltpu.VMEM((4, 4, 4, SLAB, SLAB), BF16)
 OUTS = [
@@ -1254,9 +1261,9 @@
         pltpu.VMEM((4, 8, SLAB), F32),
         pltpu.VMEM((4, SLAB, SLAB), F32),
         pltpu.VMEM((4, 256, SLAB), F32),
-        pltpu.VMEM((4, SLAB, 256), BF16),
+        pltpu.VMEM((2, 4, SLAB, SLAB), BF16),
         pltpu.VMEM((3, 4, 8, SLAB), F32),
-        pltpu.VMEM((4, SLAB, 256), BF16),
+        pltpu.VMEM((2, 4, SLAB, SLAB), BF16),
         pltpu.VMEM((4, 256, 768), BF16),
         pltpu.VMEM((SLAB, 768), F32),
         pltpu.VMEM((SLAB, 768), F32),
@@ -1268,8 +1275,8 @@
         LINE,
         pltpu.VMEM((1, SLAB, 768), F32),
         pltpu.VMEM((1, SLAB, 768), F32),
-        pltpu.VMEM((4, SLAB, 256), BF16),
-        pltpu.VMEM((4, SLAB, 256), BF16),
+        pltpu.VMEM((2, 4, SLAB, SLAB), BF16),
+        pltpu.VMEM((2, 4, SLAB, SLAB), BF16),
         pltpu.VMEM((4, 19, SLAB, SLAB), BF16),
         pltpu.VMEM((4, 256, SLAB), BF16),
         pltpu.VMEM((3, 4, SLAB, SLAB), F32),

time: 176 us -> 174 us (0.989)
  Pallas kernels: 175 us -> 173 us
where the time goes in v8:
time: 174 us
  Pallas kernels  173 us (99%)
    pallas_call x1, Pallas kernels, per_device(): pl.pallas_call(layer_kernel, out_shape=tuple((jax.ShapeDtypeStruct(shape,...  170 us

profile of v8, /device:TPU:0, one launch (start us, length us, event | category | flops | bytes accessed | tf_op | source)
XLA Modules:
  0.0 173.8 jit_solution(237882926064106577)
XLA Ops:
  0.6 170.2 %layer.1 = (bf16[128,768]{1,0:T(8,128)(2,1)}, f32[128,768]{1,0:T(8,128)}, f32[48,768]{1,0:T(8,128)}, bf16[4,16,1536]{2,1,0:T(8,128)(2,1)}, bf16[4,16,640]{2,1,0:T(8,128)(2,1)}, /*index=5*/f32[1,16,768]{2,1,0:T(8,128)}) custom-call(bf16[128,768]{1,0:T(8,128)(2,1)} %tok_ref.1, bf16[128,768]{1,0:T(8,128)(2,1)} %cot_hbm.1, bf16[12,768]{1,0:T(8,128)(2,1)} %wq_ref.3, ...), custom_call_target="tpu_custom_call" | custom-call | tf_op jit(solution)/shard_map/layer/pallas_call | solution.py:1307
  170.9 2.8 %finish.1 = (bf16[128,768]{1,0:T(8,128)(2,1)}, f32[128,768]{1,0:T(8,128)}, f32[1,12]{1,0:T(1,128)}, f32[12,768]{1,0:T(8,128)}, f32[12,768]{1,0:T(8,128)}, /*inde...) custom-call(bf16[4,16,1536]{2,1,0:T(8,128)(2,1)} %get-tuple-element., ...), custom_call_target="tpu_custom_call" | custom-call | tf_op jit(solution)/shard_map/finish/pallas_call | solution.py:1323
